TPU v7x, 32 devices: a whole 2x2x4 slice. The times are simulated.
32 devices in a mesh: parts: 2 (over x), seg: 2 (over core), tile: 8 (over z, y).
Axes of the slice: x: 2, y: 2, z: 4, core: 2. Of those that a mesh axis runs over, the one named last changes fastest.
Arguments:
- psi: float32 [4, 8, 128, 128], P(('parts', 'seg'), 'tile'), parts along dimension 0, may hold values from -162 to 162
- left_env: float32 [4, 128, 128, 128], P(('parts', 'seg'), 'tile'), parts along dimension 0, may hold values from -6 to 6
- right_env: float32 [4, 128, 128, 128], P(('parts', 'seg'), 'tile'), parts along dimension 0, may hold values from -6 to 6
- site_energy: float32 [4, 8], P(('parts', 'seg')), parts along dimension 0, may hold values from 1 to 4
- mv_counts: int32 [4, 8, 16], P(('parts', 'seg'), 'tile'), parts along dimension 0, may hold values from 1 to 24, 192 in all within a row
- mv_src: int32 [4, 8, 192], P(('parts', 'seg'), 'tile'), parts along dimension 0, may hold values from 0 to 7
- mv_dst: int32 [4, 8, 192], P(('parts', 'seg'), 'tile'), parts along dimension 0, may hold values from 0 to 7
- mv_coef: float32 [4, 8, 192], P(('parts', 'seg'), 'tile'), parts along dimension 0, may hold values from -0.01171875 to 0.01171875
- up_counts: int32 [4, 8, 16], P(('parts', 'seg'), 'tile'), parts along dimension 0, may hold values from 1 to 24, 192 in all within a row
- up_block: int32 [4, 8, 192], P(('parts', 'seg'), 'tile'), parts along dimension 0, may hold values from 0 to 15
- up_top: int32 [4, 8, 192], P(('parts', 'seg'), 'tile'), parts along dimension 0, may hold values from 0 to 7
- up_bot: int32 [4, 8, 192], P(('parts', 'seg'), 'tile'), parts along dimension 0, may hold values from 0 to 7
- up_coef: float32 [4, 8, 192], P(('parts', 'seg'), 'tile'), parts along dimension 0, may hold values from -0.005859375 to 0.005859375
Outputs:
- residual: float32 [4, 8, 128, 128], P(('parts', 'seg'), 'tile'), parts along dimension 0
- renewed: float32 [4, 128, 128, 128], P(('parts', 'seg'), 'tile'), parts along dimension 0
- rayleigh: float32 [4], P(('parts', 'seg')), parts along dimension 0
There are 2 independent parts, one for each index of `parts`. A program takes and returns all parts, laid end to end along the dimension named above; each array names one. Nothing has to cross between parts.
Inputs may be any that keep to these rules, and one draw needn't show every extreme that they name: `mv_counts`: on every tile index the counts of its 16 channels add up to 192, and one channel of each tile index has exactly 24. `up_counts`: on every tile index the counts of its 16 channels add up to 192, and one channel of each tile index has exactly 24.
All inputs are finite; a program needn't handle non-finite values.
Results may differ from a plain program's by a relative error of at most 0.0003.
Values sent between devices are 32-bit elements; how exact they have to be, the bound alone decides.
No kernel may reach another device: no remote copies, remote signals or barrier semaphores. Data moves between devices by JAX's collectives and lax.ppermute only.
A program may use at most 64 MiB of HBM per device.

v0:
```python
import jax
import jax.numpy as jnp
from jax import lax
from jax.sharding import PartitionSpec as P

MAXT = 24


def passed_along(value, axis, steps):
    count = lax.axis_size(axis)
    first, last = (max(0, -steps), min(count, count - steps))
    return lax.ppermute(value, axis, [(source, source + steps) for source in range(first, last)])


def slot_layout(counts, most):
    block_ends = jnp.cumsum(counts)
    block_starts = block_ends - counts
    slots = jnp.arange(most, dtype=jnp.int32)
    live_slot = slots[None, :] < counts[:, None]
    slot_pos = jnp.where(live_slot, block_starts[:, None] + slots[None, :], 0)
    return (slot_pos, live_slot)


def apply_terms(gathered, env_used, right_own, counts, sources, targets, coefs):
    psi_count = gathered.shape[0]
    tile_width = gathered.shape[1]
    channels = counts.shape[0]
    quarter = channels // 4
    slot_pos, live_slot = slot_layout(counts, MAXT)
    src_slots = sources[slot_pos]
    dst_slots = targets[slot_pos]
    coef_slots = jnp.where(live_slot, coefs[slot_pos], 0.0)

    def apply_one_turn(running, inputs):
        env_part, right_part, src_part, dst_part, coef_part = inputs
        inner = jnp.einsum(
            "csij,cjk->csik", gathered[src_part], right_part, precision=lax.Precision.HIGHEST
        )
        contrib = jnp.einsum("cij,csjk->csik", env_part, inner, precision=lax.Precision.HIGHEST)
        contrib = contrib * coef_part[:, :, None, None]
        added = jax.ops.segment_sum(
            contrib.reshape(-1, tile_width, tile_width),
            dst_part.reshape(-1),
            num_segments=psi_count,
        )
        return (running + added, None)

    inputs = (
        env_used.reshape(4, quarter, tile_width, tile_width),
        right_own.reshape(4, quarter, tile_width, tile_width),
        src_slots.reshape(4, quarter, MAXT),
        dst_slots.reshape(4, quarter, MAXT),
        coef_slots.reshape(4, quarter, MAXT),
    )
    start_sum = jnp.zeros((psi_count, tile_width, tile_width), jnp.float32)
    summed, unused = lax.scan(apply_one_turn, start_sum, inputs)
    return summed


def renew_env(gathered, own_env, counts, blocks, tops, bottoms, coefs):
    tile_width = gathered.shape[1]
    channels = counts.shape[0]
    quarter = channels // 4
    slot_pos, live_slot = slot_layout(counts, MAXT)
    block_slots = blocks[slot_pos]
    top_slots = tops[slot_pos]
    bottom_slots = bottoms[slot_pos]
    coef_slots = jnp.where(live_slot, coefs[slot_pos], 0.0)

    def renew_one_turn(inputs):
        block_part, top_part, bottom_part, coef_part = inputs
        inner = jnp.einsum(
            "csij,csjk->csik",
            own_env[block_part],
            gathered[bottom_part],
            precision=lax.Precision.HIGHEST,
        )
        contrib = jnp.einsum(
            "csji,csjk->csik", gathered[top_part], inner, precision=lax.Precision.HIGHEST
        )
        contrib = contrib * coef_part[:, :, None, None]
        return jnp.sum(contrib, axis=1)

    inputs = (
        block_slots.reshape(4, quarter, MAXT),
        top_slots.reshape(4, quarter, MAXT),
        bottom_slots.reshape(4, quarter, MAXT),
        coef_slots.reshape(4, quarter, MAXT),
    )
    stacked = lax.map(renew_one_turn, inputs)
    return stacked.reshape(channels, tile_width, tile_width)


def shards(
    psi,
    left_env,
    right_env,
    site_energy,
    mv_counts,
    mv_src,
    mv_dst,
    mv_coef,
    up_counts,
    up_block,
    up_top,
    up_bot,
    up_coef,
):
    own_psi = psi[0]
    own_env = left_env[0]
    gathered = lax.all_gather(own_psi, "tile", axis=0, tiled=True)
    renewal = renew_env(
        gathered,
        own_env,
        up_counts[0, 0],
        up_block[0, 0],
        up_top[0, 0],
        up_bot[0, 0],
        up_coef[0, 0],
    )
    received = passed_along(renewal, "seg", 1)
    leading = lax.axis_index("seg") == 0
    env_used = jnp.where(leading, own_env, received)
    partial_value = apply_terms(
        gathered, env_used, right_env[0], mv_counts[0, 0], mv_src[0, 0], mv_dst[0, 0], mv_coef[0, 0]
    )
    row_count = own_psi.shape[0]
    energies = site_energy[0]
    row_start = lax.axis_index("tile") * row_count
    summed_own = lax.psum_scatter(partial_value, "tile", scatter_dimension=0, tiled=True)
    own_energy = lax.dynamic_slice_in_dim(energies, row_start, row_count, 0)
    own_rows = summed_own + own_energy[:, None, None] * own_psi
    numerator = lax.psum(jnp.sum(own_psi * own_rows), "tile")
    denominator = jnp.sum(gathered * gathered)
    quotient = numerator / denominator
    residual = own_rows - quotient * own_psi
    return (residual[None], renewal[None], jnp.reshape(quotient, (1,)))


def solution(mesh):
    return jax.shard_map(
        shards,
        mesh=mesh,
        in_specs=(
            P(("parts", "seg"), "tile", None, None),
            P(("parts", "seg"), "tile", None, None),
            P(("parts", "seg"), "tile", None, None),
            P(("parts", "seg"), None),
            P(("parts", "seg"), "tile", None),
            P(("parts", "seg"), "tile", None),
            P(("parts", "seg"), "tile", None),
            P(("parts", "seg"), "tile", None),
            P(("parts", "seg"), "tile", None),
            P(("parts", "seg"), "tile", None),
            P(("parts", "seg"), "tile", None),
            P(("parts", "seg"), "tile", None),
            P(("parts", "seg"), "tile", None),
        ),
        out_specs=(
            P(("parts", "seg"), "tile", None, None),
            P(("parts", "seg"), "tile", None, None),
            P(("parts", "seg")),
        ),
        check_vma=False,
    )
```

profile of v0, /device:TPU:0, one launch (start us, length us, event | category | flops | bytes accessed | tf_op | source)
XLA Modules:
  0.0 466.7 jit_solution(8104078934030009947)
XLA Ops:
  9.6 2.8 gather_fusion.9
  16.8 2.8 gather_fusion.7
  19.7 2.8 gather_fusion.8
  22.7 33.0 %all-gather = f32[8,1,128,128]{3,2,1,0:T(8,128)S(1)} all-gather(f32[1,1,128,128]{3,2,1,0:T(8,128)S(1)} %copy-done.9), channel_id=2, replica_groups=mesh['parts'=2,'seg'=2,'tile'=8] {'tile'}, dimensions={0}, use_global_device_ids=true | all-gather | bytes 589824 | tf_op jit(solution)/shard_map/all_gather | solution.py:111
  55.7 145.4 %while.20 = (s32[]{:T(128)}, f32[4,4,128,128]{3,2,1,0:T(8,128)}, s32[4,4,24]{2,1,0:T(4,128)S(1)}, f32[8,128,128]{2,1,0:T(8,128)S(1)}, s32[4,4,24]{2,1,0:T(4,128)...) while((s32[]{:T(128)}, f32[4,4,128,128]{3,2,1,0:T(8,128)}, ...), condition=%wide.region_3.4_spmd, body=%wide.region_1.3_spmd.sunk | while | flops 4834922496 | bytes 70013416 | solution.py:90
  55.9 3.6 gather_fusion.2
  59.5 3.6 gather_fusion.1
  63.1 11.1 %fusion.34 = f32[4,24,128,128]{3,2,1,0:T(8,128)} fusion(f32[4,24,128,128]{3,2,1,0:T(8,128)} %bitcast.143, f32[4,24,128,128]{3,2,1,0:T(8,128)} %bitcast.142), kind=kOutput, calls=%fused_computation.55.clone.1 | convolution fusion | flops 2415919104 | bytes 18874368 | tf_op jit(solution)/shard_map/while/body/eval_jaxpr/csij,csjk->csik/dot_general | solution.py:72
  74.3 3.6 gather_fusion
  77.9 13.5 %multiply_reduce_fusion.3 = f32[4,128,128]{2,1,0:T(8,128)S(1)} fusion(f32[4,24]{1,0:T(4,128)S(1)} %dynamic-slice_bitcast_fusion.4, f32[4,24,128,128]{3,2,1,0:T(8,128)} %bitcast.144, f32[4,24,128,128]{3,2,1,0:T(8,128)} %fusion.34), kind=kOutput, calls=%fused_computation.12.clone.1 | convolution fusion | flops 2418999296 | bytes 12845440 | tf_op jit(solution)/shard_map/while/body/eval_jaxpr/csji,csjk->csik/dot_general | solution.py:78
  92.2 3.6 gather_fusion.2
  95.9 3.6 gather_fusion.1
  99.5 11.1 %fusion.34 = f32[4,24,128,128]{3,2,1,0:T(8,128)} fusion(f32[4,24,128,128]{3,2,1,0:T(8,128)} %bitcast.143, f32[4,24,128,128]{3,2,1,0:T(8,128)} %bitcast.142), kind=kOutput, calls=%fused_computation.55.clone.1 | convolution fusion | flops 2415919104 | bytes 18874368 | tf_op jit(solution)/shard_map/while/body/eval_jaxpr/csij,csjk->csik/dot_general | solution.py:72
  110.7 3.6 gather_fusion
  114.3 13.5 %multiply_reduce_fusion.3 = f32[4,128,128]{2,1,0:T(8,128)S(1)} fusion(f32[4,24]{1,0:T(4,128)S(1)} %dynamic-slice_bitcast_fusion.4, f32[4,24,128,128]{3,2,1,0:T(8,128)} %bitcast.144, f32[4,24,128,128]{3,2,1,0:T(8,128)} %fusion.34), kind=kOutput, calls=%fused_computation.12.clone.1 | convolution fusion | flops 2418999296 | bytes 12845440 | tf_op jit(solution)/shard_map/while/body/eval_jaxpr/csji,csjk->csik/dot_general | solution.py:78
  128.6 3.6 gather_fusion.2
  132.2 3.6 gather_fusion.1
  135.8 11.1 %fusion.34 = f32[4,24,128,128]{3,2,1,0:T(8,128)} fusion(f32[4,24,128,128]{3,2,1,0:T(8,128)} %bitcast.143, f32[4,24,128,128]{3,2,1,0:T(8,128)} %bitcast.142), kind=kOutput, calls=%fused_computation.55.clone.1 | convolution fusion | flops 2415919104 | bytes 18874368 | tf_op jit(solution)/shard_map/while/body/eval_jaxpr/csij,csjk->csik/dot_general | solution.py:72
  147.0 3.6 gather_fusion
  150.6 13.5 %multiply_reduce_fusion.3 = f32[4,128,128]{2,1,0:T(8,128)S(1)} fusion(f32[4,24]{1,0:T(4,128)S(1)} %dynamic-slice_bitcast_fusion.4, f32[4,24,128,128]{3,2,1,0:T(8,128)} %bitcast.144, f32[4,24,128,128]{3,2,1,0:T(8,128)} %fusion.34), kind=kOutput, calls=%fused_computation.12.clone.1 | convolution fusion | flops 2418999296 | bytes 12845440 | tf_op jit(solution)/shard_map/while/body/eval_jaxpr/csji,csjk->csik/dot_general | solution.py:78
  164.9 3.6 gather_fusion.2
  168.6 3.6 gather_fusion.1
  172.2 11.1 %fusion.34 = f32[4,24,128,128]{3,2,1,0:T(8,128)} fusion(f32[4,24,128,128]{3,2,1,0:T(8,128)} %bitcast.143, f32[4,24,128,128]{3,2,1,0:T(8,128)} %bitcast.142), kind=kOutput, calls=%fused_computation.55.clone.1 | convolution fusion | flops 2415919104 | bytes 18874368 | tf_op jit(solution)/shard_map/while/body/eval_jaxpr/csij,csjk->csik/dot_general | solution.py:72
  183.4 3.6 gather_fusion
  187.0 13.5 %multiply_reduce_fusion.3 = f32[4,128,128]{2,1,0:T(8,128)S(1)} fusion(f32[4,24]{1,0:T(4,128)S(1)} %dynamic-slice_bitcast_fusion.4, f32[4,24,128,128]{3,2,1,0:T(8,128)} %bitcast.144, f32[4,24,128,128]{3,2,1,0:T(8,128)} %fusion.34), kind=kOutput, calls=%fused_computation.12.clone.1 | convolution fusion | flops 2418999296 | bytes 12845440 | tf_op jit(solution)/shard_map/while/body/eval_jaxpr/csji,csjk->csik/dot_general | solution.py:78
  213.9 154.2 %while.21 = (s32[]{:T(128)}, f32[8,128,128]{2,1,0:T(8,128)S(1)}, s32[4,4,24]{2,1,0:T(4,128)S(1)}, s32[4,4,24]{2,1,0:T(4,128)S(1)}, f32[8,128,128]{2,1,0:T(8,128)...) while((s32[]{:T(128)}, f32[8,128,128]{2,1,0:T(8,128)S(1)}, ...), condition=%wide.region_7.8_spmd, body=%wide.region_5.7_spmd.sunk | while | flops 4834984960 | bytes 69742064 | solution.py:56
  214.0 3.6 gather_fusion.3
  217.6 8.0 %fusion.39 = f32[4,24,128,128]{2,3,1,0:T(8,128)S(1)} fusion(f32[4,24,128,128]{3,2,1,0:T(8,128)} %bitcast.145, f32[4,4,128,128]{3,2,1,0:T(8,128)} %get-tuple-element.275, s32[]{:T(128)} %get-tuple-element.261), kind=kOutput, calls=%fused_computation.23.clone.1 | convolution fusion | flops 2415919104 | bytes 12845568 | tf_op jit(solution)/shard_map/while/body/eval_jaxpr/csij,cjk->csik/dot_general | solution.py:36
  225.7 7.2 %broadcast_multiply_fusion.2 = f32[4,24,128,128]{3,2,1,0:T(8,128)} fusion(f32[4,24]{1,0:T(4,128)S(1)} %dynamic-slice_bitcast_fusion.5, f32[4,24,128,128]{2,3,1,0:T(8,128)S(1)} %fusion.39, f32[4,4,128,128]{3,2,1,0:T(8,128)S(1)} %get-tuple-element.276, s32[]{:T(128)} %get-tuple-element.261), kind=kOutput, calls=%fused_computation.21.clone.1 | convolution fusion | flops 2417491968 | bytes 12847108 | tf_op jit(solution)/shard_map/while/body/eval_jaxpr/cij,csjk->csik/dot_general | solution.py:39
  232.9 6.5 %copy.36 = f32[96,128,128]{2,1,0:T(8,128)} copy(f32[96,128,128]{1,2,0:T(8,128)} %bitcast.141) | data formatting | bytes 12582912 | tf_op jit(solution)/shard_map/while/body/eval_jaxpr/reshape | solution.py:42
  239.5 12.9 %scatter_fusion = f32[8,128,128]{2,1,0:T(8,128)S(1)} fusion(f32[8,128,128]{2,1,0:T(8,128)S(1)} %get-tuple-element.262, s32[96]{0:T(128)S(1)} %reshape.588, f32[96,128,128]{2,1,0:T(8,128)} %copy.36), kind=kCustom, calls=%fused_computation.11.clone.1 | custom fusion | flops 1572864 | bytes 18874752 | tf_op jit(solution)/shard_map/while/body/eval_jaxpr/scatter-add | solution.py:41
  252.6 3.6 gather_fusion.3
  256.2 8.0 %fusion.39 = f32[4,24,128,128]{2,3,1,0:T(8,128)S(1)} fusion(f32[4,24,128,128]{3,2,1,0:T(8,128)} %bitcast.145, f32[4,4,128,128]{3,2,1,0:T(8,128)} %get-tuple-element.275, s32[]{:T(128)} %get-tuple-element.261), kind=kOutput, calls=%fused_computation.23.clone.1 | convolution fusion | flops 2415919104 | bytes 12845568 | tf_op jit(solution)/shard_map/while/body/eval_jaxpr/csij,cjk->csik/dot_general | solution.py:36
  264.2 7.2 %broadcast_multiply_fusion.2 = f32[4,24,128,128]{3,2,1,0:T(8,128)} fusion(f32[4,24]{1,0:T(4,128)S(1)} %dynamic-slice_bitcast_fusion.5, f32[4,24,128,128]{2,3,1,0:T(8,128)S(1)} %fusion.39, f32[4,4,128,128]{3,2,1,0:T(8,128)S(1)} %get-tuple-element.276, s32[]{:T(128)} %get-tuple-element.261), kind=kOutput, calls=%fused_computation.21.clone.1 | convolution fusion | flops 2417491968 | bytes 12847108 | tf_op jit(solution)/shard_map/while/body/eval_jaxpr/cij,csjk->csik/dot_general | solution.py:39
  271.5 6.5 %copy.36 = f32[96,128,128]{2,1,0:T(8,128)} copy(f32[96,128,128]{1,2,0:T(8,128)} %bitcast.141) | data formatting | bytes 12582912 | tf_op jit(solution)/shard_map/while/body/eval_jaxpr/reshape | solution.py:42
  278.1 12.9 %scatter_fusion = f32[8,128,128]{2,1,0:T(8,128)S(1)} fusion(f32[8,128,128]{2,1,0:T(8,128)S(1)} %get-tuple-element.262, s32[96]{0:T(128)S(1)} %reshape.588, f32[96,128,128]{2,1,0:T(8,128)} %copy.36), kind=kCustom, calls=%fused_computation.11.clone.1 | custom fusion | flops 1572864 | bytes 18874752 | tf_op jit(solution)/shard_map/while/body/eval_jaxpr/scatter-add | solution.py:41
  291.1 3.6 gather_fusion.3
  294.7 8.0 %fusion.39 = f32[4,24,128,128]{2,3,1,0:T(8,128)S(1)} fusion(f32[4,24,128,128]{3,2,1,0:T(8,128)} %bitcast.145, f32[4,4,128,128]{3,2,1,0:T(8,128)} %get-tuple-element.275, s32[]{:T(128)} %get-tuple-element.261), kind=kOutput, calls=%fused_computation.23.clone.1 | convolution fusion | flops 2415919104 | bytes 12845568 | tf_op jit(solution)/shard_map/while/body/eval_jaxpr/csij,cjk->csik/dot_general | solution.py:36
  302.8 7.2 %broadcast_multiply_fusion.2 = f32[4,24,128,128]{3,2,1,0:T(8,128)} fusion(f32[4,24]{1,0:T(4,128)S(1)} %dynamic-slice_bitcast_fusion.5, f32[4,24,128,128]{2,3,1,0:T(8,128)S(1)} %fusion.39, f32[4,4,128,128]{3,2,1,0:T(8,128)S(1)} %get-tuple-element.276, s32[]{:T(128)} %get-tuple-element.261), kind=kOutput, calls=%fused_computation.21.clone.1 | convolution fusion | flops 2417491968 | bytes 12847108 | tf_op jit(solution)/shard_map/while/body/eval_jaxpr/cij,csjk->csik/dot_general | solution.py:39
  310.0 6.5 %copy.36 = f32[96,128,128]{2,1,0:T(8,128)} copy(f32[96,128,128]{1,2,0:T(8,128)} %bitcast.141) | data formatting | bytes 12582912 | tf_op jit(solution)/shard_map/while/body/eval_jaxpr/reshape | solution.py:42
  316.7 12.9 %scatter_fusion = f32[8,128,128]{2,1,0:T(8,128)S(1)} fusion(f32[8,128,128]{2,1,0:T(8,128)S(1)} %get-tuple-element.262, s32[96]{0:T(128)S(1)} %reshape.588, f32[96,128,128]{2,1,0:T(8,128)} %copy.36), kind=kCustom, calls=%fused_computation.11.clone.1 | custom fusion | flops 1572864 | bytes 18874752 | tf_op jit(solution)/shard_map/while/body/eval_jaxpr/scatter-add | solution.py:41
  329.7 3.6 gather_fusion.3
  333.3 8.0 %fusion.39 = f32[4,24,128,128]{2,3,1,0:T(8,128)S(1)} fusion(f32[4,24,128,128]{3,2,1,0:T(8,128)} %bitcast.145, f32[4,4,128,128]{3,2,1,0:T(8,128)} %get-tuple-element.275, s32[]{:T(128)} %get-tuple-element.261), kind=kOutput, calls=%fused_computation.23.clone.1 | convolution fusion | flops 2415919104 | bytes 12845568 | tf_op jit(solution)/shard_map/while/body/eval_jaxpr/csij,cjk->csik/dot_general | solution.py:36
  341.4 7.2 %broadcast_multiply_fusion.2 = f32[4,24,128,128]{3,2,1,0:T(8,128)} fusion(f32[4,24]{1,0:T(4,128)S(1)} %dynamic-slice_bitcast_fusion.5, f32[4,24,128,128]{2,3,1,0:T(8,128)S(1)} %fusion.39, f32[4,4,128,128]{3,2,1,0:T(8,128)S(1)} %get-tuple-element.276, s32[]{:T(128)} %get-tuple-element.261), kind=kOutput, calls=%fused_computation.21.clone.1 | convolution fusion | flops 2417491968 | bytes 12847108 | tf_op jit(solution)/shard_map/while/body/eval_jaxpr/cij,csjk->csik/dot_general | solution.py:39
  348.6 6.5 %copy.36 = f32[96,128,128]{2,1,0:T(8,128)} copy(f32[96,128,128]{1,2,0:T(8,128)} %bitcast.141) | data formatting | bytes 12582912 | tf_op jit(solution)/shard_map/while/body/eval_jaxpr/reshape | solution.py:42
  355.2 12.9 %scatter_fusion = f32[8,128,128]{2,1,0:T(8,128)S(1)} fusion(f32[8,128,128]{2,1,0:T(8,128)S(1)} %get-tuple-element.262, s32[96]{0:T(128)S(1)} %reshape.588, f32[96,128,128]{2,1,0:T(8,128)} %copy.36), kind=kCustom, calls=%fused_computation.11.clone.1 | custom fusion | flops 1572864 | bytes 18874752 | tf_op jit(solution)/shard_map/while/body/eval_jaxpr/scatter-add | solution.py:41
  369.5 62.9 %reduce-scatter.2.cloned.1.call-done = f32[1,128,128]{2,1,0:T(8,128)} async-done(((f32[8,128,128]{2,1,0:T(8,128)}), f32[1,128,128]{2,1,0:T(8,128)}) %reduce-scatter.2.cloned.1.call-update) | async-done | bytes 65552 | tf_op jit(solution)/shard_map/reduce_scatter | solution.py:130
  435.2 20.1 %psum.7 = f32[]{:T(128)} all-reduce(f32[]{:T(128)} %fusion.10), channel_id=1, replica_groups=mesh['parts'=2,'seg'=2,'tile'=8] {'tile'}, use_global_device_ids=true, to_apply=%region_10.11 | all-reduce | flops 1 | bytes 8 | tf_op jit(solution)/shard_map/psum | solution.py:133
  (135 shorter events, 30.6 us)
Async XLA Ops:
  7.2 2.5 copy-start
  7.2 5.9 %copy-start.11 = (s32[1,1,16]{2,1,0:T(1,128)S(1)}, s32[1,1,16]{2,1,0:T(1,128)}, u32[]{:S(2)}) copy-start(s32[1,1,16]{2,1,0:T(1,128)} %param.25) | copy-start | bytes 196
  7.2 6.7 %copy-start.1 = (s32[1,1,192]{2,1,0:T(1,128)S(1)}, s32[1,1,192]{2,1,0:T(1,128)}, u32[]{:S(2)}) copy-start(s32[1,1,192]{2,1,0:T(1,128)} %param.27) | copy-start | bytes 2308
  7.2 425.2 %reduce-scatter.2.cloned.1.call-start = ((), (), s32[]{:S(2)}) async-start(), calls=%async_computation.1 | async-start | bytes 589824 | tf_op jit(solution)/shard_map/reduce_scatter | solution.py:130
  12.5 4.3 copy-start.2
  16.7 3.1 copy-start.3
  19.6 3.0 copy-start.9
  19.6 36.1 %copy-start.8 = (f32[1,16,128,128]{3,2,1,0:T(8,128)S(1)}, f32[1,16,128,128]{3,2,1,0:T(8,128)}, u32[]{:S(2)}) copy-start(f32[1,16,128,128]{3,2,1,0:T(8,128)} %param.18) | copy-start | bytes 3145732
  55.7 147.9 %copy-start.12 = (s32[1,1,16]{2,1,0:T(1,128)S(1)}, s32[1,1,16]{2,1,0:T(1,128)}, u32[]{:S(2)}) copy-start(s32[1,1,16]{2,1,0:T(1,128)} %param.21) | copy-start | bytes 196
  55.7 149.0 %copy-start.4 = (f32[1,1,192]{2,1,0:T(1,128)S(1)}, f32[1,1,192]{2,1,0:T(1,128)}, u32[]{:S(2)}) copy-start(f32[1,1,192]{2,1,0:T(1,128)} %param.24) | copy-start | bytes 2308
  201.2 6.5 %copy-start.5 = (s32[1,1,192]{2,1,0:T(1,128)S(1)}, s32[1,1,192]{2,1,0:T(1,128)}, u32[]{:S(2)}) copy-start(s32[1,1,192]{2,1,0:T(1,128)} %param.23) | copy-start | bytes 2308
  201.2 12.4 %collective-permute-start = (f32[16,128,128]{2,1,0:T(8,128)}, f32[16,128,128]{2,1,0:T(8,128)}, u32[]{:S(2)}, u32[]{:S(2)}) collective-permute-start(f32[16,128,128]{2,1,0:T(8,128)} %bitcast.32), channel_id=1, source_target_pairs={{0,8},{1,9},{2,10},{3,11},{4,12},{5,13},{6,14},{7,15},{16,24},{17,... | collective-permute-start | bytes 3145736 | tf_op jit(solution)/shard_map/ppermute | solution.py:12
  207.5 3.1 copy-start.6
  213.9 155.1 %copy-start.13 = (f32[1,8]{1,0:T(1,128)S(1)}, f32[1,8]{1,0:T(1,128)}, u32[]{:S(2)}) copy-start(f32[1,8]{1,0:T(1,128)} %param.20) | copy-start | bytes 100
  213.9 218.6 %copy-start.10 = (f32[1,1,128,128]{3,2,1,0:T(8,128)S(1)}, f32[1,1,128,128]{3,2,1,0:T(8,128)}, u32[]{:S(2)}) copy-start(f32[1,1,128,128]{3,2,1,0:T(8,128)} %param.17) | copy-start | bytes 196612
  368.1 0.8 copy-start.7
Sparse Core Ops, SparseCore 0:
  369.1 63.3 reduce-scatter.1
where the time goes:
time: 468 us; the launch traced here: 467 us
  matrix products  159 us (34%)
  local copies, waits for them, and re-layouts  112 us (24%)
  waiting for transfers between devices  62.9 us (13%)
  other arithmetic  60.1 us (13%)
  blocking collectives  53.1 us (11%)
  between operations  16.8 us (4%)
    reduce_scatter x1, waiting for transfers between devices, shards(): lax.psum_scatter(partial_value, 'tile', scatter_dimension=0, tiled=True)  62.9 us
    dot_general x4, matrix products, renew_one_turn(): jnp.einsum('csji,csjk->csik', gathered[top_part], inner, precision=lax.Pr...  53.8 us
    scatter-add x4, other arithmetic, apply_one_turn(): jax.ops.segment_sum(contrib.reshape(-1, tile_width, tile_width), dst_part...  51.6 us
    dot_general x4, matrix products, renew_one_turn(): jnp.einsum('csij,csjk->csik', own_env[block_part], gathered[bottom_part],...  44.4 us
    all_gather x1, blocking collectives, shards(): gathered = lax.all_gather(own_psi, 'tile', axis=0, tiled=True)  33 us
    dot_general x4, matrix products, apply_one_turn(): jnp.einsum('csij,cjk->csik', gathered[src_part], right_part, precision=la...  32.1 us
    dot_general x4, matrix products, apply_one_turn(): jnp.einsum('cij,csjk->csik', env_part, inner, precision=lax.Precision.HIG...  29 us
    reshape x4, local copies, waits for them, and re-layouts, apply_one_turn(): contrib.reshape(-1, tile_width, tile_width)  26.1 us
  transfers between devices with their start and end apart: 2, of which 1 were waited for; matrix products, arithmetic and copies ran while one was open for 2% of the time, Pallas kernels for 0%

commit v1 on v0

--- a/solution.py
+++ b/solution.py
@@ -1,9 +1,18 @@
+import functools
+
 import jax
 import jax.numpy as jnp
 from jax import lax
+from jax.experimental import pallas as pl
+from jax.experimental.pallas import tpu as pltpu
 from jax.sharding import PartitionSpec as P
 
 MAXT = 24
+F32 = jnp.float32
+BF16 = jnp.bfloat16
+VMEM = pl.BlockSpec(memory_space=pltpu.VMEM)
+SMEM = pl.BlockSpec(memory_space=pltpu.SMEM)
+ANY = pl.BlockSpec(memory_space=pl.ANY)
 
 
 def passed_along(value, axis, steps):
@@ -91,7 +100,7 @@
     return stacked.reshape(channels, tile_width, tile_width)
 
 
-def shards(
+def general_shards(
     psi,
     left_env,
     right_env,
@@ -137,24 +146,297 @@
     return (residual[None], renewal[None], jnp.reshape(quotient, (1,)))
 
 
+def heads_tails(value):
+    head = value.astype(BF16)
+    return head, (value - head.astype(F32)).astype(BF16)
+
+
+def add_entries(total, entries, dst, src, coef, blocks):
+    blocks[...] = jnp.zeros_like(blocks)
+
+    def step(e, unused):
+        target = dst[e]
+        blocks[target] += coef[e] * entries[src[e]]
+        return unused
+
+    lax.fori_loop(0, total, step, 0, unroll=4)
+
+
+def renew_kernel(*refs):
+    n = len(refs) - 9
+    dst, src, coef = refs[:3]
+    tiles = refs[3 : 3 + n]
+    env, out, bottoms, tops, entries, blocks = refs[3 + n : 9 + n]
+    channels, w = env.shape[0], env.shape[1]
+    for k in range(n):
+        at = slice(k * w, (k + 1) * w)
+        value = tiles[k][...]
+        head, tail = heads_tails(value)
+        bottoms[0:w, at] = head
+        bottoms[w : 2 * w, at] = head
+        bottoms[2 * w : 3 * w, at] = tail
+        bottoms[3 * w : 4 * w, at] = tail
+        head, tail = heads_tails(value.T)
+        tops[0:w, at] = head
+        tops[w : 2 * w, at] = tail
+    group = channels // 2
+
+    def products(g, unused):
+        head, tail = heads_tails(env[pl.ds(g * group, group)].reshape(group * w, w))
+        both = jnp.concatenate([head, tail, head, tail], axis=1)
+        found = jnp.dot(both, bottoms[...], preferred_element_type=F32)
+        for h in range(group):
+            for k in range(n):
+                entries[(g * group + h) * n + k] = found[h * w : (h + 1) * w, k * w : (k + 1) * w]
+        return unused
+
+    lax.fori_loop(0, 2, products, 0)
+    add_entries(dst.shape[0], entries, dst, src, coef, blocks)
+
+    def finish(b, unused):
+        head, tail = heads_tails(blocks[pl.ds(b * n, n)].reshape(n * w, w))
+        both = jnp.concatenate([head, tail], axis=1)
+        found = jnp.dot(tops[...], both, preferred_element_type=F32)
+        out[b] = (found[:w, :w] + found[w:, w:]) + (found[:w, w:] + found[w:, :w])
+        return unused
+
+    lax.fori_loop(0, channels, finish, 0, unroll=4)
+
+
+def renew_call(dst, src, coef, tiles, env):
+    n, w, channels = len(tiles), env.shape[1], env.shape[0]
+    return pl.pallas_call(
+        renew_kernel,
+        out_shape=jax.ShapeDtypeStruct(env.shape, F32),
+        in_specs=[SMEM] * 3 + [VMEM] * (n + 1),
+        out_specs=VMEM,
+        scratch_shapes=[
+            pltpu.VMEM((4 * w, n * w), BF16),
+            pltpu.VMEM((2 * w, n * w), BF16),
+            pltpu.VMEM((channels * n, w, w), F32),
+            pltpu.VMEM((channels * n, w, w), F32),
+        ],
+        compiler_params=pltpu.CompilerParams(vmem_limit_bytes=40 << 20),
+        cost_estimate=pl.CostEstimate(flops=10**10, bytes_accessed=3 << 20, transcendentals=0),
+        name="renew",
+    )(dst, src, coef, *tiles, env)
+
+
+def source_kernel(n, dst, src, coef, energies, *refs):
+    tiles = refs[:n]
+    right, out, stats, sources, entries, blocks = refs[n:]
+    channels, w = right.shape[0], right.shape[1]
+    weight = jnp.zeros((8, w), F32)
+    energy = jnp.zeros((8, w), F32)
+    for k in range(n):
+        at = slice(k * w, (k + 1) * w)
+        value = tiles[k][...]
+        head, tail = heads_tails(value)
+        sources[at, 0:w] = head
+        sources[at, w : 2 * w] = tail
+        sources[at, 2 * w : 3 * w] = head
+        sources[at, 3 * w : 4 * w] = tail
+        squares = jnp.sum((value * value).reshape(w // 8, 8, w), axis=0)
+        weight += squares
+        energy += energies[k] * squares
+    stats[0:8] = weight
+    stats[8:16] = energy
+
+    def products(g, unused):
+        columns = []
+        for h in range(2):
+            head, tail = heads_tails(right[2 * g + h])
+            columns.append(jnp.concatenate([head, head, tail, tail], axis=0))
+        found = jnp.dot(sources[...], jnp.concatenate(columns, axis=1), preferred_element_type=F32)
+        for h in range(2):
+            for k in range(n):
+                entries[(2 * g + h) * n + k] = found[k * w : (k + 1) * w, h * w : (h + 1) * w]
+        return unused
+
+    lax.fori_loop(0, channels // 2, products, 0, unroll=2)
+    add_entries(dst.shape[0], entries, dst, src, coef, blocks)
+
+    def finish(c, unused):
+        for k in range(n):
+            head, tail = heads_tails(blocks[c * n + k])
+            rows = pl.ds(pl.multiple_of(c * w, w), w)
+            out[k, rows, 0:w] = head
+            out[k, rows, w : 2 * w] = tail
+        return unused
+
+    lax.fori_loop(0, channels, finish, 0)
+
+
+def source_call(dst, src, coef, energies, tiles, right):
+    n, w, channels = len(tiles), right.shape[1], right.shape[0]
+    return pl.pallas_call(
+        functools.partial(source_kernel, n),
+        out_shape=(
+            jax.ShapeDtypeStruct((n, channels * w, 2 * w), BF16),
+            jax.ShapeDtypeStruct((16, w), F32),
+        ),
+        in_specs=[SMEM] * 4 + [VMEM] * (n + 1),
+        out_specs=(VMEM, VMEM),
+        scratch_shapes=[
+            pltpu.VMEM((n * w, 4 * w), BF16),
+            pltpu.VMEM((channels * n, w, w), F32),
+            pltpu.VMEM((channels * n, w, w), F32),
+        ],
+        compiler_params=pltpu.CompilerParams(vmem_limit_bytes=48 << 20),
+        cost_estimate=pl.CostEstimate(flops=10**10, bytes_accessed=10 << 20, transcendentals=0),
+        name="sources",
+    )(dst, src, coef, energies, *tiles, right)
+
+
+def apply_kernel(n, *refs):
+    tiles = refs[:n]
+    own, received, blocks = refs[n : n + 3]
+    outs = refs[n + 3 : 2 * n + 3]
+    env, lefts, arrived = refs[2 * n + 3 :]
+    channels, w = env.shape[0], env.shape[1]
+    leading = lax.axis_index("seg") == 0
+
+    @pl.when(leading)
+    def _():
+        pltpu.make_async_copy(own, env, arrived).start()
+
+    @pl.when(jnp.logical_not(leading))
+    def _():
+        pltpu.make_async_copy(received, env, arrived).start()
+
+    pltpu.make_async_copy(own, env, arrived).wait()
+    for c in range(channels):
+        head, tail = heads_tails(env[c])
+        lefts[0:w, c * w : (c + 1) * w] = head
+        lefts[w : 2 * w, c * w : (c + 1) * w] = tail
+    inner = jnp.zeros((8, w), F32)
+    for k in range(n):
+        found = jnp.dot(lefts[...], blocks[k], preferred_element_type=F32)
+        value = (found[:w, :w] + found[w:, w:]) + (found[:w, w:] + found[w:, :w])
+        outs[k][0:w] = value
+        inner += jnp.sum((value * tiles[k][...]).reshape(w // 8, 8, w), axis=0)
+    for k in range(n):
+        outs[k][w : w + 8] = inner
+
+
+def apply_call(tiles, own, received, blocks):
+    n, w = len(tiles), own.shape[1]
+    return pl.pallas_call(
+        functools.partial(apply_kernel, n),
+        out_shape=tuple(jax.ShapeDtypeStruct((w + 8, w), F32) for _ in range(n)),
+        in_specs=[VMEM] * n + [ANY, ANY, VMEM],
+        out_specs=(VMEM,) * n,
+        scratch_shapes=[
+            pltpu.VMEM(own.shape, F32),
+            pltpu.VMEM((2 * w, own.shape[0] * w), BF16),
+            pltpu.SemaphoreType.DMA,
+        ],
+        compiler_params=pltpu.CompilerParams(vmem_limit_bytes=32 << 20),
+        cost_estimate=pl.CostEstimate(flops=5 * 10**9, bytes_accessed=10 << 20, transcendentals=0),
+        name="applied",
+    )(*tiles, own, received, blocks)
+
+
+def finish_kernel(energy, *refs):
+    parts = refs[:-4]
+    own, stats, residual, quotient = refs[-4:]
+    w = own.shape[0]
+    total = parts[0][...]
+    for part in parts[1:]:
+        total = total + part[...]
+    value = own[...]
+    numerator = jnp.sum(total[w : w + 8]) + jnp.sum(stats[8:16])
+    ratio = jnp.full((1, 128), numerator, F32) / jnp.full((1, 128), jnp.sum(stats[0:8]), F32)
+    residual[...] = total[:w] + (energy[0] - ratio) * value
+    quotient[...] = ratio
+
+
+def finish_call(energy, parts, own, stats):
+    w = own.shape[0]
+    return pl.pallas_call(
+        finish_kernel,
+        out_shape=(jax.ShapeDtypeStruct((w, w), F32), jax.ShapeDtypeStruct((1, 128), F32)),
+        in_specs=[SMEM] + [VMEM] * (len(parts) + 2),
+        out_specs=(VMEM, VMEM),
+        name="finish",
+    )(energy, *parts, own, stats)
+
+
+def channel_of(counts, live):
+    ends = jnp.cumsum(counts)
+    return jnp.sum((jnp.arange(live)[:, None] >= ends[None, :]).astype(jnp.int32), axis=1)
+
+
+def shards(
+    psi,
+    left_env,
+    right_env,
+    site_energy,
+    mv_counts,
+    mv_src,
+    mv_dst,
+    mv_coef,
+    up_counts,
+    up_block,
+    up_top,
+    up_bot,
+    up_coef,
+):
+    n = lax.axis_size("tile")
+    me = lax.axis_index("tile")
+    live = mv_src.shape[2]
+
+    def across(value, k):
+        return lax.ppermute(value, "tile", [(i, i ^ k) for i in range(n)])
+
+    own = psi[0, 0]
+    tiles = {0: own, 1: across(own, 1)}
+    for k in range(n - 2, 0, -2):
+        tiles[k] = across(own, k)
+    for k in range(2, n, 2):
+        tiles[k + 1] = across(tiles[k], 1)
+    tiles = [tiles[k] for k in range(n)]
+
+    up_channel = channel_of(up_counts[0, 0], live)
+    up_dst = up_channel * n + (up_top[0, 0] ^ me)
+    up_from = up_block[0, 0] * n + (up_bot[0, 0] ^ me)
+    mv_channel = channel_of(mv_counts[0, 0], live)
+    mv_to = mv_channel * n + (mv_dst[0, 0] ^ me)
+    mv_from = mv_channel * n + (mv_src[0, 0] ^ me)
+    energies = site_energy[0][jnp.arange(n) ^ me]
+
+    renewal = renew_call(up_dst, up_from, up_coef[0, 0], tiles, left_env[0])
+    received = passed_along(renewal, "seg", 1)
+    blocks, stats = source_call(mv_to, mv_from, mv_coef[0, 0], energies, tiles, right_env[0])
+    partials = apply_call(tiles, left_env[0], received, blocks)
+
+    parts = [partials[0]]
+    for k in range(n - 2, 0, -2):
+        parts.append(across(partials[k] + across(partials[k + 1], 1), k))
+    parts.append(across(partials[1], 1))
+    residual, quotient = finish_call(energies, parts, own, stats)
+    return (residual[None, None], renewal[None], quotient[0, :1])
+
+
 def solution(mesh):
+    per_run = P(("parts", "seg"), "tile", None)
     return jax.shard_map(
-        shards,
+        shards if mesh.shape["tile"] == 8 else general_shards,
         mesh=mesh,
         in_specs=(
             P(("parts", "seg"), "tile", None, None),
             P(("parts", "seg"), "tile", None, None),
             P(("parts", "seg"), "tile", None, None),
             P(("parts", "seg"), None),
-            P(("parts", "seg"), "tile", None),
-            P(("parts", "seg"), "tile", None),
-            P(("parts", "seg"), "tile", None),
-            P(("parts", "seg"), "tile", None),
-            P(("parts", "seg"), "tile", None),
-            P(("parts", "seg"), "tile", None),
-            P(("parts", "seg"), "tile", None),
-            P(("parts", "seg"), "tile", None),
-            P(("parts", "seg"), "tile", None),
+            per_run,
+            per_run,
+            per_run,
+            per_run,
+            per_run,
+            per_run,
+            per_run,
+            per_run,
+            per_run,
         ),
         out_specs=(
             P(("parts", "seg"), "tile", None, None),

time: 468 us -> 66.1 us (0.14)
  matrix products: 159 us -> 0 us
  local copies, waits for them, and re-layouts: 112 us -> 9.54 us
  other arithmetic: 60.1 us -> 2.62 us
  waiting for transfers between devices: 62.9 us -> 8.08 us
  blocking collectives: 53.1 us -> 0 us
  Pallas kernels: 0 us -> 24.4 us
  starting transfers between devices: 2.45 us -> 20.3 us
  between operations: 16.8 us -> 0.82 us
    dot_general x16 -> x0, matrix products: 159 us -> none  [the longest x4 53.8 us: renew_one_turn(): jnp.einsum('csji,csjk->csik', gathered[top_part], inner, precision=lax.Pr...]
    gather x25 -> x1, local copies, waits for them, and re-layouts: 77.4 us -> 0.64 us  [shards(): energies = site_energy[0][jnp.arange(n) ^ me]]
    reduce_scatter x1 -> x0, waiting for transfers between devices: 62.9 us -> none  [shards(): lax.psum_scatter(partial_value, 'tile', scatter_dimension=0, tiled=True)]
    scatter-add x4 -> x0, other arithmetic: 51.6 us -> none  [apply_one_turn(): jax.ops.segment_sum(contrib.reshape(-1, tile_width, tile_width), dst_part...]
    all_gather x1 -> x0, blocking collectives: 33 us -> none  [shards(): gathered = lax.all_gather(own_psi, 'tile', axis=0, tiled=True)]
    reshape x13 -> x0, local copies, waits for them, and re-layouts: 26.9 us -> none  [the longest x4 26.1 us: apply_one_turn(): contrib.reshape(-1, tile_width, tile_width)]
    pallas_call x0 -> x4, Pallas kernels: none -> 24.4 us  [the longest x1 10.5 us: source_call(): pl.pallas_call(functools.partial(source_kernel, n), out_shape=(jax.ShapeD...]
    psum x1 -> x0, blocking collectives: 20.1 us -> none  [shards(): numerator = lax.psum(jnp.sum(own_psi * own_rows), 'tile')]
  transfers between devices with their start and end apart: 2 -> 15, of which waited for: 1 -> 6; matrix products, arithmetic and copies ran while one was open for 2% -> 7% of each run, Pallas kernels for 0% -> 16%
where the time goes in v1:
time: 66.1 us; the launch traced here: 65.7 us
  Pallas kernels  24.4 us (37%)
  starting transfers between devices  20.3 us (31%)
  local copies, waits for them, and re-layouts  9.54 us (14%)
  waiting for transfers between devices  8.08 us (12%)
  other arithmetic  2.62 us (4%)
  between operations  0.82 us (1%)
    ppermute x14, starting transfers between devices, across(): return lax.ppermute(value, 'tile', [(i, i ^ k) for i in range(n)])  18.9 us
    pallas_call x1, Pallas kernels, source_call(): pl.pallas_call(functools.partial(source_kernel, n), out_shape=(jax.ShapeD...  10.5 us
    pallas_call x1, Pallas kernels, renew_call(): pl.pallas_call(renew_kernel, out_shape=jax.ShapeDtypeStruct(env.shape, F3...  9.52 us
    ppermute x14, waiting for transfers between devices, across(): return lax.ppermute(value, 'tile', [(i, i ^ k) for i in range(n)])  8.07 us
    unnamed x32, local copies, waits for them, and re-layouts  7.44 us
    pallas_call x1, Pallas kernels, apply_call(): pl.pallas_call(functools.partial(apply_kernel, n), out_shape=tuple((jax.S...  2.52 us
    pallas_call x1, Pallas kernels, finish_call(): pl.pallas_call(finish_kernel, out_shape=(jax.ShapeDtypeStruct((w, w), F32...  1.83 us
    another operation x2, local copies, waits for them, and re-layouts  1.46 us
  transfers between devices with their start and end apart: 15, of which 6 were waited for; matrix products, arithmetic and copies ran while one was open for 7% of the time, Pallas kernels for 16%

profile of v1, /device:TPU:0, one launch (start us, length us, event | category | flops | bytes accessed | tf_op | source)
XLA Modules:
  0.0 65.7 jit_solution(12791698300034550915)
XLA Ops:
  0.6 0.0 copy-start
  0.6 5.1 %collective-permute-start.5 = (f32[128,128]{1,0:T(8,128)}, f32[128,128]{1,0:T(8,128)S(1)}, u32[]{:S(2)}, u32[]{:S(2)}) collective-permute-start(f32[128,128]{1,0:T(8,128)} %bitcast.19), channel_id=1, source_target_pairs={{0,6},{1,7},{2,4},{3,5},{4,2},{5,3},{6,0},{7,1},{8,14},{9,15},{10,... | collective-permute-start | bytes 196616 | tf_op jit(solution)/shard_map/ppermute | solution.py:390
  5.8 0.0 collective-permute-start.3
  5.8 0.6 collective-permute-start.1
  6.4 1.7 %collective-permute-start = (f32[128,128]{1,0:T(8,128)}, f32[128,128]{1,0:T(8,128)S(1)}, u32[]{:S(2)}, u32[]{:S(2)}) collective-permute-start(f32[128,128]{1,0:T(8,128)} %bitcast.22), channel_id=1, source_target_pairs={{0,1},{1,0},{2,3},{3,2},{4,5},{5,4},{6,7},{7,6},{8,9},{9,8},{10,11... | collective-permute-start | bytes 196616 | tf_op jit(solution)/shard_map/ppermute | solution.py:390
  8.1 0.7 %copy.21 = s32[16,1]{1,0:T(8,128)S(1)} copy(s32[16,1]{0,1:T(1,128)} %bitcast.36) | data formatting | bytes 128 | tf_op jit(solution)/shard_map/reshape.55
  8.8 0.1 reduce.1
  9.0 0.1 convert_reduce_fusion
  9.0 0.7 %copy.20 = s32[16,1]{1,0:T(8,128)S(1)} copy(s32[16,1]{0,1:T(1,128)} %bitcast.37) | data formatting | bytes 128 | tf_op jit(solution)/shard_map/reshape.53
  9.8 0.1 reduce
  9.9 0.1 convert_reduce_fusion.1
  10.0 0.7 %broadcast_xor_fusion.2 = s32[1,1,192]{2,1,0:T(1,128)S(1)} fusion(s32[1,1,192]{2,1,0:T(1,128)} %param.23, s32[]{:T(128)S(6)} %axis_index.12), kind=kLoop, calls=%fused_computation.14 | loop fusion | flops 192 | bytes 1540 | tf_op jit(solution)/shard_map/xor | solution.py:401
  10.7 0.7 %xor_add_fusion = s32[1,1,192]{2,1,0:T(1,128)S(1)} fusion(s32[1,1,192]{2,1,0:T(1,128)} %param.24, s32[1,1,192]{2,1,0:T(1,128)} %param.22, s32[]{:T(128)S(6)} %axis_index.12), kind=kLoop, calls=%fused_computation.7 | loop fusion | flops 576 | bytes 2308 | tf_op jit(solution)/shard_map/add | solution.py:402
  11.4 0.7 %broadcast_xor_fusion = (s32[1,1,192]{2,1,0:T(1,128)S(1)}, s32[1,1,192]{2,1,0:T(1,128)S(1)}) fusion(s32[1,1,192]{2,1,0:T(1,128)} %param.18, s32[]{:T(128)S(6)} %axis_index.12, s32[1,1,192]{2,1,0:T(1,128)} %param.19), kind=kLoop, calls=%fused_computation.12 | loop fusion | flops 384 | bytes 3076 | tf_op jit(solution)/shard_map/xor | solution.py:405
  12.1 0.0 collective-permute-done.5.refs_9_.refs_6_
  12.1 0.5 collective-permute-start.6
  12.6 0.0 collective-permute-done.3.refs_7_.refs_4_
  12.6 1.6 %collective-permute-start.4 = (f32[128,128]{1,0:T(8,128)S(1)}, f32[128,128]{1,0:T(8,128)S(1)}, u32[]{:S(2)}, u32[]{:S(2)}) collective-permute-start(f32[128,128]{1,0:T(8,128)S(1)} %collective-permute-done.3.refs_7_.refs_4_), channel_id=1, source_target_pairs={{0,1},{1,0},{2,3},{3,2},{4,5},{5,4},{6,7},{7,6},{8,9},{9,8},{10,11... | collective-permute-start | bytes 196616 | tf_op jit(solution)/shard_map/ppermute | solution.py:390
  14.2 0.0 collective-permute-done.1.refs_5_.refs_2_
  14.2 0.4 collective-permute-start.2
  14.6 2.0 %collective-permute-done.6.refs_10_.refs_7_ = f32[128,128]{1,0:T(8,128)S(1)} collective-permute-done((f32[128,128]{1,0:T(8,128)S(1)}, f32[128,128]{1,0:T(8,128)S(1)}, u32[]{:S(2)}, u32[]{:S(2)}) %collective-permute-start.6) | collective-permute-done | bytes 65568 | tf_op jit(solution)/shard_map/ppermute | solution.py:390
  16.7 0.7 %collective-permute-done.4.refs_8_.refs_5_ = f32[128,128]{1,0:T(8,128)S(1)} collective-permute-done((f32[128,128]{1,0:T(8,128)S(1)}, f32[128,128]{1,0:T(8,128)S(1)}, u32[]{:S(2)}, u32[]{:S(2)}) %collective-permute-start.4) | collective-permute-done | bytes 65568 | tf_op jit(solution)/shard_map/ppermute | solution.py:390
  17.4 1.1 %collective-permute-done.2.refs_6_.refs_3_ = f32[128,128]{1,0:T(8,128)S(1)} collective-permute-done((f32[128,128]{1,0:T(8,128)S(1)}, f32[128,128]{1,0:T(8,128)S(1)}, u32[]{:S(2)}, u32[]{:S(2)}) %collective-permute-start.2) | collective-permute-done | bytes 65568 | tf_op jit(solution)/shard_map/ppermute | solution.py:390
  18.5 0.8 %copy-done.2 = f32[1,1,128,128]{3,2,1,0:T(8,128)S(1)} copy-done((f32[1,1,128,128]{3,2,1,0:T(8,128)S(1)}, f32[1,1,128,128]{3,2,1,0:T(8,128)}, u32[]{:S(2)}) %copy-start.2) | copy-done | bytes 65560
  19.3 1.2 %copy-done.7 = f32[1,16,128,128]{3,2,1,0:T(8,128)S(1)} copy-done((f32[1,16,128,128]{3,2,1,0:T(8,128)S(1)}, f32[1,16,128,128]{3,2,1,0:T(8,128)}, u32[]{:S(2)}) %copy-start.7) | copy-done | bytes 1048600
  20.6 0.7 %copy-done.9 = f32[1,1,192]{2,1,0:T(1,128)S(1)} copy-done((f32[1,1,192]{2,1,0:T(1,128)S(1)}, f32[1,1,192]{2,1,0:T(1,128)}, u32[]{:S(2)}) %copy-start.9) | copy-done | bytes 792
  21.2 9.5 %renew.1 = f32[16,128,128]{2,1,0:T(8,128)} custom-call(s32[192]{0:T(256)S(1)} %multiply_add_fusion.refs_0_, s32[192]{0:T(256)S(1)} %bitcast.27, f32[192]{0:T(256)S(1)} %bitcast.31, f32[128,128]{1,0:T(8,128)S(1)} %bitcast.24, f32[128,128]{1,0:T(8,128)S(1)} %collective-permute-done.refs_4_.refs_1_, f32[128,128]{1,0:T(8,128)S(1)} %collective-permute-done.1.refs_5_.refs_2_, ...), custom_call_target="tpu_custom_call" | custom-call | flops 10000000000 | bytes 3145728 | tf_op jit(solution)/shard_map/renew/pallas_call | solution.py:208
  30.8 1.3 %collective-permute-start.7 = (f32[16,128,128]{2,1,0:T(8,128)}, f32[16,128,128]{2,1,0:T(8,128)S(1)}, u32[]{:S(2)}, u32[]{:S(2)}) collective-permute-start(f32[16,128,128]{2,1,0:T(8,128)} %renew.1), channel_id=1, source_target_pairs={{0,8},{1,9},{2,10},{3,11},{4,12},{5,13},{6,14},{7,15},{16,24},{17,... | collective-permute-start | bytes 3145736 | tf_op jit(solution)/shard_map/ppermute | solution.py:21
  32.1 0.6 gather_fusion
  32.8 0.0 copy-start.8
  32.8 10.5 %sources.1 = (bf16[8,2048,256]{2,1,0:T(8,128)(2,1)}, f32[16,128]{1,0:T(8,128)S(1)}) custom-call(s32[192]{0:T(256)S(1)} %get-tuple-element.28.dst, s32[192]{0:T(256)S(1)} %get-tuple-element.27.src, f32[192]{0:T(256)S(1)} %bitcast.32, f32[8]{0:T(128)S(1)} %gather_fusion, f32[128,128]{1,0:T(8,128)S(1)} %bitcast.25, ...), custom_call_target="tpu_custom_call" | custom-call | flops 10000000000 | bytes 10485760 | tf_op jit(solution)/shard_map/sources/pallas_call | solution.py:272
  43.4 0.0 collective-permute-done.7.refs_9_
  43.4 3.4 %copy-done.11 = bf16[8,2048,256]{2,1,0:T(8,128)(2,1)S(1)} copy-done((bf16[8,2048,256]{2,1,0:T(8,128)(2,1)S(1)}, bf16[8,2048,256]{2,1,0:T(8,128)(2,1)}, u32[]{:S(2)}) %copy-start.11) | copy-done | bytes 8388632
  46.8 2.5 %applied.1 = (f32[136,128]{1,0:T(8,128)S(1)}, f32[136,128]{1,0:T(8,128)S(1)}, f32[136,128]{1,0:T(8,128)S(1)}, f32[136,128]{1,0:T(8,128)S(1)}, f32[136,128]{1,0:T...) custom-call(f32[128,128]{1,0:T(8,128)S(1)} %bitcast.26, ...), custom_call_target="tpu_custom_call" | custom-call | flops 5000000000 | bytes 10485760 | tf_op jit(solution)/shard_map/applied/pallas_call | solution.py:324
  49.3 0.6 copy-done.1
  49.9 0.7 %collective-permute-start.8 = (f32[136,128]{1,0:T(8,128)S(1)}, f32[136,128]{1,0:T(8,128)S(1)}, u32[]{:S(2)}, u32[]{:S(2)}) collective-permute-start(f32[136,128]{1,0:T(8,128)S(1)} %get-tuple-element.18), channel_id=1, source_target_pairs={{0,1},{1,0},{2,3},{3,2},{4,5},{5,4},{6,7},{7,6},{8,9},{9,8},{10,11... | collective-permute-start | bytes 208904 | tf_op jit(solution)/shard_map/ppermute | solution.py:390
  50.6 1.3 %collective-permute-start.10 = (f32[136,128]{1,0:T(8,128)S(1)}, f32[136,128]{1,0:T(8,128)S(1)}, u32[]{:S(2)}, u32[]{:S(2)}) collective-permute-start(f32[136,128]{1,0:T(8,128)S(1)} %get-tuple-element.20), channel_id=1, source_target_pairs={{0,1},{1,0},{2,3},{3,2},{4,5},{5,4},{6,7},{7,6},{8,9},{9,8},{10,11... | collective-permute-start | bytes 208904 | tf_op jit(solution)/shard_map/ppermute | solution.py:390
  52.0 0.7 %collective-permute-start.12 = (f32[136,128]{1,0:T(8,128)S(1)}, f32[136,128]{1,0:T(8,128)S(1)}, u32[]{:S(2)}, u32[]{:S(2)}) collective-permute-start(f32[136,128]{1,0:T(8,128)S(1)} %get-tuple-element.22), channel_id=1, source_target_pairs={{0,1},{1,0},{2,3},{3,2},{4,5},{5,4},{6,7},{7,6},{8,9},{9,8},{10,11... | collective-permute-start | bytes 208904 | tf_op jit(solution)/shard_map/ppermute | solution.py:390
  52.7 1.3 %collective-permute-start.14 = (f32[136,128]{1,0:T(8,128)S(1)}, f32[136,128]{1,0:T(8,128)S(1)}, u32[]{:S(2)}, u32[]{:S(2)}) collective-permute-start(f32[136,128]{1,0:T(8,128)S(1)} %get-tuple-element.23), channel_id=1, source_target_pairs={{0,1},{1,0},{2,3},{3,2},{4,5},{5,4},{6,7},{7,6},{8,9},{9,8},{10,11... | collective-permute-start | bytes 208904 | tf_op jit(solution)/shard_map/ppermute | solution.py:390
  54.0 0.3 collective-permute-done.8
  54.3 3.6 %collective-permute-start.9 = (f32[136,128]{1,0:T(8,128)S(1)}, f32[136,128]{1,0:T(8,128)S(1)}, u32[]{:S(2)}, u32[]{:S(2)}) collective-permute-start(f32[136,128]{1,0:T(8,128)S(1)} %add.39), channel_id=1, source_target_pairs={{0,6},{1,7},{2,4},{3,5},{4,2},{5,3},{6,0},{7,1},{8,14},{9,15},{10,... | collective-permute-start | bytes 208904 | tf_op jit(solution)/shard_map/ppermute | solution.py:390
  58.0 0.1 collective-permute-start.11
  58.1 1.3 %collective-permute-start.13 = (f32[136,128]{1,0:T(8,128)S(1)}, f32[136,128]{1,0:T(8,128)S(1)}, u32[]{:S(2)}, u32[]{:S(2)}) collective-permute-start(f32[136,128]{1,0:T(8,128)S(1)} %add.41), channel_id=1, source_target_pairs={{0,2},{1,3},{2,0},{3,1},{4,6},{5,7},{6,4},{7,5},{8,10},{9,11},{10,... | collective-permute-start | bytes 208904 | tf_op jit(solution)/shard_map/ppermute | solution.py:390
  59.3 1.1 %collective-permute-done.9.refs_1_ = f32[136,128]{1,0:T(8,128)S(1)} collective-permute-done((f32[136,128]{1,0:T(8,128)S(1)}, f32[136,128]{1,0:T(8,128)S(1)}, u32[]{:S(2)}, u32[]{:S(2)}) %collective-permute-start.9) | collective-permute-done | bytes 69664 | tf_op jit(solution)/shard_map/ppermute | solution.py:390
  60.5 2.7 %collective-permute-done.11.refs_2_ = f32[136,128]{1,0:T(8,128)S(1)} collective-permute-done((f32[136,128]{1,0:T(8,128)S(1)}, f32[136,128]{1,0:T(8,128)S(1)}, u32[]{:S(2)}, u32[]{:S(2)}) %collective-permute-start.11) | collective-permute-done | bytes 69664 | tf_op jit(solution)/shard_map/ppermute | solution.py:390
  63.2 0.6 copy-done.14
  63.8 0.0 copy-done.15
  63.9 1.8 %finish.1 = (f32[128,128]{1,0:T(8,128)}, f32[1,128]{1,0:T(1,128)}) custom-call(f32[8]{0:T(128)} %copy-done.5, f32[136,128]{1,0:T(8,128)} %copy-done.1, f32[136,128]{1,0:T(8,128)} %copy-done.13, f32[136,128]{1,0:T(8,128)} %copy-done.14, f32[136,128]{1,0:T(8,128)} %copy-done.15, f32[136,128]{1,0:T(8,128)} %copy-done.12, f32[128,128]{1,0:T(8,128)} %bitcast.23, ...), custom_call_target="tpu_custom_call" | custom-call | tf_op jit(solution)/shard_map/finish/pallas_call | solution.py:356
  (37 shorter events, 0.2 us)
Async XLA Ops:
  0.6 31.5 %copy-start = (f32[1,8]{1,0:T(1,128)S(1)}, f32[1,8]{1,0:T(1,128)}, u32[]{:S(2)}) copy-start(f32[1,8]{1,0:T(1,128)} %param.16) | copy-start | bytes 100
  0.6 11.5 %collective-permute-start.5 = (f32[128,128]{1,0:T(8,128)}, f32[128,128]{1,0:T(8,128)S(1)}, u32[]{:S(2)}, u32[]{:S(2)}) collective-permute-start(f32[128,128]{1,0:T(8,128)} %bitcast.19), channel_id=1, source_target_pairs={{0,6},{1,7},{2,4},{3,5},{4,2},{5,3},{6,0},{7,1},{8,14},{9,15},{10,... | collective-permute-start | bytes 196616 | tf_op jit(solution)/shard_map/ppermute | solution.py:390
  5.8 6.8 %collective-permute-start.3 = (f32[128,128]{1,0:T(8,128)}, f32[128,128]{1,0:T(8,128)S(1)}, u32[]{:S(2)}, u32[]{:S(2)}) collective-permute-start(f32[128,128]{1,0:T(8,128)} %bitcast.20), channel_id=1, source_target_pairs={{0,4},{1,5},{2,6},{3,7},{4,0},{5,1},{6,2},{7,3},{8,12},{9,13},{10,... | collective-permute-start | bytes 196616 | tf_op jit(solution)/shard_map/ppermute | solution.py:390
  5.8 8.5 %collective-permute-start.1 = (f32[128,128]{1,0:T(8,128)}, f32[128,128]{1,0:T(8,128)S(1)}, u32[]{:S(2)}, u32[]{:S(2)}) collective-permute-start(f32[128,128]{1,0:T(8,128)} %bitcast.21), channel_id=1, source_target_pairs={{0,2},{1,3},{2,0},{3,1},{4,6},{5,7},{6,4},{7,5},{8,10},{9,11},{10,... | collective-permute-start | bytes 196616 | tf_op jit(solution)/shard_map/ppermute | solution.py:390
  6.4 8.2 %collective-permute-start = (f32[128,128]{1,0:T(8,128)}, f32[128,128]{1,0:T(8,128)S(1)}, u32[]{:S(2)}, u32[]{:S(2)}) collective-permute-start(f32[128,128]{1,0:T(8,128)} %bitcast.22), channel_id=1, source_target_pairs={{0,1},{1,0},{2,3},{3,2},{4,5},{5,4},{6,7},{7,6},{8,9},{9,8},{10,11... | collective-permute-start | bytes 196616 | tf_op jit(solution)/shard_map/ppermute | solution.py:390
  12.1 4.5 %collective-permute-start.6 = (f32[128,128]{1,0:T(8,128)S(1)}, f32[128,128]{1,0:T(8,128)S(1)}, u32[]{:S(2)}, u32[]{:S(2)}) collective-permute-start(f32[128,128]{1,0:T(8,128)S(1)} %collective-permute-done.5.refs_9_.refs_6_), channel_id=1, source_target_pairs={{0,1},{1,0},{2,3},{3,2},{4,5},{5,4},{6,7},{7,6},{8,9},{9,8},{10,11... | collective-permute-start | bytes 196616 | tf_op jit(solution)/shard_map/ppermute | solution.py:390
  12.6 4.8 %collective-permute-start.4 = (f32[128,128]{1,0:T(8,128)S(1)}, f32[128,128]{1,0:T(8,128)S(1)}, u32[]{:S(2)}, u32[]{:S(2)}) collective-permute-start(f32[128,128]{1,0:T(8,128)S(1)} %collective-permute-done.3.refs_7_.refs_4_), channel_id=1, source_target_pairs={{0,1},{1,0},{2,3},{3,2},{4,5},{5,4},{6,7},{7,6},{8,9},{9,8},{10,11... | collective-permute-start | bytes 196616 | tf_op jit(solution)/shard_map/ppermute | solution.py:390
  14.2 4.3 %collective-permute-start.2 = (f32[128,128]{1,0:T(8,128)S(1)}, f32[128,128]{1,0:T(8,128)S(1)}, u32[]{:S(2)}, u32[]{:S(2)}) collective-permute-start(f32[128,128]{1,0:T(8,128)S(1)} %collective-permute-done.1.refs_5_.refs_2_), channel_id=1, source_target_pairs={{0,1},{1,0},{2,3},{3,2},{4,5},{5,4},{6,7},{7,6},{8,9},{9,8},{10,11... | collective-permute-start | bytes 196616 | tf_op jit(solution)/shard_map/ppermute | solution.py:390
  18.5 0.8 %copy-start.2 = (f32[1,1,128,128]{3,2,1,0:T(8,128)S(1)}, f32[1,1,128,128]{3,2,1,0:T(8,128)}, u32[]{:S(2)}) copy-start(f32[1,1,128,128]{3,2,1,0:T(8,128)} %param.13) | copy-start | bytes 196612
  19.3 1.2 %copy-start.7 = (f32[1,16,128,128]{3,2,1,0:T(8,128)S(1)}, f32[1,16,128,128]{3,2,1,0:T(8,128)}, u32[]{:S(2)}) copy-start(f32[1,16,128,128]{3,2,1,0:T(8,128)} %param.14) | copy-start | bytes 3145732
  20.6 0.7 %copy-start.9 = (f32[1,1,192]{2,1,0:T(1,128)S(1)}, f32[1,1,192]{2,1,0:T(1,128)}, u32[]{:S(2)}) copy-start(f32[1,1,192]{2,1,0:T(1,128)} %param.25) | copy-start | bytes 2308
  21.2 11.5 %copy-start.3 = (f32[1,1,128,128]{3,2,1,0:T(8,128)S(1)}, f32[1,1,128,128]{3,2,1,0:T(8,128)}, u32[]{:S(2)}) copy-start(f32[1,1,128,128]{3,2,1,0:T(8,128)} %param.13) | copy-start | bytes 196612
  21.2 11.6 %copy-start.6 = (f32[1,16,128,128]{3,2,1,0:T(8,128)S(1)}, f32[1,16,128,128]{3,2,1,0:T(8,128)}, u32[]{:S(2)}) copy-start(f32[1,16,128,128]{3,2,1,0:T(8,128)} %param.15) | copy-start | bytes 3145732
  21.2 11.6 %copy-start.10 = (f32[1,1,192]{2,1,0:T(1,128)S(1)}, f32[1,1,192]{2,1,0:T(1,128)}, u32[]{:S(2)}) copy-start(f32[1,1,192]{2,1,0:T(1,128)} %param.20) | copy-start | bytes 2308
  30.8 12.6 %collective-permute-start.7 = (f32[16,128,128]{2,1,0:T(8,128)}, f32[16,128,128]{2,1,0:T(8,128)S(1)}, u32[]{:S(2)}, u32[]{:S(2)}) collective-permute-start(f32[16,128,128]{2,1,0:T(8,128)} %renew.1), channel_id=1, source_target_pairs={{0,8},{1,9},{2,10},{3,11},{4,12},{5,13},{6,14},{7,15},{16,24},{17,... | collective-permute-start | bytes 3145736 | tf_op jit(solution)/shard_map/ppermute | solution.py:21
  32.8 10.6 %copy-start.5 = (f32[8]{0:T(128)}, f32[8]{0:T(128)S(1)}, u32[]{:S(2)}) copy-start(f32[8]{0:T(128)S(1)} %gather_fusion) | copy-start | bytes 100
  32.8 10.5 %copy-start.8 = (f32[1,16,128,128]{3,2,1,0:T(8,128)S(1)}, f32[1,16,128,128]{3,2,1,0:T(8,128)}, u32[]{:S(2)}) copy-start(f32[1,16,128,128]{3,2,1,0:T(8,128)} %param.14) | copy-start | bytes 3145732
  43.4 5.9 %copy-start.4 = (f32[16,128]{1,0:T(8,128)}, f32[16,128]{1,0:T(8,128)S(1)}, u32[]{:S(2)}) copy-start(f32[16,128]{1,0:T(8,128)S(1)} %get-tuple-element.24.refs_6_) | copy-start | bytes 24580
  43.4 3.4 %copy-start.11 = (bf16[8,2048,256]{2,1,0:T(8,128)(2,1)S(1)}, bf16[8,2048,256]{2,1,0:T(8,128)(2,1)}, u32[]{:S(2)}) copy-start(bf16[8,2048,256]{2,1,0:T(8,128)(2,1)} %get-tuple-element.15.refs_10_) | copy-start | bytes 25165828
  49.3 0.6 copy-start.1
  49.9 4.4 %collective-permute-start.8 = (f32[136,128]{1,0:T(8,128)S(1)}, f32[136,128]{1,0:T(8,128)S(1)}, u32[]{:S(2)}, u32[]{:S(2)}) collective-permute-start(f32[136,128]{1,0:T(8,128)S(1)} %get-tuple-element.18), channel_id=1, source_target_pairs={{0,1},{1,0},{2,3},{3,2},{4,5},{5,4},{6,7},{7,6},{8,9},{9,8},{10,11... | collective-permute-start | bytes 208904 | tf_op jit(solution)/shard_map/ppermute | solution.py:390
  50.6 7.3 %collective-permute-start.10 = (f32[136,128]{1,0:T(8,128)S(1)}, f32[136,128]{1,0:T(8,128)S(1)}, u32[]{:S(2)}, u32[]{:S(2)}) collective-permute-start(f32[136,128]{1,0:T(8,128)S(1)} %get-tuple-element.20), channel_id=1, source_target_pairs={{0,1},{1,0},{2,3},{3,2},{4,5},{5,4},{6,7},{7,6},{8,9},{9,8},{10,11... | collective-permute-start | bytes 208904 | tf_op jit(solution)/shard_map/ppermute | solution.py:390
  52.0 6.1 %collective-permute-start.12 = (f32[136,128]{1,0:T(8,128)S(1)}, f32[136,128]{1,0:T(8,128)S(1)}, u32[]{:S(2)}, u32[]{:S(2)}) collective-permute-start(f32[136,128]{1,0:T(8,128)S(1)} %get-tuple-element.22), channel_id=1, source_target_pairs={{0,1},{1,0},{2,3},{3,2},{4,5},{5,4},{6,7},{7,6},{8,9},{9,8},{10,11... | collective-permute-start | bytes 208904 | tf_op jit(solution)/shard_map/ppermute | solution.py:390
  52.7 6.7 %collective-permute-start.14 = (f32[136,128]{1,0:T(8,128)S(1)}, f32[136,128]{1,0:T(8,128)S(1)}, u32[]{:S(2)}, u32[]{:S(2)}) collective-permute-start(f32[136,128]{1,0:T(8,128)S(1)} %get-tuple-element.23), channel_id=1, source_target_pairs={{0,1},{1,0},{2,3},{3,2},{4,5},{5,4},{6,7},{7,6},{8,9},{9,8},{10,11... | collective-permute-start | bytes 208904 | tf_op jit(solution)/shard_map/ppermute | solution.py:390
  54.3 6.2 %collective-permute-start.9 = (f32[136,128]{1,0:T(8,128)S(1)}, f32[136,128]{1,0:T(8,128)S(1)}, u32[]{:S(2)}, u32[]{:S(2)}) collective-permute-start(f32[136,128]{1,0:T(8,128)S(1)} %add.39), channel_id=1, source_target_pairs={{0,6},{1,7},{2,4},{3,5},{4,2},{5,3},{6,0},{7,1},{8,14},{9,15},{10,... | collective-permute-start | bytes 208904 | tf_op jit(solution)/shard_map/ppermute | solution.py:390
  58.0 5.3 %collective-permute-start.11 = (f32[136,128]{1,0:T(8,128)S(1)}, f32[136,128]{1,0:T(8,128)S(1)}, u32[]{:S(2)}, u32[]{:S(2)}) collective-permute-start(f32[136,128]{1,0:T(8,128)S(1)} %add.40), channel_id=1, source_target_pairs={{0,4},{1,5},{2,6},{3,7},{4,0},{5,1},{6,2},{7,3},{8,12},{9,13},{10,... | collective-permute-start | bytes 208904 | tf_op jit(solution)/shard_map/ppermute | solution.py:390
  58.1 5.2 %collective-permute-start.13 = (f32[136,128]{1,0:T(8,128)S(1)}, f32[136,128]{1,0:T(8,128)S(1)}, u32[]{:S(2)}, u32[]{:S(2)}) collective-permute-start(f32[136,128]{1,0:T(8,128)S(1)} %add.41), channel_id=1, source_target_pairs={{0,2},{1,3},{2,0},{3,1},{4,6},{5,7},{6,4},{7,5},{8,10},{9,11},{10,... | collective-permute-start | bytes 208904 | tf_op jit(solution)/shard_map/ppermute | solution.py:390
  59.3 3.9 %copy-start.12 = (f32[136,128]{1,0:T(8,128)}, f32[136,128]{1,0:T(8,128)S(1)}, u32[]{:S(2)}) copy-start(f32[136,128]{1,0:T(8,128)S(1)} %collective-permute-done.14.refs_4_) | copy-start | bytes 208900
  60.5 2.8 %copy-start.13 = (f32[136,128]{1,0:T(8,128)}, f32[136,128]{1,0:T(8,128)S(1)}, u32[]{:S(2)}) copy-start(f32[136,128]{1,0:T(8,128)S(1)} %collective-permute-done.9.refs_1_) | copy-start | bytes 208900
  63.2 0.6 copy-start.14
  63.2 0.7 copy-start.15

commit v2 on v1

--- a/solution.py
+++ b/solution.py
@@ -13,6 +13,7 @@
 VMEM = pl.BlockSpec(memory_space=pltpu.VMEM)
 SMEM = pl.BlockSpec(memory_space=pltpu.SMEM)
 ANY = pl.BlockSpec(memory_space=pl.ANY)
+HBM = pl.BlockSpec(memory_space=pltpu.HBM)
 
 
 def passed_along(value, axis, steps):
@@ -151,23 +152,187 @@
     return head, (value - head.astype(F32)).astype(BF16)
 
 
-def add_entries(total, entries, dst, src, coef, blocks):
-    blocks[...] = jnp.zeros_like(blocks)
-
-    def step(e, unused):
-        target = dst[e]
-        blocks[target] += coef[e] * entries[src[e]]
+def side_by_side(value):
+    return jnp.concatenate(heads_tails(value), axis=1)
+
+
+def product(left, right):
+    return jnp.dot(left, right, preferred_element_type=F32)
+
+
+def channel_row(counts, live, channels):
+    at = lax.broadcasted_iota(jnp.int32, (1, live), 1)
+    found = jnp.zeros((1, live), jnp.int32)
+    end = 0
+    for c in range(channels):
+        end = end + counts[0, 0, c]
+        found += (at >= end).astype(jnp.int32)
+    return found
+
+
+def thirds(value):
+    first = value.astype(BF16)
+    value = value - first.astype(F32)
+    second = value.astype(BF16)
+    return [first.astype(F32), second.astype(F32), value - second.astype(F32)]
+
+
+def over_entries(rows, chosen):
+    return lax.dot_general(
+        rows.astype(BF16), chosen, (((1,), (1,)), ((), ())), preferred_element_type=F32
+    )
+
+
+def plan_terms(group, source, coef, ints, floats):
+    w, live = 128, group.shape[1]
+    groups = lax.broadcasted_iota(jnp.int32, (w, live), 0)
+    member = group == groups
+    ones = jnp.where(member, 1.0, 0.0)
+    earlier = lax.broadcasted_iota(jnp.int32, (live, live), 0) < lax.broadcasted_iota(
+        jnp.int32, (live, live), 1
+    )
+    earlier = jnp.where(earlier, 1.0, 0.0).astype(BF16)
+    before = product(ones.astype(BF16), earlier)
+    size = jnp.sum(ones, axis=1, keepdims=True)
+    rank = jnp.sum(ones * before, axis=0, keepdims=True)
+    size_here = jnp.sum(ones * size, axis=0, keepdims=True)
+    spilled = jnp.where(size_here > 2.0, jnp.where(rank > 0.0, 1.0, 0.0), 0.0)
+    parts = thirds(coef)
+    sources = source.astype(F32)
+    zero = jnp.zeros_like(coef)
+    rows = jnp.concatenate([sources, *parts, ones[0:1] * 0.0 + 1.0, zero, zero, zero], axis=0)
+    first = over_entries(rows, jnp.where(before == 0.0, ones, 0.0).astype(BF16))
+    second = over_entries(rows, jnp.where(before == 1.0, ones, 0.0).astype(BF16))
+    large = over_entries(rows, ones.astype(BF16))[4:5] > 2.0
+    at = lax.broadcasted_iota(jnp.int32, (1, w), 1)
+    ints[0:1, 0:w] = first[0:1].astype(jnp.int32)
+    ints[1:2, 0:w] = jnp.where(large, w + at, second[0:1].astype(jnp.int32))
+    floats[0:1, 0:w] = first[1:2] + first[2:3] + first[3:4]
+    floats[1:2, 0:w] = jnp.where(large, 1.0, second[1:2] + second[2:3] + second[3:4])
+
+    place = product(jnp.concatenate([spilled] * 8, axis=0).astype(BF16), earlier)[0:1]
+    place = jnp.where(spilled > 0.0, place, -1.0)
+    column = lax.broadcasted_iota(jnp.int32, (live, live), 0).astype(F32)
+    chosen = jnp.where(place == column, 1.0, 0.0).astype(BF16)
+    again = jnp.where(rank > 1.0, 1.0, 0.0)
+    rows = jnp.concatenate(
+        [sources, *parts, (group + w).astype(F32), again, zero, zero], axis=0
+    )
+    listed = over_entries(rows, chosen)
+    ints[2:3] = listed[0:1].astype(jnp.int32)
+    ints[3:4] = listed[4:5].astype(jnp.int32)
+    ints[4:5] = jnp.full((1, live), jnp.sum(spilled)).astype(jnp.int32)
+    floats[2:3] = listed[1:2] + listed[2:3] + listed[3:4]
+    floats[3:4] = listed[5:6]
+
+
+def spill(ints, floats, blocks):
+    def add(q, unused):
+        to = ints[3, q]
+        held = jnp.where(floats[3, q] > 0.0, blocks[to], 0.0)
+        blocks[to] = held + floats[2, q] * blocks[ints[2, q]]
         return unused
 
-    lax.fori_loop(0, total, step, 0, unroll=4)
-
-
-def renew_kernel(*refs):
-    n = len(refs) - 9
-    dst, src, coef = refs[:3]
-    tiles = refs[3 : 3 + n]
-    env, out, bottoms, tops, entries, blocks = refs[3 + n : 9 + n]
-    channels, w = env.shape[0], env.shape[1]
+    lax.fori_loop(0, ints[4, 0], add, 0)
+
+
+def two_terms(ints, floats, blocks, g):
+    return floats[0, g] * blocks[ints[0, g]] + floats[1, g] * blocks[ints[1, g]]
+
+
+def prepare_kernel(n, *refs):
+    psi, given, refs = refs[0], refs[1:12], refs[12:]
+    lefts, rights, up_ints, up_floats, mv_ints, mv_floats, own = refs[:7]
+    held = refs[7:18]
+    arrived, own_arrived = refs[18:]
+    own_copy = pltpu.make_async_copy(psi.at[0, 0], own, own_arrived)
+    own_copy.start()
+    copies = [
+        pltpu.make_async_copy(source, target, arrived.at[index])
+        for index, (source, target) in enumerate(zip(given, held))
+    ]
+    for copy in copies:
+        copy.start()
+    up_counts, up_block, up_top, up_bot, up_coef, mv_counts, mv_src, mv_dst, mv_coef = held[:9]
+    left, right = held[9:]
+    channels, w = left.shape[1], left.shape[2]
+    live = up_block.shape[2]
+    me = lax.axis_index("tile")
+    for copy in copies[:9]:
+        copy.wait()
+    channel = channel_row(up_counts, live, channels)
+    plan_terms(
+        channel * n + (up_top[0] ^ me), up_block[0] * n + (up_bot[0] ^ me), up_coef[0], up_ints, up_floats
+    )
+    channel = channel_row(mv_counts, live, channels)
+    plan_terms(
+        channel * n + (mv_dst[0] ^ me), channel * n + (mv_src[0] ^ me), mv_coef[0], mv_ints, mv_floats
+    )
+    copies[9].wait()
+
+    def halve_left(c, unused):
+        lefts[pl.ds(pl.multiple_of(c * w, w), w)] = side_by_side(left[0, c])
+        return unused
+
+    lax.fori_loop(0, channels, halve_left, 0, unroll=2)
+    copies[10].wait()
+
+    def halve_right(c, unused):
+        head, tail = heads_tails(right[0, c])
+        rights[c, 0:w] = head
+        rights[c, w : 2 * w] = tail
+        return unused
+
+    lax.fori_loop(0, channels, halve_right, 0, unroll=2)
+    own_copy.wait()
+
+
+def prepare_call(n, psi, given):
+    channels, w = given[-1].shape[1], given[-1].shape[2]
+    live = given[1].shape[2]
+    table = (8, live)
+    return pl.pallas_call(
+        functools.partial(prepare_kernel, n),
+        out_shape=(
+            jax.ShapeDtypeStruct((channels * w, 2 * w), BF16),
+            jax.ShapeDtypeStruct((channels, 2 * w, w), BF16),
+            jax.ShapeDtypeStruct(table, jnp.int32),
+            jax.ShapeDtypeStruct(table, F32),
+            jax.ShapeDtypeStruct(table, jnp.int32),
+            jax.ShapeDtypeStruct(table, F32),
+            jax.ShapeDtypeStruct((w, w), F32),
+        ),
+        in_specs=[HBM] * (len(given) + 1),
+        out_specs=(VMEM,) * 7,
+        scratch_shapes=[
+            *(
+                pltpu.SMEM(x.shape, x.dtype) if x.shape[-1] == channels else pltpu.VMEM(x.shape, x.dtype)
+                for x in given
+            ),
+            pltpu.SemaphoreType.DMA((len(given),)),
+            pltpu.SemaphoreType.DMA,
+        ],
+        compiler_params=pltpu.CompilerParams(vmem_limit_bytes=12 << 20),
+        cost_estimate=pl.CostEstimate(flops=10**9, bytes_accessed=6 << 20, transcendentals=0),
+        name="prepare",
+    )(*(pltpu.with_memory_space_constraint(x, pltpu.HBM) for x in (psi, *given)))
+
+
+def fetch_tables(sources, targets, arrived):
+    copies = [
+        pltpu.make_async_copy(source, target, arrived.at[index])
+        for index, (source, target) in enumerate(zip(sources, targets))
+    ]
+    for copy in copies:
+        copy.start()
+    return copies
+
+
+def renew_kernel(n, *refs):
+    tiles = refs[:n]
+    lefts, int_table, float_table, out, bottoms, tops, entries, renewed, ints, floats, arrived, left = refs[n:]
+    channels, w = out.shape[0], out.shape[1]
+    copies = fetch_tables((int_table, float_table), (ints, floats), arrived)
     for k in range(n):
         at = slice(k * w, (k + 1) * w)
         value = tiles[k][...]
@@ -181,51 +346,61 @@
         tops[w : 2 * w, at] = tail
     group = channels // 2
 
-    def products(g, unused):
-        head, tail = heads_tails(env[pl.ds(g * group, group)].reshape(group * w, w))
-        both = jnp.concatenate([head, tail, head, tail], axis=1)
-        found = jnp.dot(both, bottoms[...], preferred_element_type=F32)
+    def multiply(g, unused):
+        own = lefts[pl.ds(pl.multiple_of(g * (group * w), group * w), group * w)]
+        found = product(jnp.concatenate([own, own], axis=1), bottoms[...])
         for h in range(group):
             for k in range(n):
                 entries[(g * group + h) * n + k] = found[h * w : (h + 1) * w, k * w : (k + 1) * w]
         return unused
 
-    lax.fori_loop(0, 2, products, 0)
-    add_entries(dst.shape[0], entries, dst, src, coef, blocks)
+    lax.fori_loop(0, 2, multiply, 0)
+    for copy in copies:
+        copy.wait()
+    spill(ints, floats, entries)
 
     def finish(b, unused):
-        head, tail = heads_tails(blocks[pl.ds(b * n, n)].reshape(n * w, w))
-        both = jnp.concatenate([head, tail], axis=1)
-        found = jnp.dot(tops[...], both, preferred_element_type=F32)
-        out[b] = (found[:w, :w] + found[w:, w:]) + (found[:w, w:] + found[w:, :w])
+        pairs = [heads_tails(two_terms(ints, floats, entries, b * n + k)) for k in range(n)]
+        stack = [jnp.concatenate([pair[i] for pair in pairs], axis=0) for i in range(2)]
+        found = product(tops[...], jnp.concatenate(stack, axis=1))
+        renewed[b] = (found[:w, :w] + found[w:, w:]) + (found[:w, w:] + found[w:, :w])
+        pltpu.make_async_copy(renewed.at[b], out.at[b], left.at[b]).start()
         return unused
 
-    lax.fori_loop(0, channels, finish, 0, unroll=4)
-
-
-def renew_call(dst, src, coef, tiles, env):
-    n, w, channels = len(tiles), env.shape[1], env.shape[0]
+    lax.fori_loop(0, channels, finish, 0, unroll=8)
+    for b in range(channels):
+        pltpu.make_async_copy(renewed.at[b], out.at[b], left.at[b]).wait()
+
+
+def renew_call(tiles, lefts, int_table, float_table, channels):
+    n, w = len(tiles), tiles[0].shape[0]
     return pl.pallas_call(
-        renew_kernel,
-        out_shape=jax.ShapeDtypeStruct(env.shape, F32),
-        in_specs=[SMEM] * 3 + [VMEM] * (n + 1),
-        out_specs=VMEM,
+        functools.partial(renew_kernel, n),
+        out_shape=jax.ShapeDtypeStruct((channels, w, w), F32),
+        in_specs=[VMEM] * (n + 1) + [ANY] * 2,
+        out_specs=HBM,
         scratch_shapes=[
             pltpu.VMEM((4 * w, n * w), BF16),
             pltpu.VMEM((2 * w, n * w), BF16),
-            pltpu.VMEM((channels * n, w, w), F32),
-            pltpu.VMEM((channels * n, w, w), F32),
+            pltpu.VMEM((2 * w, w, w), F32),
+            pltpu.VMEM((channels, w, w), F32),
+            pltpu.SMEM(int_table.shape, jnp.int32),
+            pltpu.SMEM(float_table.shape, F32),
+            pltpu.SemaphoreType.DMA((2,)),
+            pltpu.SemaphoreType.DMA((channels,)),
         ],
-        compiler_params=pltpu.CompilerParams(vmem_limit_bytes=40 << 20),
+        compiler_params=pltpu.CompilerParams(vmem_limit_bytes=28 << 20),
         cost_estimate=pl.CostEstimate(flops=10**10, bytes_accessed=3 << 20, transcendentals=0),
         name="renew",
-    )(dst, src, coef, *tiles, env)
-
-
-def source_kernel(n, dst, src, coef, energies, *refs):
+    )(*tiles, lefts, int_table, float_table)
+
+
+def source_kernel(n, energies, *refs):
     tiles = refs[:n]
-    right, out, stats, sources, entries, blocks = refs[n:]
-    channels, w = right.shape[0], right.shape[1]
+    rights, int_table, float_table, out, stats, sources, entries, ints, floats, arrived = refs[n:]
+    channels, w = rights.shape[0], rights.shape[2]
+    copies = fetch_tables((int_table, float_table), (ints, floats), arrived)
+    me = lax.axis_index("tile")
     weight = jnp.zeros((8, w), F32)
     energy = jnp.zeros((8, w), F32)
     for k in range(n):
@@ -238,54 +413,58 @@
         sources[at, 3 * w : 4 * w] = tail
         squares = jnp.sum((value * value).reshape(w // 8, 8, w), axis=0)
         weight += squares
-        energy += energies[k] * squares
+        energy += energies[0, k ^ me] * squares
     stats[0:8] = weight
     stats[8:16] = energy
-
-    def products(g, unused):
+    stats[16:24] = jnp.full((8, w), energies[0, me], F32)
+    group = channels // 2
+
+    def multiply(g, unused):
         columns = []
-        for h in range(2):
-            head, tail = heads_tails(right[2 * g + h])
-            columns.append(jnp.concatenate([head, head, tail, tail], axis=0))
-        found = jnp.dot(sources[...], jnp.concatenate(columns, axis=1), preferred_element_type=F32)
-        for h in range(2):
+        for h in range(group):
+            value = rights[g * group + h]
+            columns.append(jnp.concatenate([value[:w], value[:w], value[w:], value[w:]], axis=0))
+        found = product(sources[...], jnp.concatenate(columns, axis=1))
+        for h in range(group):
             for k in range(n):
-                entries[(2 * g + h) * n + k] = found[k * w : (k + 1) * w, h * w : (h + 1) * w]
+                entries[(g * group + h) * n + k] = found[k * w : (k + 1) * w, h * w : (h + 1) * w]
         return unused
 
-    lax.fori_loop(0, channels // 2, products, 0, unroll=2)
-    add_entries(dst.shape[0], entries, dst, src, coef, blocks)
+    lax.fori_loop(0, 2, multiply, 0)
+    for copy in copies:
+        copy.wait()
+    spill(ints, floats, entries)
 
     def finish(c, unused):
+        rows = pl.ds(pl.multiple_of(c * w, w), w)
         for k in range(n):
-            head, tail = heads_tails(blocks[c * n + k])
-            rows = pl.ds(pl.multiple_of(c * w, w), w)
-            out[k, rows, 0:w] = head
-            out[k, rows, w : 2 * w] = tail
+            out[k, rows] = side_by_side(two_terms(ints, floats, entries, c * n + k))
         return unused
 
-    lax.fori_loop(0, channels, finish, 0)
-
-
-def source_call(dst, src, coef, energies, tiles, right):
-    n, w, channels = len(tiles), right.shape[1], right.shape[0]
+    lax.fori_loop(0, channels, finish, 0, unroll=2)
+
+
+def source_call(energies, tiles, rights, int_table, float_table):
+    n, w, channels = len(tiles), rights.shape[2], rights.shape[0]
     return pl.pallas_call(
         functools.partial(source_kernel, n),
         out_shape=(
             jax.ShapeDtypeStruct((n, channels * w, 2 * w), BF16),
-            jax.ShapeDtypeStruct((16, w), F32),
+            jax.ShapeDtypeStruct((24, w), F32),
         ),
-        in_specs=[SMEM] * 4 + [VMEM] * (n + 1),
+        in_specs=[SMEM] + [VMEM] * (n + 1) + [ANY] * 2,
         out_specs=(VMEM, VMEM),
         scratch_shapes=[
             pltpu.VMEM((n * w, 4 * w), BF16),
-            pltpu.VMEM((channels * n, w, w), F32),
-            pltpu.VMEM((channels * n, w, w), F32),
+            pltpu.VMEM((2 * w, w, w), F32),
+            pltpu.SMEM(int_table.shape, jnp.int32),
+            pltpu.SMEM(float_table.shape, F32),
+            pltpu.SemaphoreType.DMA((2,)),
         ],
-        compiler_params=pltpu.CompilerParams(vmem_limit_bytes=48 << 20),
+        compiler_params=pltpu.CompilerParams(vmem_limit_bytes=28 << 20),
         cost_estimate=pl.CostEstimate(flops=10**10, bytes_accessed=10 << 20, transcendentals=0),
         name="sources",
-    )(dst, src, coef, energies, *tiles, right)
+    )(energies, *tiles, rights, int_table, float_table)
 
 
 def apply_kernel(n, *refs):
@@ -331,13 +510,13 @@
             pltpu.VMEM((2 * w, own.shape[0] * w), BF16),
             pltpu.SemaphoreType.DMA,
         ],
-        compiler_params=pltpu.CompilerParams(vmem_limit_bytes=32 << 20),
+        compiler_params=pltpu.CompilerParams(vmem_limit_bytes=8 << 20),
         cost_estimate=pl.CostEstimate(flops=5 * 10**9, bytes_accessed=10 << 20, transcendentals=0),
         name="applied",
     )(*tiles, own, received, blocks)
 
 
-def finish_kernel(energy, *refs):
+def finish_kernel(*refs):
     parts = refs[:-4]
     own, stats, residual, quotient = refs[-4:]
     w = own.shape[0]
@@ -347,24 +526,20 @@
     value = own[...]
     numerator = jnp.sum(total[w : w + 8]) + jnp.sum(stats[8:16])
     ratio = jnp.full((1, 128), numerator, F32) / jnp.full((1, 128), jnp.sum(stats[0:8]), F32)
-    residual[...] = total[:w] + (energy[0] - ratio) * value
+    residual[...] = total[:w] + (stats[16:17] - ratio) * value
     quotient[...] = ratio
 
 
-def finish_call(energy, parts, own, stats):
+def finish_call(parts, own, stats):
     w = own.shape[0]
     return pl.pallas_call(
         finish_kernel,
         out_shape=(jax.ShapeDtypeStruct((w, w), F32), jax.ShapeDtypeStruct((1, 128), F32)),
-        in_specs=[SMEM] + [VMEM] * (len(parts) + 2),
+        in_specs=[VMEM] * (len(parts) + 2),
         out_specs=(VMEM, VMEM),
+        compiler_params=pltpu.CompilerParams(vmem_limit_bytes=2 << 20),
         name="finish",
-    )(energy, *parts, own, stats)
-
-
-def channel_of(counts, live):
-    ends = jnp.cumsum(counts)
-    return jnp.sum((jnp.arange(live)[:, None] >= ends[None, :]).astype(jnp.int32), axis=1)
+    )(*parts, own, stats)
 
 
 def shards(
@@ -383,9 +558,6 @@
     up_coef,
 ):
     n = lax.axis_size("tile")
-    me = lax.axis_index("tile")
-    live = mv_src.shape[2]
-
     def across(value, k):
         return lax.ppermute(value, "tile", [(i, i ^ k) for i in range(n)])
 
@@ -397,24 +569,21 @@
         tiles[k + 1] = across(tiles[k], 1)
     tiles = [tiles[k] for k in range(n)]
 
-    up_channel = channel_of(up_counts[0, 0], live)
-    up_dst = up_channel * n + (up_top[0, 0] ^ me)
-    up_from = up_block[0, 0] * n + (up_bot[0, 0] ^ me)
-    mv_channel = channel_of(mv_counts[0, 0], live)
-    mv_to = mv_channel * n + (mv_dst[0, 0] ^ me)
-    mv_from = mv_channel * n + (mv_src[0, 0] ^ me)
-    energies = site_energy[0][jnp.arange(n) ^ me]
-
-    renewal = renew_call(up_dst, up_from, up_coef[0, 0], tiles, left_env[0])
+    given = [up_counts, up_block, up_top, up_bot, up_coef, mv_counts, mv_src, mv_dst, mv_coef]
+    lefts, rights, up_ints, up_floats, mv_ints, mv_floats, own = prepare_call(
+        n, psi, [*given, left_env, right_env]
+    )
+    tiles[0] = own
+    renewal = renew_call(tiles, lefts, up_ints, up_floats, left_env.shape[1])
     received = passed_along(renewal, "seg", 1)
-    blocks, stats = source_call(mv_to, mv_from, mv_coef[0, 0], energies, tiles, right_env[0])
+    blocks, stats = source_call(site_energy, tiles, rights, mv_ints, mv_floats)
     partials = apply_call(tiles, left_env[0], received, blocks)
 
     parts = [partials[0]]
     for k in range(n - 2, 0, -2):
         parts.append(across(partials[k] + across(partials[k + 1], 1), k))
     parts.append(across(partials[1], 1))
-    residual, quotient = finish_call(energies, parts, own, stats)
+    residual, quotient = finish_call(parts, own, stats)
     return (residual[None, None], renewal[None], quotient[0, :1])
 
 

time: 66.1 us -> 51.1 us (0.77)
  local copies, waits for them, and re-layouts: 9.54 us -> 0.01 us
  Pallas kernels: 24.4 us -> 20 us
  other arithmetic: 2.62 us -> 0.03 us
  waiting for transfers between devices: 8.08 us -> 9.45 us
    unnamed x32 -> x4, local copies, waits for them, and re-layouts: 7.44 us -> 0.01 us
    pallas_call x1, Pallas kernels: 10.5 us -> 7.1 us  [source_call(): pl.pallas_call(functools.partial(source_kernel, n), out_shape=(jax.ShapeD...]
    another operation x2 -> x0, local copies, waits for them, and re-layouts: 1.46 us -> none
    xor x2 -> x0, other arithmetic: 1.38 us -> none  [the longest x1 0.7 us: shards(): mv_from = mv_channel * n + (mv_src[0, 0] ^ me)]
    ppermute x14, waiting for transfers between devices: 8.07 us -> 9.45 us  [across(): return lax.ppermute(value, 'tile', [(i, i ^ k) for i in range(n)])]
    pallas_call x1, Pallas kernels: 1.83 us -> 0.77 us  [finish_call(): pl.pallas_call(finish_kernel, out_shape=(jax.ShapeDtypeStruct((w, w), F32...]
    add x3 -> x0, other arithmetic: 0.71 us -> none  [the longest x1 0.7 us: shards(): up_from = up_block[0, 0] * n + (up_bot[0, 0] ^ me)]
    pallas_call x1 -> x2, Pallas kernels: 9.52 us -> 9.53 us  [the longest x1 7.58 us: renew_call(): pl.pallas_call(functools.partial(renew_kernel, n), out_shape=jax.ShapeDty...]
  transfers between devices with their start and end apart: 15 -> 15, of which waited for: 6 -> 6; matrix products, arithmetic and copies ran while one was open for 7% -> 0% of each run, Pallas kernels for 16% -> 18%
where the time goes in v2:
time: 51.1 us; the launch traced here: 50.9 us
  starting transfers between devices  20.7 us (41%)
  Pallas kernels  20 us (39%)
  waiting for transfers between devices  9.45 us (18%)
  between operations  0.75 us (1%)
    ppermute x14, starting transfers between devices, across(): return lax.ppermute(value, 'tile', [(i, i ^ k) for i in range(n)])  19.3 us
    ppermute x14, waiting for transfers between devices, across(): return lax.ppermute(value, 'tile', [(i, i ^ k) for i in range(n)])  9.45 us
    pallas_call x1, Pallas kernels, renew_call(): pl.pallas_call(functools.partial(renew_kernel, n), out_shape=jax.ShapeDty...  7.58 us
    pallas_call x1, Pallas kernels, source_call(): pl.pallas_call(functools.partial(source_kernel, n), out_shape=(jax.ShapeD...  7.1 us
    pallas_call x1, Pallas kernels, apply_call(): pl.pallas_call(functools.partial(apply_kernel, n), out_shape=tuple((jax.S...  2.59 us
    pallas_call x1, Pallas kernels, prepare_call(): pl.pallas_call(functools.partial(prepare_kernel, n), out_shape=(jax.Shape...  1.95 us
    ppermute x1, starting transfers between devices, passed_along(): lax.ppermute(value, axis, [(source, source + steps) for source in range(f...  1.36 us
  transfers between devices with their start and end apart: 15, of which 6 were waited for; matrix products, arithmetic and copies ran while one was open for 0% of the time, Pallas kernels for 18%

profile of v2, /device:TPU:0, one launch (start us, length us, event | category | flops | bytes accessed | tf_op | source)
XLA Modules:
  0.0 50.9 jit_solution(7036585398549462273)
XLA Ops:
  0.6 3.1 %collective-permute-start.1 = (f32[128,128]{1,0:T(8,128)}, f32[128,128]{1,0:T(8,128)S(1)}, u32[]{:S(2)}, u32[]{:S(2)}) collective-permute-start(f32[128,128]{1,0:T(8,128)} %bitcast.8), channel_id=1, source_target_pairs={{0,2},{1,3},{2,0},{3,1},{4,6},{5,7},{6,4},{7,5},{8,10},{9,11},{10,... | collective-permute-start | bytes 196616 | tf_op jit(solution)/shard_map/ppermute | solution.py:562
  3.7 2.6 %collective-permute-start.3 = (f32[128,128]{1,0:T(8,128)}, f32[128,128]{1,0:T(8,128)S(1)}, u32[]{:S(2)}, u32[]{:S(2)}) collective-permute-start(f32[128,128]{1,0:T(8,128)} %bitcast.9), channel_id=1, source_target_pairs={{0,4},{1,5},{2,6},{3,7},{4,0},{5,1},{6,2},{7,3},{8,12},{9,13},{10,... | collective-permute-start | bytes 196616 | tf_op jit(solution)/shard_map/ppermute | solution.py:562
  6.3 0.0 collective-permute-start.5
  6.3 1.7 %collective-permute-start = (f32[128,128]{1,0:T(8,128)}, f32[128,128]{1,0:T(8,128)S(1)}, u32[]{:S(2)}, u32[]{:S(2)}) collective-permute-start(f32[128,128]{1,0:T(8,128)} %bitcast.11), channel_id=1, source_target_pairs={{0,1},{1,0},{2,3},{3,2},{4,5},{5,4},{6,7},{7,6},{8,9},{9,8},{10,11... | collective-permute-start | bytes 196616 | tf_op jit(solution)/shard_map/ppermute | solution.py:562
  8.1 0.0 collective-permute-done.1.refs_2_
  8.1 0.3 collective-permute-start.2
  8.3 2.9 %collective-permute-done.3.refs_4_ = f32[128,128]{1,0:T(8,128)S(1)} collective-permute-done((f32[128,128]{1,0:T(8,128)}, f32[128,128]{1,0:T(8,128)S(1)}, u32[]{:S(2)}, u32[]{:S(2)}) %collective-permute-start.3) | collective-permute-done | bytes 65568 | tf_op jit(solution)/shard_map/ppermute | solution.py:562
  11.2 1.5 %collective-permute-start.4 = (f32[128,128]{1,0:T(8,128)S(1)}, f32[128,128]{1,0:T(8,128)S(1)}, u32[]{:S(2)}, u32[]{:S(2)}) collective-permute-start(f32[128,128]{1,0:T(8,128)S(1)} %collective-permute-done.3.refs_4_), channel_id=1, source_target_pairs={{0,1},{1,0},{2,3},{3,2},{4,5},{5,4},{6,7},{7,6},{8,9},{9,8},{10,11... | collective-permute-start | bytes 196616 | tf_op jit(solution)/shard_map/ppermute | solution.py:562
  12.7 0.0 collective-permute-done.5.refs_6_
  12.7 1.4 %collective-permute-start.6 = (f32[128,128]{1,0:T(8,128)S(1)}, f32[128,128]{1,0:T(8,128)S(1)}, u32[]{:S(2)}, u32[]{:S(2)}) collective-permute-start(f32[128,128]{1,0:T(8,128)S(1)} %collective-permute-done.5.refs_6_), channel_id=1, source_target_pairs={{0,1},{1,0},{2,3},{3,2},{4,5},{5,4},{6,7},{7,6},{8,9},{9,8},{10,11... | collective-permute-start | bytes 196616 | tf_op jit(solution)/shard_map/ppermute | solution.py:562
  14.1 2.0 %prepare.1 = (bf16[2048,256]{1,0:T(8,128)(2,1)S(1)}, bf16[16,256,128]{2,1,0:T(8,128)(2,1)S(1)}, s32[8,192]{1,0:T(8,128)S(1)}, f32[8,192]{1,0:T(8,128)S(1)}, s32[...) custom-call(f32[1,1,128,128]{3,2,1,0:T(8,128)} %refs_0_.1, s32[1,1,16]{2,1,0:T(1,128)} %refs_1_.1, ...), custom_call_target="tpu_custom_call" | custom-call | flops 1000000000 | bytes 6291456 | tf_op jit(solution)/shard_map/prepare/pallas_call | solution.py:294
  16.1 0.0 collective-permute-done.refs_1_
  16.1 0.0 collective-permute-done.2.refs_3_
  16.1 0.0 collective-permute-done.4.refs_5_
  16.1 0.9 %collective-permute-done.6.refs_7_ = f32[128,128]{1,0:T(8,128)S(1)} collective-permute-done((f32[128,128]{1,0:T(8,128)S(1)}, f32[128,128]{1,0:T(8,128)S(1)}, u32[]{:S(2)}, u32[]{:S(2)}) %collective-permute-start.6) | collective-permute-done | bytes 65568 | tf_op jit(solution)/shard_map/ppermute | solution.py:562
  17.0 0.0 copy-start.1
  17.0 7.6 %renew.1 = f32[16,128,128]{2,1,0:T(8,128)} custom-call(f32[128,128]{1,0:T(8,128)S(1)} %get-tuple-element.22.refs_0_.refs_5_, f32[128,128]{1,0:T(8,128)S(1)} %collective-permute-done.refs_1_, f32[128,128]{1,0:T(8,128)S(1)} %collective-permute-done.1.refs_2_, f32[128,128]{1,0:T(8,128)S(1)} %collective-permute-done.2.refs_3_, ...), custom_call_target="tpu_custom_call" | custom-call | flops 10000000000 | bytes 3145728 | tf_op jit(solution)/shard_map/renew/pallas_call | solution.py:377
  24.6 1.4 %collective-permute-start.7 = (f32[16,128,128]{2,1,0:T(8,128)}, f32[16,128,128]{2,1,0:T(8,128)S(1)}, u32[]{:S(2)}, u32[]{:S(2)}) collective-permute-start(f32[16,128,128]{2,1,0:T(8,128)} %renew.1), channel_id=1, source_target_pairs={{0,8},{1,9},{2,10},{3,11},{4,12},{5,13},{6,14},{7,15},{16,24},{17,... | collective-permute-start | bytes 3145736 | tf_op jit(solution)/shard_map/ppermute | solution.py:22
  26.0 0.0 copy-done.1
  26.0 0.0 copy-start
  26.0 7.1 %sources.1 = (bf16[8,2048,256]{2,1,0:T(8,128)(2,1)S(1)}, f32[24,128]{1,0:T(8,128)S(1)}) custom-call(f32[1,8]{1,0:T(1,128)S(1)} %copy-done.1, f32[128,128]{1,0:T(8,128)S(1)} %get-tuple-element.22.refs_0_.refs_5_, f32[128,128]{1,0:T(8,128)S(1)} %collective-permute-done.refs_1_, f32[128,128]{1,0:T(8,128)S(1)} %collective-permute-done.1.refs_2_, ...), custom_call_target="tpu_custom_call" | custom-call | flops 10000000000 | bytes 10485760 | tf_op jit(solution)/shard_map/sources/pallas_call | solution.py:449
  33.1 0.0 collective-permute-done.7.refs_9_
  33.1 0.0 copy-done
  33.1 2.6 %applied.1 = (f32[136,128]{1,0:T(8,128)S(1)}, f32[136,128]{1,0:T(8,128)S(1)}, f32[136,128]{1,0:T(8,128)S(1)}, f32[136,128]{1,0:T(8,128)S(1)}, f32[136,128]{1,0:T...) custom-call(f32[128,128]{1,0:T(8,128)S(1)} %get-tuple-element.22.refs_0_.refs_5_, ...), custom_call_target="tpu_custom_call" | custom-call | flops 5000000000 | bytes 10485760 | tf_op jit(solution)/shard_map/applied/pallas_call | solution.py:503
  35.7 1.4 %collective-permute-start.12 = (f32[136,128]{1,0:T(8,128)S(1)}, f32[136,128]{1,0:T(8,128)S(1)}, u32[]{:S(2)}, u32[]{:S(2)}) collective-permute-start(f32[136,128]{1,0:T(8,128)S(1)} %get-tuple-element.36), channel_id=1, source_target_pairs={{0,1},{1,0},{2,3},{3,2},{4,5},{5,4},{6,7},{7,6},{8,9},{9,8},{10,11... | collective-permute-start | bytes 208904 | tf_op jit(solution)/shard_map/ppermute | solution.py:562
  37.1 0.7 %collective-permute-start.10 = (f32[136,128]{1,0:T(8,128)S(1)}, f32[136,128]{1,0:T(8,128)S(1)}, u32[]{:S(2)}, u32[]{:S(2)}) collective-permute-start(f32[136,128]{1,0:T(8,128)S(1)} %get-tuple-element.34), channel_id=1, source_target_pairs={{0,1},{1,0},{2,3},{3,2},{4,5},{5,4},{6,7},{7,6},{8,9},{9,8},{10,11... | collective-permute-start | bytes 208904 | tf_op jit(solution)/shard_map/ppermute | solution.py:562
  37.8 1.3 %collective-permute-start.8 = (f32[136,128]{1,0:T(8,128)S(1)}, f32[136,128]{1,0:T(8,128)S(1)}, u32[]{:S(2)}, u32[]{:S(2)}) collective-permute-start(f32[136,128]{1,0:T(8,128)S(1)} %get-tuple-element.32), channel_id=1, source_target_pairs={{0,1},{1,0},{2,3},{3,2},{4,5},{5,4},{6,7},{7,6},{8,9},{9,8},{10,11... | collective-permute-start | bytes 208904 | tf_op jit(solution)/shard_map/ppermute | solution.py:562
  39.1 0.7 %collective-permute-start.14 = (f32[136,128]{1,0:T(8,128)S(1)}, f32[136,128]{1,0:T(8,128)S(1)}, u32[]{:S(2)}, u32[]{:S(2)}) collective-permute-start(f32[136,128]{1,0:T(8,128)S(1)} %get-tuple-element.37), channel_id=1, source_target_pairs={{0,1},{1,0},{2,3},{3,2},{4,5},{5,4},{6,7},{7,6},{8,9},{9,8},{10,11... | collective-permute-start | bytes 208904 | tf_op jit(solution)/shard_map/ppermute | solution.py:562
  39.8 0.3 collective-permute-done.12
  40.1 0.7 %collective-permute-start.13 = (f32[136,128]{1,0:T(8,128)S(1)}, f32[136,128]{1,0:T(8,128)S(1)}, u32[]{:S(2)}, u32[]{:S(2)}) collective-permute-start(f32[136,128]{1,0:T(8,128)S(1)} %add.11), channel_id=1, source_target_pairs={{0,2},{1,3},{2,0},{3,1},{4,6},{5,7},{6,4},{7,5},{8,10},{9,11},{10,... | collective-permute-start | bytes 208904 | tf_op jit(solution)/shard_map/ppermute | solution.py:562
  40.8 0.6 %collective-permute-done.10 = f32[136,128]{1,0:T(8,128)S(1)} collective-permute-done((f32[136,128]{1,0:T(8,128)S(1)}, f32[136,128]{1,0:T(8,128)S(1)}, u32[]{:S(2)}, u32[]{:S(2)}) %collective-permute-start.10) | collective-permute-done | bytes 69664 | tf_op jit(solution)/shard_map/ppermute | solution.py:562
  41.4 2.5 %collective-permute-start.11 = (f32[136,128]{1,0:T(8,128)S(1)}, f32[136,128]{1,0:T(8,128)S(1)}, u32[]{:S(2)}, u32[]{:S(2)}) collective-permute-start(f32[136,128]{1,0:T(8,128)S(1)} %add.10), channel_id=1, source_target_pairs={{0,4},{1,5},{2,6},{3,7},{4,0},{5,1},{6,2},{7,3},{8,12},{9,13},{10,... | collective-permute-start | bytes 208904 | tf_op jit(solution)/shard_map/ppermute | solution.py:562
  43.9 0.0 collective-permute-done.8
  43.9 1.4 %collective-permute-start.9 = (f32[136,128]{1,0:T(8,128)S(1)}, f32[136,128]{1,0:T(8,128)S(1)}, u32[]{:S(2)}, u32[]{:S(2)}) collective-permute-start(f32[136,128]{1,0:T(8,128)S(1)} %add.9), channel_id=1, source_target_pairs={{0,6},{1,7},{2,4},{3,5},{4,2},{5,3},{6,0},{7,1},{8,14},{9,15},{10,... | collective-permute-start | bytes 208904 | tf_op jit(solution)/shard_map/ppermute | solution.py:562
  45.3 0.0 collective-permute-done.14.refs_4_
  45.3 0.0 collective-permute-done.13.refs_3_
  45.3 2.1 %collective-permute-done.11.refs_2_ = f32[136,128]{1,0:T(8,128)S(1)} collective-permute-done((f32[136,128]{1,0:T(8,128)S(1)}, f32[136,128]{1,0:T(8,128)S(1)}, u32[]{:S(2)}, u32[]{:S(2)}) %collective-permute-start.11) | collective-permute-done | bytes 69664 | tf_op jit(solution)/shard_map/ppermute | solution.py:562
  47.5 2.7 %collective-permute-done.9.refs_1_ = f32[136,128]{1,0:T(8,128)S(1)} collective-permute-done((f32[136,128]{1,0:T(8,128)S(1)}, f32[136,128]{1,0:T(8,128)S(1)}, u32[]{:S(2)}, u32[]{:S(2)}) %collective-permute-start.9) | collective-permute-done | bytes 69664 | tf_op jit(solution)/shard_map/ppermute | solution.py:562
  50.1 0.8 %finish.1 = (f32[128,128]{1,0:T(8,128)}, f32[1,128]{1,0:T(1,128)}) custom-call(f32[136,128]{1,0:T(8,128)S(1)} %get-tuple-element.30.refs_0_, f32[136,128]{1,0:T(8,128)S(1)} %collective-permute-done.9.refs_1_, f32[136,128]{1,0:T(8,128)S(1)} %collective-permute-done.11.refs_2_, f32[136,128]{1,0:T(8,128)S(1)} %collective-permute-done.13.refs_3_, ...), custom_call_target="tpu_custom_call" | custom-call | tf_op jit(solution)/shard_map/finish/pallas_call | solution.py:535
  (3 shorter events, 0.0 us)
Async XLA Ops:
  0.6 7.4 %collective-permute-start.1 = (f32[128,128]{1,0:T(8,128)}, f32[128,128]{1,0:T(8,128)S(1)}, u32[]{:S(2)}, u32[]{:S(2)}) collective-permute-start(f32[128,128]{1,0:T(8,128)} %bitcast.8), channel_id=1, source_target_pairs={{0,2},{1,3},{2,0},{3,1},{4,6},{5,7},{6,4},{7,5},{8,10},{9,11},{10,... | collective-permute-start | bytes 196616 | tf_op jit(solution)/shard_map/ppermute | solution.py:562
  3.7 7.5 %collective-permute-start.3 = (f32[128,128]{1,0:T(8,128)}, f32[128,128]{1,0:T(8,128)S(1)}, u32[]{:S(2)}, u32[]{:S(2)}) collective-permute-start(f32[128,128]{1,0:T(8,128)} %bitcast.9), channel_id=1, source_target_pairs={{0,4},{1,5},{2,6},{3,7},{4,0},{5,1},{6,2},{7,3},{8,12},{9,13},{10,... | collective-permute-start | bytes 196616 | tf_op jit(solution)/shard_map/ppermute | solution.py:562
  6.3 6.4 %collective-permute-start.5 = (f32[128,128]{1,0:T(8,128)}, f32[128,128]{1,0:T(8,128)S(1)}, u32[]{:S(2)}, u32[]{:S(2)}) collective-permute-start(f32[128,128]{1,0:T(8,128)} %bitcast.10), channel_id=1, source_target_pairs={{0,6},{1,7},{2,4},{3,5},{4,2},{5,3},{6,0},{7,1},{8,14},{9,15},{10,... | collective-permute-start | bytes 196616 | tf_op jit(solution)/shard_map/ppermute | solution.py:562
  6.3 9.8 %collective-permute-start = (f32[128,128]{1,0:T(8,128)}, f32[128,128]{1,0:T(8,128)S(1)}, u32[]{:S(2)}, u32[]{:S(2)}) collective-permute-start(f32[128,128]{1,0:T(8,128)} %bitcast.11), channel_id=1, source_target_pairs={{0,1},{1,0},{2,3},{3,2},{4,5},{5,4},{6,7},{7,6},{8,9},{9,8},{10,11... | collective-permute-start | bytes 196616 | tf_op jit(solution)/shard_map/ppermute | solution.py:562
  8.1 8.1 %collective-permute-start.2 = (f32[128,128]{1,0:T(8,128)S(1)}, f32[128,128]{1,0:T(8,128)S(1)}, u32[]{:S(2)}, u32[]{:S(2)}) collective-permute-start(f32[128,128]{1,0:T(8,128)S(1)} %collective-permute-done.1.refs_2_), channel_id=1, source_target_pairs={{0,1},{1,0},{2,3},{3,2},{4,5},{5,4},{6,7},{7,6},{8,9},{9,8},{10,11... | collective-permute-start | bytes 196616 | tf_op jit(solution)/shard_map/ppermute | solution.py:562
  11.2 4.9 %collective-permute-start.4 = (f32[128,128]{1,0:T(8,128)S(1)}, f32[128,128]{1,0:T(8,128)S(1)}, u32[]{:S(2)}, u32[]{:S(2)}) collective-permute-start(f32[128,128]{1,0:T(8,128)S(1)} %collective-permute-done.3.refs_4_), channel_id=1, source_target_pairs={{0,1},{1,0},{2,3},{3,2},{4,5},{5,4},{6,7},{7,6},{8,9},{9,8},{10,11... | collective-permute-start | bytes 196616 | tf_op jit(solution)/shard_map/ppermute | solution.py:562
  12.7 4.3 %collective-permute-start.6 = (f32[128,128]{1,0:T(8,128)S(1)}, f32[128,128]{1,0:T(8,128)S(1)}, u32[]{:S(2)}, u32[]{:S(2)}) collective-permute-start(f32[128,128]{1,0:T(8,128)S(1)} %collective-permute-done.5.refs_6_), channel_id=1, source_target_pairs={{0,1},{1,0},{2,3},{3,2},{4,5},{5,4},{6,7},{7,6},{8,9},{9,8},{10,11... | collective-permute-start | bytes 196616 | tf_op jit(solution)/shard_map/ppermute | solution.py:562
  17.0 9.0 %copy-start.1 = (f32[1,8]{1,0:T(1,128)S(1)}, f32[1,8]{1,0:T(1,128)}, u32[]{:S(2)}) copy-start(f32[1,8]{1,0:T(1,128)} %energies.1) | copy-start | bytes 100
  24.6 8.5 %collective-permute-start.7 = (f32[16,128,128]{2,1,0:T(8,128)}, f32[16,128,128]{2,1,0:T(8,128)S(1)}, u32[]{:S(2)}, u32[]{:S(2)}) collective-permute-start(f32[16,128,128]{2,1,0:T(8,128)} %renew.1), channel_id=1, source_target_pairs={{0,8},{1,9},{2,10},{3,11},{4,12},{5,13},{6,14},{7,15},{16,24},{17,... | collective-permute-start | bytes 3145736 | tf_op jit(solution)/shard_map/ppermute | solution.py:22
  26.0 7.1 %copy-start = (f32[1,16,128,128]{3,2,1,0:T(8,128)S(1)}, f32[1,16,128,128]{3,2,1,0:T(8,128)}, u32[]{:S(2)}) copy-start(f32[1,16,128,128]{3,2,1,0:T(8,128)} %refs_10_.1) | copy-start | bytes 3145732
  35.7 4.4 %collective-permute-start.12 = (f32[136,128]{1,0:T(8,128)S(1)}, f32[136,128]{1,0:T(8,128)S(1)}, u32[]{:S(2)}, u32[]{:S(2)}) collective-permute-start(f32[136,128]{1,0:T(8,128)S(1)} %get-tuple-element.36), channel_id=1, source_target_pairs={{0,1},{1,0},{2,3},{3,2},{4,5},{5,4},{6,7},{7,6},{8,9},{9,8},{10,11... | collective-permute-start | bytes 208904 | tf_op jit(solution)/shard_map/ppermute | solution.py:562
  37.1 4.3 %collective-permute-start.10 = (f32[136,128]{1,0:T(8,128)S(1)}, f32[136,128]{1,0:T(8,128)S(1)}, u32[]{:S(2)}, u32[]{:S(2)}) collective-permute-start(f32[136,128]{1,0:T(8,128)S(1)} %get-tuple-element.34), channel_id=1, source_target_pairs={{0,1},{1,0},{2,3},{3,2},{4,5},{5,4},{6,7},{7,6},{8,9},{9,8},{10,11... | collective-permute-start | bytes 208904 | tf_op jit(solution)/shard_map/ppermute | solution.py:562
  37.8 6.1 %collective-permute-start.8 = (f32[136,128]{1,0:T(8,128)S(1)}, f32[136,128]{1,0:T(8,128)S(1)}, u32[]{:S(2)}, u32[]{:S(2)}) collective-permute-start(f32[136,128]{1,0:T(8,128)S(1)} %get-tuple-element.32), channel_id=1, source_target_pairs={{0,1},{1,0},{2,3},{3,2},{4,5},{5,4},{6,7},{7,6},{8,9},{9,8},{10,11... | collective-permute-start | bytes 208904 | tf_op jit(solution)/shard_map/ppermute | solution.py:562
  39.1 6.2 %collective-permute-start.14 = (f32[136,128]{1,0:T(8,128)S(1)}, f32[136,128]{1,0:T(8,128)S(1)}, u32[]{:S(2)}, u32[]{:S(2)}) collective-permute-start(f32[136,128]{1,0:T(8,128)S(1)} %get-tuple-element.37), channel_id=1, source_target_pairs={{0,1},{1,0},{2,3},{3,2},{4,5},{5,4},{6,7},{7,6},{8,9},{9,8},{10,11... | collective-permute-start | bytes 208904 | tf_op jit(solution)/shard_map/ppermute | solution.py:562
  40.1 5.2 %collective-permute-start.13 = (f32[136,128]{1,0:T(8,128)S(1)}, f32[136,128]{1,0:T(8,128)S(1)}, u32[]{:S(2)}, u32[]{:S(2)}) collective-permute-start(f32[136,128]{1,0:T(8,128)S(1)} %add.11), channel_id=1, source_target_pairs={{0,2},{1,3},{2,0},{3,1},{4,6},{5,7},{6,4},{7,5},{8,10},{9,11},{10,... | collective-permute-start | bytes 208904 | tf_op jit(solution)/shard_map/ppermute | solution.py:562
  41.4 6.0 %collective-permute-start.11 = (f32[136,128]{1,0:T(8,128)S(1)}, f32[136,128]{1,0:T(8,128)S(1)}, u32[]{:S(2)}, u32[]{:S(2)}) collective-permute-start(f32[136,128]{1,0:T(8,128)S(1)} %add.10), channel_id=1, source_target_pairs={{0,4},{1,5},{2,6},{3,7},{4,0},{5,1},{6,2},{7,3},{8,12},{9,13},{10,... | collective-permute-start | bytes 208904 | tf_op jit(solution)/shard_map/ppermute | solution.py:562
  43.9 6.2 %collective-permute-start.9 = (f32[136,128]{1,0:T(8,128)S(1)}, f32[136,128]{1,0:T(8,128)S(1)}, u32[]{:S(2)}, u32[]{:S(2)}) collective-permute-start(f32[136,128]{1,0:T(8,128)S(1)} %add.9), channel_id=1, source_target_pairs={{0,6},{1,7},{2,4},{3,5},{4,2},{5,3},{6,0},{7,1},{8,14},{9,15},{10,... | collective-permute-start | bytes 208904 | tf_op jit(solution)/shard_map/ppermute | solution.py:562

commit v3 on v2

--- a/solution.py
+++ b/solution.py
@@ -8,6 +8,7 @@
 from jax.sharding import PartitionSpec as P
 
 MAXT = 24
+ORDER = (0, 1, 4, 2, 6, 5, 3, 7)
 F32 = jnp.float32
 BF16 = jnp.bfloat16
 VMEM = pl.BlockSpec(memory_space=pltpu.VMEM)
@@ -220,8 +221,10 @@
     )
     listed = over_entries(rows, chosen)
     ints[2:3] = listed[0:1].astype(jnp.int32)
-    ints[3:4] = listed[4:5].astype(jnp.int32)
-    ints[4:5] = jnp.full((1, live), jnp.sum(spilled)).astype(jnp.int32)
+    count = jnp.sum(spilled)
+    past = lax.broadcasted_iota(jnp.int32, (1, live), 1).astype(F32) >= count
+    ints[3:4] = jnp.where(past, 2 * w, listed[4:5].astype(jnp.int32))
+    ints[4:5] = jnp.full((1, live), count).astype(jnp.int32)
     floats[2:3] = listed[1:2] + listed[2:3] + listed[3:4]
     floats[3:4] = listed[5:6]
 
@@ -233,7 +236,12 @@
         blocks[to] = held + floats[2, q] * blocks[ints[2, q]]
         return unused
 
-    lax.fori_loop(0, ints[4, 0], add, 0)
+    def four(q, unused):
+        for i in range(4):
+            add(4 * q + i, unused)
+        return unused
+
+    lax.fori_loop(0, lax.div(ints[4, 0] + 3, 4), four, 0)
 
 
 def two_terms(ints, floats, blocks, g):
@@ -241,10 +249,10 @@
 
 
 def prepare_kernel(n, *refs):
-    psi, given, refs = refs[0], refs[1:12], refs[12:]
+    psi, given, refs = refs[0], refs[1:13], refs[13:]
     lefts, rights, up_ints, up_floats, mv_ints, mv_floats, own = refs[:7]
-    held = refs[7:18]
-    arrived, own_arrived = refs[18:]
+    held = refs[7:19]
+    arrived, own_arrived = refs[19:]
     own_copy = pltpu.make_async_copy(psi.at[0, 0], own, own_arrived)
     own_copy.start()
     copies = [
@@ -253,12 +261,13 @@
     ]
     for copy in copies:
         copy.start()
-    up_counts, up_block, up_top, up_bot, up_coef, mv_counts, mv_src, mv_dst, mv_coef = held[:9]
-    left, right = held[9:]
+    up_counts, up_block, up_top, up_bot, up_coef = held[:5]
+    mv_counts, mv_src, mv_dst, mv_coef, energies = held[5:10]
+    left, right = held[10:]
     channels, w = left.shape[1], left.shape[2]
     live = up_block.shape[2]
     me = lax.axis_index("tile")
-    for copy in copies[:9]:
+    for copy in copies[:10]:
         copy.wait()
     channel = channel_row(up_counts, live, channels)
     plan_terms(
@@ -268,14 +277,19 @@
     plan_terms(
         channel * n + (mv_dst[0] ^ me), channel * n + (mv_src[0] ^ me), mv_coef[0], mv_ints, mv_floats
     )
-    copies[9].wait()
+    at = lax.broadcasted_iota(jnp.int32, (1, live), 1)
+    by_slot = jnp.zeros((1, live), F32)
+    for k in range(n):
+        by_slot += jnp.where(at == k, energies[0, k ^ me], 0.0)
+    mv_floats[4:5] = by_slot
+    copies[10].wait()
 
     def halve_left(c, unused):
         lefts[pl.ds(pl.multiple_of(c * w, w), w)] = side_by_side(left[0, c])
         return unused
 
     lax.fori_loop(0, channels, halve_left, 0, unroll=2)
-    copies[10].wait()
+    copies[11].wait()
 
     def halve_right(c, unused):
         head, tail = heads_tails(right[0, c])
@@ -306,7 +320,7 @@
         out_specs=(VMEM,) * 7,
         scratch_shapes=[
             *(
-                pltpu.SMEM(x.shape, x.dtype) if x.shape[-1] == channels else pltpu.VMEM(x.shape, x.dtype)
+                pltpu.SMEM(x.shape, x.dtype) if x.shape[-1] in (channels, n) else pltpu.VMEM(x.shape, x.dtype)
                 for x in given
             ),
             pltpu.SemaphoreType.DMA((len(given),)),
@@ -329,7 +343,7 @@
 
 
 def renew_kernel(n, *refs):
-    tiles = refs[:n]
+    tiles = [refs[ORDER.index(k)] for k in range(n)]
     lefts, int_table, float_table, out, bottoms, tops, entries, renewed, ints, floats, arrived, left = refs[n:]
     channels, w = out.shape[0], out.shape[1]
     copies = fetch_tables((int_table, float_table), (ints, floats), arrived)
@@ -354,20 +368,26 @@
                 entries[(g * group + h) * n + k] = found[h * w : (h + 1) * w, k * w : (k + 1) * w]
         return unused
 
-    lax.fori_loop(0, 2, multiply, 0)
+    lax.fori_loop(0, 2, multiply, 0, unroll=2)
     for copy in copies:
         copy.wait()
     spill(ints, floats, entries)
 
-    def finish(b, unused):
-        pairs = [heads_tails(two_terms(ints, floats, entries, b * n + k)) for k in range(n)]
-        stack = [jnp.concatenate([pair[i] for pair in pairs], axis=0) for i in range(2)]
-        found = product(tops[...], jnp.concatenate(stack, axis=1))
-        renewed[b] = (found[:w, :w] + found[w:, w:]) + (found[:w, w:] + found[w:, :w])
-        pltpu.make_async_copy(renewed.at[b], out.at[b], left.at[b]).start()
+    def finish(g, unused):
+        heads, tails = [], []
+        for b in (2 * g, 2 * g + 1):
+            pairs = [heads_tails(two_terms(ints, floats, entries, b * n + k)) for k in range(n)]
+            heads.append(jnp.concatenate([pair[0] for pair in pairs], axis=0))
+            tails.append(jnp.concatenate([pair[1] for pair in pairs], axis=0))
+        small = product(tops[w:], jnp.concatenate(heads, axis=1))
+        for i in range(2):
+            b = 2 * g + i
+            found = product(tops[0:w], jnp.concatenate([heads[i], tails[i]], axis=1))
+            renewed[b] = found[:, :w] + (found[:, w:] + small[:, i * w : (i + 1) * w])
+            pltpu.make_async_copy(renewed.at[b], out.at[b], left.at[b]).start()
         return unused
 
-    lax.fori_loop(0, channels, finish, 0, unroll=8)
+    lax.fori_loop(0, channels // 2, finish, 0, unroll=4)
     for b in range(channels):
         pltpu.make_async_copy(renewed.at[b], out.at[b], left.at[b]).wait()
 
@@ -382,7 +402,7 @@
         scratch_shapes=[
             pltpu.VMEM((4 * w, n * w), BF16),
             pltpu.VMEM((2 * w, n * w), BF16),
-            pltpu.VMEM((2 * w, w, w), F32),
+            pltpu.VMEM((2 * w + 1, w, w), F32),
             pltpu.VMEM((channels, w, w), F32),
             pltpu.SMEM(int_table.shape, jnp.int32),
             pltpu.SMEM(float_table.shape, F32),
@@ -392,31 +412,21 @@
         compiler_params=pltpu.CompilerParams(vmem_limit_bytes=28 << 20),
         cost_estimate=pl.CostEstimate(flops=10**10, bytes_accessed=3 << 20, transcendentals=0),
         name="renew",
-    )(*tiles, lefts, int_table, float_table)
-
-
-def source_kernel(n, energies, *refs):
+    )(*(tiles[k] for k in ORDER), lefts, int_table, float_table)
+
+
+def source_kernel(n, *refs):
     tiles = refs[:n]
-    rights, int_table, float_table, out, stats, sources, entries, ints, floats, arrived = refs[n:]
+    rights, int_table, float_table, entries, stats, sources, ints, floats, arrived = refs[n:]
     channels, w = rights.shape[0], rights.shape[2]
     copies = fetch_tables((int_table, float_table), (ints, floats), arrived)
-    me = lax.axis_index("tile")
-    weight = jnp.zeros((8, w), F32)
-    energy = jnp.zeros((8, w), F32)
     for k in range(n):
         at = slice(k * w, (k + 1) * w)
-        value = tiles[k][...]
-        head, tail = heads_tails(value)
+        head, tail = heads_tails(tiles[k][...])
         sources[at, 0:w] = head
         sources[at, w : 2 * w] = tail
         sources[at, 2 * w : 3 * w] = head
         sources[at, 3 * w : 4 * w] = tail
-        squares = jnp.sum((value * value).reshape(w // 8, 8, w), axis=0)
-        weight += squares
-        energy += energies[0, k ^ me] * squares
-    stats[0:8] = weight
-    stats[8:16] = energy
-    stats[16:24] = jnp.full((8, w), energies[0, me], F32)
     group = channels // 2
 
     def multiply(g, unused):
@@ -430,90 +440,112 @@
                 entries[(g * group + h) * n + k] = found[k * w : (k + 1) * w, h * w : (h + 1) * w]
         return unused
 
-    lax.fori_loop(0, 2, multiply, 0)
+    lax.fori_loop(0, 2, multiply, 0, unroll=2)
     for copy in copies:
         copy.wait()
     spill(ints, floats, entries)
-
-    def finish(c, unused):
-        rows = pl.ds(pl.multiple_of(c * w, w), w)
-        for k in range(n):
-            out[k, rows] = side_by_side(two_terms(ints, floats, entries, c * n + k))
-        return unused
-
-    lax.fori_loop(0, channels, finish, 0, unroll=2)
-
-
-def source_call(energies, tiles, rights, int_table, float_table):
-    n, w, channels = len(tiles), rights.shape[2], rights.shape[0]
+    weight = jnp.zeros((8, w), F32)
+    energy = jnp.zeros((8, w), F32)
+    for k in range(n):
+        value = tiles[k][...]
+        squares = jnp.sum((value * value).reshape(w // 8, 8, w), axis=0)
+        weight += squares
+        energy += floats[4, k] * squares
+    stats[0:8] = weight
+    stats[8:16] = energy
+    stats[16:24] = jnp.full((8, w), floats[4, 0], F32)
+
+
+def source_call(tiles, rights, int_table, float_table):
+    n, w = len(tiles), rights.shape[2]
     return pl.pallas_call(
         functools.partial(source_kernel, n),
         out_shape=(
-            jax.ShapeDtypeStruct((n, channels * w, 2 * w), BF16),
+            pltpu.VMEM((2 * w + 1, w, w), F32),
             jax.ShapeDtypeStruct((24, w), F32),
         ),
-        in_specs=[SMEM] + [VMEM] * (n + 1) + [ANY] * 2,
+        in_specs=[VMEM] * (n + 1) + [ANY] * 2,
         out_specs=(VMEM, VMEM),
         scratch_shapes=[
             pltpu.VMEM((n * w, 4 * w), BF16),
-            pltpu.VMEM((2 * w, w, w), F32),
             pltpu.SMEM(int_table.shape, jnp.int32),
             pltpu.SMEM(float_table.shape, F32),
             pltpu.SemaphoreType.DMA((2,)),
         ],
-        compiler_params=pltpu.CompilerParams(vmem_limit_bytes=28 << 20),
+        compiler_params=pltpu.CompilerParams(vmem_limit_bytes=12 << 20),
         cost_estimate=pl.CostEstimate(flops=10**10, bytes_accessed=10 << 20, transcendentals=0),
         name="sources",
-    )(energies, *tiles, rights, int_table, float_table)
+    )(*tiles, rights, int_table, float_table)
 
 
 def apply_kernel(n, *refs):
     tiles = refs[:n]
-    own, received, blocks = refs[n : n + 3]
-    outs = refs[n + 3 : 2 * n + 3]
-    env, lefts, arrived = refs[2 * n + 3 :]
-    channels, w = env.shape[0], env.shape[1]
+    own, received, entries, int_table, float_table = refs[n : n + 5]
+    outs = refs[n + 5 : 2 * n + 5]
+    lefts, ints, floats, arrived = refs[2 * n + 5 :]
+    channels, w = own.shape[0], own.shape[1]
+    copies = fetch_tables((int_table, float_table), (ints, floats), arrived)
     leading = lax.axis_index("seg") == 0
+
+    def halve(env):
+        for c in range(channels):
+            head, tail = heads_tails(env[c])
+            lefts[0:w, c * w : (c + 1) * w] = head
+            lefts[w : 2 * w, c * w : (c + 1) * w] = tail
 
     @pl.when(leading)
     def _():
-        pltpu.make_async_copy(own, env, arrived).start()
+        halve(own)
 
     @pl.when(jnp.logical_not(leading))
     def _():
-        pltpu.make_async_copy(received, env, arrived).start()
-
-    pltpu.make_async_copy(own, env, arrived).wait()
-    for c in range(channels):
-        head, tail = heads_tails(env[c])
-        lefts[0:w, c * w : (c + 1) * w] = head
-        lefts[w : 2 * w, c * w : (c + 1) * w] = tail
+        halve(received)
+
+    for copy in copies:
+        copy.wait()
     inner = jnp.zeros((8, w), F32)
-    for k in range(n):
-        found = jnp.dot(lefts[...], blocks[k], preferred_element_type=F32)
-        value = (found[:w, :w] + found[w:, w:]) + (found[:w, w:] + found[w:, :w])
-        outs[k][0:w] = value
-        inner += jnp.sum((value * tiles[k][...]).reshape(w // 8, 8, w), axis=0)
+    for k in range(0, n, 2):
+        heads, tails = [], []
+        for t in (k, k + 1):
+            pairs = [
+                heads_tails(two_terms(ints, floats, entries, c * n + t)) for c in range(channels)
+            ]
+            heads.append(jnp.concatenate([pair[0] for pair in pairs], axis=0))
+            tails.append(jnp.concatenate([pair[1] for pair in pairs], axis=0))
+        small = product(lefts[w:], jnp.concatenate(heads, axis=1))
+        for i in range(2):
+            found = product(lefts[0:w], jnp.concatenate([heads[i], tails[i]], axis=1))
+            value = found[:, :w] + (found[:, w:] + small[:, i * w : (i + 1) * w])
+            outs[k + i][0:w] = value
+            inner += jnp.sum((value * tiles[k + i][...]).reshape(w // 8, 8, w), axis=0)
     for k in range(n):
         outs[k][w : w + 8] = inner
 
 
-def apply_call(tiles, own, received, blocks):
+def apply_call(tiles, own, received, entries, int_table, float_table):
     n, w = len(tiles), own.shape[1]
     return pl.pallas_call(
         functools.partial(apply_kernel, n),
         out_shape=tuple(jax.ShapeDtypeStruct((w + 8, w), F32) for _ in range(n)),
-        in_specs=[VMEM] * n + [ANY, ANY, VMEM],
+        in_specs=[VMEM] * (n + 3) + [ANY] * 2,
         out_specs=(VMEM,) * n,
         scratch_shapes=[
-            pltpu.VMEM(own.shape, F32),
             pltpu.VMEM((2 * w, own.shape[0] * w), BF16),
-            pltpu.SemaphoreType.DMA,
+            pltpu.SMEM(int_table.shape, jnp.int32),
+            pltpu.SMEM(float_table.shape, F32),
+            pltpu.SemaphoreType.DMA((2,)),
         ],
-        compiler_params=pltpu.CompilerParams(vmem_limit_bytes=8 << 20),
+        compiler_params=pltpu.CompilerParams(vmem_limit_bytes=12 << 20),
         cost_estimate=pl.CostEstimate(flops=5 * 10**9, bytes_accessed=10 << 20, transcendentals=0),
         name="applied",
-    )(*tiles, own, received, blocks)
+    )(
+        *tiles,
+        own,
+        received,
+        pltpu.with_memory_space_constraint(entries, pltpu.VMEM),
+        int_table,
+        float_table,
+    )
 
 
 def finish_kernel(*refs):
@@ -562,27 +594,23 @@
         return lax.ppermute(value, "tile", [(i, i ^ k) for i in range(n)])
 
     own = psi[0, 0]
-    tiles = {0: own, 1: across(own, 1)}
-    for k in range(n - 2, 0, -2):
-        tiles[k] = across(own, k)
-    for k in range(2, n, 2):
-        tiles[k + 1] = across(tiles[k], 1)
-    tiles = [tiles[k] for k in range(n)]
-
-    given = [up_counts, up_block, up_top, up_bot, up_coef, mv_counts, mv_src, mv_dst, mv_coef]
+    tiles = {k: across(own, k) for k in (1, 2, 3, 4, 6)}
+    tiles[5], tiles[7] = across(tiles[4], 1), across(tiles[6], 1)
+
+    given = [up_counts, up_block, up_top, up_bot, up_coef, mv_counts, mv_src, mv_dst, mv_coef, site_energy]
     lefts, rights, up_ints, up_floats, mv_ints, mv_floats, own = prepare_call(
         n, psi, [*given, left_env, right_env]
     )
     tiles[0] = own
+    tiles = [tiles[k] for k in range(n)]
     renewal = renew_call(tiles, lefts, up_ints, up_floats, left_env.shape[1])
-    received = passed_along(renewal, "seg", 1)
-    blocks, stats = source_call(site_energy, tiles, rights, mv_ints, mv_floats)
-    partials = apply_call(tiles, left_env[0], received, blocks)
-
-    parts = [partials[0]]
-    for k in range(n - 2, 0, -2):
+    received = lax.ppermute(renewal, "seg", [(0, 1), (1, 0)])
+    entries, stats = source_call(tiles, rights, mv_ints, mv_floats)
+    partials = apply_call(tiles, left_env[0], received, entries, mv_ints, mv_floats)
+
+    parts = [partials[0], across(partials[1], 1)]
+    for k in (2, 4, 6):
         parts.append(across(partials[k] + across(partials[k + 1], 1), k))
-    parts.append(across(partials[1], 1))
     residual, quotient = finish_call(parts, own, stats)
     return (residual[None, None], renewal[None], quotient[0, :1])
 

time: 51.1 us -> 45.4 us (0.89)
  Pallas kernels: 20 us -> 16.3 us
  waiting for transfers between devices: 9.45 us -> 6.14 us
  starting transfers between devices: 20.7 us -> 22.1 us
    pallas_call x1, Pallas kernels: 7.1 us -> 3.48 us  [source_call(): pl.pallas_call(functools.partial(source_kernel, n), out_shape=(pltpu.VMEM...]
    ppermute x14, waiting for transfers between devices: 9.45 us -> 6.14 us  [across(): return lax.ppermute(value, 'tile', [(i, i ^ k) for i in range(n)])]
    ppermute x14, starting transfers between devices: 19.3 us -> 22 us  [across(): return lax.ppermute(value, 'tile', [(i, i ^ k) for i in range(n)])]
    ppermute x1, starting transfers between devices: 1.36 us -> 0.07 us  [shards(): received = lax.ppermute(renewal, 'seg', [(0, 1), (1, 0)])]
    pallas_call x1, Pallas kernels: 7.58 us -> 6.85 us  [renew_call(): pl.pallas_call(functools.partial(renew_kernel, n), out_shape=jax.ShapeDty...]
    pallas_call x1, Pallas kernels: 2.59 us -> 3.22 us  [apply_call(): pl.pallas_call(functools.partial(apply_kernel, n), out_shape=tuple((jax.S...]
  transfers between devices with their start and end apart: 15 -> 15, of which waited for: 6 -> 6; matrix products, arithmetic and copies ran while one was open for 0% -> 0% of each run, Pallas kernels for 18% -> 12%
where the time goes in v3:
time: 45.4 us
  starting transfers between devices  22.1 us (49%)
  Pallas kernels  16.3 us (36%)
  waiting for transfers between devices  6.14 us (14%)
  between operations  0.77 us (2%)
    ppermute x14, starting transfers between devices, across(): return lax.ppermute(value, 'tile', [(i, i ^ k) for i in range(n)])  22 us
    pallas_call x1, Pallas kernels, renew_call(): pl.pallas_call(functools.partial(renew_kernel, n), out_shape=jax.ShapeDty...  6.85 us
    ppermute x14, waiting for transfers between devices, across(): return lax.ppermute(value, 'tile', [(i, i ^ k) for i in range(n)])  6.14 us
    pallas_call x1, Pallas kernels, source_call(): pl.pallas_call(functools.partial(source_kernel, n), out_shape=(pltpu.VMEM...  3.48 us
    pallas_call x1, Pallas kernels, apply_call(): pl.pallas_call(functools.partial(apply_kernel, n), out_shape=tuple((jax.S...  3.22 us
    pallas_call x1, Pallas kernels, prepare_call(): pl.pallas_call(functools.partial(prepare_kernel, n), out_shape=(jax.Shape...  1.96 us
  transfers between devices with their start and end apart: 15, of which 6 were waited for; matrix products, arithmetic and copies ran while one was open for 0% of the time, Pallas kernels for 12%

profile of v3, /device:TPU:0, one launch (start us, length us, event | category | flops | bytes accessed | tf_op | source)
XLA Modules:
  0.0 45.4 jit_solution(9249807956384229804)
XLA Ops:
  0.6 4.1 %collective-permute-start.3 = (f32[128,128]{1,0:T(8,128)}, f32[128,128]{1,0:T(8,128)S(1)}, u32[]{:S(2)}, u32[]{:S(2)}) collective-permute-start(f32[128,128]{1,0:T(8,128)} %bitcast.8), channel_id=1, source_target_pairs={{0,4},{1,5},{2,6},{3,7},{4,0},{5,1},{6,2},{7,3},{8,12},{9,13},{10,... | collective-permute-start | bytes 196616 | tf_op jit(solution)/shard_map/ppermute | solution.py:594
  4.7 1.3 %collective-permute-start.5 = (f32[128,128]{1,0:T(8,128)}, f32[128,128]{1,0:T(8,128)S(1)}, u32[]{:S(2)}, u32[]{:S(2)}) collective-permute-start(f32[128,128]{1,0:T(8,128)} %bitcast.9), channel_id=1, source_target_pairs={{0,6},{1,7},{2,4},{3,5},{4,2},{5,3},{6,0},{7,1},{8,14},{9,15},{10,... | collective-permute-start | bytes 196616 | tf_op jit(solution)/shard_map/ppermute | solution.py:594
  6.1 1.5 %collective-permute-start = (f32[128,128]{1,0:T(8,128)}, f32[128,128]{1,0:T(8,128)S(1)}, u32[]{:S(2)}, u32[]{:S(2)}) collective-permute-start(f32[128,128]{1,0:T(8,128)} %bitcast.10), channel_id=1, source_target_pairs={{0,1},{1,0},{2,3},{3,2},{4,5},{5,4},{6,7},{7,6},{8,9},{9,8},{10,11... | collective-permute-start | bytes 196616 | tf_op jit(solution)/shard_map/ppermute | solution.py:594
  7.6 0.2 collective-permute-start.1
  7.8 1.7 %collective-permute-start.2 = (f32[128,128]{1,0:T(8,128)}, f32[128,128]{1,0:T(8,128)S(1)}, u32[]{:S(2)}, u32[]{:S(2)}) collective-permute-start(f32[128,128]{1,0:T(8,128)} %bitcast.12), channel_id=1, source_target_pairs={{0,3},{1,2},{2,1},{3,0},{4,7},{5,6},{6,5},{7,4},{8,11},{9,10},{10,... | collective-permute-start | bytes 196616 | tf_op jit(solution)/shard_map/ppermute | solution.py:594
  9.6 0.0 collective-permute-done.3.refs_2_.refs_4_
  9.6 1.7 %collective-permute-start.4 = (f32[128,128]{1,0:T(8,128)S(1)}, f32[128,128]{1,0:T(8,128)S(1)}, u32[]{:S(2)}, u32[]{:S(2)}) collective-permute-start(f32[128,128]{1,0:T(8,128)S(1)} %collective-permute-done.3.refs_2_.refs_4_), channel_id=1, source_target_pairs={{0,1},{1,0},{2,3},{3,2},{4,5},{5,4},{6,7},{7,6},{8,9},{9,8},{10,11... | collective-permute-start | bytes 196616 | tf_op jit(solution)/shard_map/ppermute | solution.py:594
  11.3 0.2 collective-permute-done.5.refs_4_.refs_6_
  11.5 1.1 %collective-permute-start.6 = (f32[128,128]{1,0:T(8,128)S(1)}, f32[128,128]{1,0:T(8,128)S(1)}, u32[]{:S(2)}, u32[]{:S(2)}) collective-permute-start(f32[128,128]{1,0:T(8,128)S(1)} %collective-permute-done.5.refs_4_.refs_6_), channel_id=1, source_target_pairs={{0,1},{1,0},{2,3},{3,2},{4,5},{5,4},{6,7},{7,6},{8,9},{9,8},{10,11... | collective-permute-start | bytes 196616 | tf_op jit(solution)/shard_map/ppermute | solution.py:594
  12.6 2.0 %prepare.1 = (bf16[2048,256]{1,0:T(8,128)(2,1)S(1)}, bf16[16,256,128]{2,1,0:T(8,128)(2,1)S(1)}, s32[8,192]{1,0:T(8,128)S(1)}, f32[8,192]{1,0:T(8,128)S(1)}, s32[...) custom-call(f32[1,1,128,128]{3,2,1,0:T(8,128)} %refs_0_.1, s32[1,1,16]{2,1,0:T(1,128)} %refs_1_.1, ...), custom_call_target="tpu_custom_call" | custom-call | flops 1000000000 | bytes 6291456 | tf_op jit(solution)/shard_map/prepare/pallas_call | solution.py:308
  14.6 0.0 collective-permute-done.refs_1_
  14.6 0.0 collective-permute-done.1.refs_3_.refs_2_
  14.6 0.0 collective-permute-done.2.refs_6_.refs_3_
  14.6 0.0 collective-permute-done.4.refs_5_
  14.7 1.1 %collective-permute-done.6.refs_7_ = f32[128,128]{1,0:T(8,128)S(1)} collective-permute-done((f32[128,128]{1,0:T(8,128)S(1)}, f32[128,128]{1,0:T(8,128)S(1)}, u32[]{:S(2)}, u32[]{:S(2)}) %collective-permute-start.6) | collective-permute-done | bytes 65568 | tf_op jit(solution)/shard_map/ppermute | solution.py:594
  15.8 6.9 %renew.1 = f32[16,128,128]{2,1,0:T(8,128)} custom-call(f32[128,128]{1,0:T(8,128)S(1)} %get-tuple-element.22.refs_0_.refs_5_, f32[128,128]{1,0:T(8,128)S(1)} %collective-permute-done.refs_1_, f32[128,128]{1,0:T(8,128)S(1)} %collective-permute-done.3.refs_2_.refs_4_, f32[128,128]{1,0:T(8,128)S(1)} %collective-permute-done.1.refs_3_.refs_2_, ...), custom_call_target="tpu_custom_call" | custom-call | flops 10000000000 | bytes 3145728 | tf_op jit(solution)/shard_map/renew/pallas_call | solution.py:397
  22.6 0.1 collective-permute-start.7
  22.7 0.0 copy-start
  22.7 3.5 %sources.1 = (f32[257,128,128]{2,1,0:T(8,128)S(1)}, f32[24,128]{1,0:T(8,128)S(1)}) custom-call(f32[128,128]{1,0:T(8,128)S(1)} %get-tuple-element.22.refs_0_.refs_5_, f32[128,128]{1,0:T(8,128)S(1)} %collective-permute-done.refs_1_, f32[128,128]{1,0:T(8,128)S(1)} %collective-permute-done.1.refs_3_.refs_2_, ...), custom_call_target="tpu_custom_call" | custom-call | flops 10000000000 | bytes 10485760 | tf_op jit(solution)/shard_map/sources/pallas_call | solution.py:461
  26.2 0.0 collective-permute-done.7.refs_9_
  26.2 0.0 copy-done
  26.2 3.2 %applied.1 = (f32[136,128]{1,0:T(8,128)S(1)}, f32[136,128]{1,0:T(8,128)S(1)}, f32[136,128]{1,0:T(8,128)S(1)}, f32[136,128]{1,0:T(8,128)S(1)}, f32[136,128]{1,0:T...) custom-call(f32[128,128]{1,0:T(8,128)S(1)} %get-tuple-element.22.refs_0_.refs_5_, ...), custom_call_target="tpu_custom_call" | custom-call | flops 5000000000 | bytes 10485760 | tf_op jit(solution)/shard_map/applied/pallas_call | solution.py:527
  29.5 1.3 %collective-permute-start.13 = (f32[136,128]{1,0:T(8,128)S(1)}, f32[136,128]{1,0:T(8,128)S(1)}, u32[]{:S(2)}, u32[]{:S(2)}) collective-permute-start(f32[136,128]{1,0:T(8,128)S(1)} %get-tuple-element.37), channel_id=1, source_target_pairs={{0,1},{1,0},{2,3},{3,2},{4,5},{5,4},{6,7},{7,6},{8,9},{9,8},{10,11... | collective-permute-start | bytes 208904 | tf_op jit(solution)/shard_map/ppermute | solution.py:594
  30.7 0.8 %collective-permute-start.11 = (f32[136,128]{1,0:T(8,128)S(1)}, f32[136,128]{1,0:T(8,128)S(1)}, u32[]{:S(2)}, u32[]{:S(2)}) collective-permute-start(f32[136,128]{1,0:T(8,128)S(1)} %get-tuple-element.35), channel_id=1, source_target_pairs={{0,1},{1,0},{2,3},{3,2},{4,5},{5,4},{6,7},{7,6},{8,9},{9,8},{10,11... | collective-permute-start | bytes 208904 | tf_op jit(solution)/shard_map/ppermute | solution.py:594
  31.5 1.2 %collective-permute-start.9 = (f32[136,128]{1,0:T(8,128)S(1)}, f32[136,128]{1,0:T(8,128)S(1)}, u32[]{:S(2)}, u32[]{:S(2)}) collective-permute-start(f32[136,128]{1,0:T(8,128)S(1)} %get-tuple-element.33), channel_id=1, source_target_pairs={{0,1},{1,0},{2,3},{3,2},{4,5},{5,4},{6,7},{7,6},{8,9},{9,8},{10,11... | collective-permute-start | bytes 208904 | tf_op jit(solution)/shard_map/ppermute | solution.py:594
  32.8 0.8 %collective-permute-start.8 = (f32[136,128]{1,0:T(8,128)S(1)}, f32[136,128]{1,0:T(8,128)S(1)}, u32[]{:S(2)}, u32[]{:S(2)}) collective-permute-start(f32[136,128]{1,0:T(8,128)S(1)} %get-tuple-element.31), channel_id=1, source_target_pairs={{0,1},{1,0},{2,3},{3,2},{4,5},{5,4},{6,7},{7,6},{8,9},{9,8},{10,11... | collective-permute-start | bytes 208904 | tf_op jit(solution)/shard_map/ppermute | solution.py:594
  33.6 0.9 %collective-permute-done.13 = f32[136,128]{1,0:T(8,128)S(1)} collective-permute-done((f32[136,128]{1,0:T(8,128)S(1)}, f32[136,128]{1,0:T(8,128)S(1)}, u32[]{:S(2)}, u32[]{:S(2)}) %collective-permute-start.13) | collective-permute-done | bytes 69664 | tf_op jit(solution)/shard_map/ppermute | solution.py:594
  34.5 4.1 %collective-permute-start.14 = (f32[136,128]{1,0:T(8,128)S(1)}, f32[136,128]{1,0:T(8,128)S(1)}, u32[]{:S(2)}, u32[]{:S(2)}) collective-permute-start(f32[136,128]{1,0:T(8,128)S(1)} %add.11), channel_id=1, source_target_pairs={{0,6},{1,7},{2,4},{3,5},{4,2},{5,3},{6,0},{7,1},{8,14},{9,15},{10,... | collective-permute-start | bytes 208904 | tf_op jit(solution)/shard_map/ppermute | solution.py:594
  38.6 0.0 collective-permute-done.11
  38.6 0.1 collective-permute-start.12
  38.7 0.0 collective-permute-done.9
  38.7 2.0 %collective-permute-start.10 = (f32[136,128]{1,0:T(8,128)S(1)}, f32[136,128]{1,0:T(8,128)S(1)}, u32[]{:S(2)}, u32[]{:S(2)}) collective-permute-start(f32[136,128]{1,0:T(8,128)S(1)} %add.9), channel_id=1, source_target_pairs={{0,2},{1,3},{2,0},{3,1},{4,6},{5,7},{6,4},{7,5},{8,10},{9,11},{10,... | collective-permute-start | bytes 208904 | tf_op jit(solution)/shard_map/ppermute | solution.py:594
  40.7 0.0 collective-permute-done.8.refs_1_
  40.7 0.9 %collective-permute-done.14.refs_4_ = f32[136,128]{1,0:T(8,128)S(1)} collective-permute-done((f32[136,128]{1,0:T(8,128)S(1)}, f32[136,128]{1,0:T(8,128)S(1)}, u32[]{:S(2)}, u32[]{:S(2)}) %collective-permute-start.14) | collective-permute-done | bytes 69664 | tf_op jit(solution)/shard_map/ppermute | solution.py:594
  41.6 2.4 %collective-permute-done.12.refs_3_ = f32[136,128]{1,0:T(8,128)S(1)} collective-permute-done((f32[136,128]{1,0:T(8,128)S(1)}, f32[136,128]{1,0:T(8,128)S(1)}, u32[]{:S(2)}, u32[]{:S(2)}) %collective-permute-start.12) | collective-permute-done | bytes 69664 | tf_op jit(solution)/shard_map/ppermute | solution.py:594
  44.1 0.5 %collective-permute-done.10.refs_2_ = f32[136,128]{1,0:T(8,128)S(1)} collective-permute-done((f32[136,128]{1,0:T(8,128)S(1)}, f32[136,128]{1,0:T(8,128)S(1)}, u32[]{:S(2)}, u32[]{:S(2)}) %collective-permute-start.10) | collective-permute-done | bytes 69664 | tf_op jit(solution)/shard_map/ppermute | solution.py:594
  44.6 0.8 %finish.1 = (f32[128,128]{1,0:T(8,128)}, f32[1,128]{1,0:T(1,128)}) custom-call(f32[136,128]{1,0:T(8,128)S(1)} %get-tuple-element.30.refs_0_, f32[136,128]{1,0:T(8,128)S(1)} %collective-permute-done.8.refs_1_, f32[136,128]{1,0:T(8,128)S(1)} %collective-permute-done.10.refs_2_, f32[136,128]{1,0:T(8,128)S(1)} %collective-permute-done.12.refs_3_, ...), custom_call_target="tpu_custom_call" | custom-call | tf_op jit(solution)/shard_map/finish/pallas_call | solution.py:567
  (3 shorter events, 0.0 us)
Async XLA Ops:
  0.6 8.9 %collective-permute-start.3 = (f32[128,128]{1,0:T(8,128)}, f32[128,128]{1,0:T(8,128)S(1)}, u32[]{:S(2)}, u32[]{:S(2)}) collective-permute-start(f32[128,128]{1,0:T(8,128)} %bitcast.8), channel_id=1, source_target_pairs={{0,4},{1,5},{2,6},{3,7},{4,0},{5,1},{6,2},{7,3},{8,12},{9,13},{10,... | collective-permute-start | bytes 196616 | tf_op jit(solution)/shard_map/ppermute | solution.py:594
  4.7 6.8 %collective-permute-start.5 = (f32[128,128]{1,0:T(8,128)}, f32[128,128]{1,0:T(8,128)S(1)}, u32[]{:S(2)}, u32[]{:S(2)}) collective-permute-start(f32[128,128]{1,0:T(8,128)} %bitcast.9), channel_id=1, source_target_pairs={{0,6},{1,7},{2,4},{3,5},{4,2},{5,3},{6,0},{7,1},{8,14},{9,15},{10,... | collective-permute-start | bytes 196616 | tf_op jit(solution)/shard_map/ppermute | solution.py:594
  6.1 8.5 %collective-permute-start = (f32[128,128]{1,0:T(8,128)}, f32[128,128]{1,0:T(8,128)S(1)}, u32[]{:S(2)}, u32[]{:S(2)}) collective-permute-start(f32[128,128]{1,0:T(8,128)} %bitcast.10), channel_id=1, source_target_pairs={{0,1},{1,0},{2,3},{3,2},{4,5},{5,4},{6,7},{7,6},{8,9},{9,8},{10,11... | collective-permute-start | bytes 196616 | tf_op jit(solution)/shard_map/ppermute | solution.py:594
  7.6 7.0 %collective-permute-start.1 = (f32[128,128]{1,0:T(8,128)}, f32[128,128]{1,0:T(8,128)S(1)}, u32[]{:S(2)}, u32[]{:S(2)}) collective-permute-start(f32[128,128]{1,0:T(8,128)} %bitcast.11), channel_id=1, source_target_pairs={{0,2},{1,3},{2,0},{3,1},{4,6},{5,7},{6,4},{7,5},{8,10},{9,11},{10,... | collective-permute-start | bytes 196616 | tf_op jit(solution)/shard_map/ppermute | solution.py:594
  7.8 6.8 %collective-permute-start.2 = (f32[128,128]{1,0:T(8,128)}, f32[128,128]{1,0:T(8,128)S(1)}, u32[]{:S(2)}, u32[]{:S(2)}) collective-permute-start(f32[128,128]{1,0:T(8,128)} %bitcast.12), channel_id=1, source_target_pairs={{0,3},{1,2},{2,1},{3,0},{4,7},{5,6},{6,5},{7,4},{8,11},{9,10},{10,... | collective-permute-start | bytes 196616 | tf_op jit(solution)/shard_map/ppermute | solution.py:594
  9.6 5.1 %collective-permute-start.4 = (f32[128,128]{1,0:T(8,128)S(1)}, f32[128,128]{1,0:T(8,128)S(1)}, u32[]{:S(2)}, u32[]{:S(2)}) collective-permute-start(f32[128,128]{1,0:T(8,128)S(1)} %collective-permute-done.3.refs_2_.refs_4_), channel_id=1, source_target_pairs={{0,1},{1,0},{2,3},{3,2},{4,5},{5,4},{6,7},{7,6},{8,9},{9,8},{10,11... | collective-permute-start | bytes 196616 | tf_op jit(solution)/shard_map/ppermute | solution.py:594
  11.5 4.3 %collective-permute-start.6 = (f32[128,128]{1,0:T(8,128)S(1)}, f32[128,128]{1,0:T(8,128)S(1)}, u32[]{:S(2)}, u32[]{:S(2)}) collective-permute-start(f32[128,128]{1,0:T(8,128)S(1)} %collective-permute-done.5.refs_4_.refs_6_), channel_id=1, source_target_pairs={{0,1},{1,0},{2,3},{3,2},{4,5},{5,4},{6,7},{7,6},{8,9},{9,8},{10,11... | collective-permute-start | bytes 196616 | tf_op jit(solution)/shard_map/ppermute | solution.py:594
  22.6 3.6 %collective-permute-start.7 = (f32[16,128,128]{2,1,0:T(8,128)}, f32[16,128,128]{2,1,0:T(8,128)S(1)}, u32[]{:S(2)}, u32[]{:S(2)}) collective-permute-start(f32[16,128,128]{2,1,0:T(8,128)} %renew.1), channel_id=1, source_target_pairs={{0,8},{8,0},{1,9},{9,1},{2,10},{10,2},{3,11},{11,3},{4,12},{12,4},... | collective-permute-start | bytes 3145736 | tf_op jit(solution)/shard_map/ppermute | solution.py:607
  22.7 3.5 %copy-start = (f32[1,16,128,128]{3,2,1,0:T(8,128)S(1)}, f32[1,16,128,128]{3,2,1,0:T(8,128)}, u32[]{:S(2)}) copy-start(f32[1,16,128,128]{3,2,1,0:T(8,128)} %refs_11_.1) | copy-start | bytes 3145732
  29.5 5.1 %collective-permute-start.13 = (f32[136,128]{1,0:T(8,128)S(1)}, f32[136,128]{1,0:T(8,128)S(1)}, u32[]{:S(2)}, u32[]{:S(2)}) collective-permute-start(f32[136,128]{1,0:T(8,128)S(1)} %get-tuple-element.37), channel_id=1, source_target_pairs={{0,1},{1,0},{2,3},{3,2},{4,5},{5,4},{6,7},{7,6},{8,9},{9,8},{10,11... | collective-permute-start | bytes 208904 | tf_op jit(solution)/shard_map/ppermute | solution.py:594
  30.7 7.9 %collective-permute-start.11 = (f32[136,128]{1,0:T(8,128)S(1)}, f32[136,128]{1,0:T(8,128)S(1)}, u32[]{:S(2)}, u32[]{:S(2)}) collective-permute-start(f32[136,128]{1,0:T(8,128)S(1)} %get-tuple-element.35), channel_id=1, source_target_pairs={{0,1},{1,0},{2,3},{3,2},{4,5},{5,4},{6,7},{7,6},{8,9},{9,8},{10,11... | collective-permute-start | bytes 208904 | tf_op jit(solution)/shard_map/ppermute | solution.py:594
  31.5 7.2 %collective-permute-start.9 = (f32[136,128]{1,0:T(8,128)S(1)}, f32[136,128]{1,0:T(8,128)S(1)}, u32[]{:S(2)}, u32[]{:S(2)}) collective-permute-start(f32[136,128]{1,0:T(8,128)S(1)} %get-tuple-element.33), channel_id=1, source_target_pairs={{0,1},{1,0},{2,3},{3,2},{4,5},{5,4},{6,7},{7,6},{8,9},{9,8},{10,11... | collective-permute-start | bytes 208904 | tf_op jit(solution)/shard_map/ppermute | solution.py:594
  32.8 8.0 %collective-permute-start.8 = (f32[136,128]{1,0:T(8,128)S(1)}, f32[136,128]{1,0:T(8,128)S(1)}, u32[]{:S(2)}, u32[]{:S(2)}) collective-permute-start(f32[136,128]{1,0:T(8,128)S(1)} %get-tuple-element.31), channel_id=1, source_target_pairs={{0,1},{1,0},{2,3},{3,2},{4,5},{5,4},{6,7},{7,6},{8,9},{9,8},{10,11... | collective-permute-start | bytes 208904 | tf_op jit(solution)/shard_map/ppermute | solution.py:594
  34.5 7.1 %collective-permute-start.14 = (f32[136,128]{1,0:T(8,128)S(1)}, f32[136,128]{1,0:T(8,128)S(1)}, u32[]{:S(2)}, u32[]{:S(2)}) collective-permute-start(f32[136,128]{1,0:T(8,128)S(1)} %add.11), channel_id=1, source_target_pairs={{0,6},{1,7},{2,4},{3,5},{4,2},{5,3},{6,0},{7,1},{8,14},{9,15},{10,... | collective-permute-start | bytes 208904 | tf_op jit(solution)/shard_map/ppermute | solution.py:594
  38.6 5.5 %collective-permute-start.12 = (f32[136,128]{1,0:T(8,128)S(1)}, f32[136,128]{1,0:T(8,128)S(1)}, u32[]{:S(2)}, u32[]{:S(2)}) collective-permute-start(f32[136,128]{1,0:T(8,128)S(1)} %add.10), channel_id=1, source_target_pairs={{0,4},{1,5},{2,6},{3,7},{4,0},{5,1},{6,2},{7,3},{8,12},{9,13},{10,... | collective-permute-start | bytes 208904 | tf_op jit(solution)/shard_map/ppermute | solution.py:594
  38.7 5.9 %collective-permute-start.10 = (f32[136,128]{1,0:T(8,128)S(1)}, f32[136,128]{1,0:T(8,128)S(1)}, u32[]{:S(2)}, u32[]{:S(2)}) collective-permute-start(f32[136,128]{1,0:T(8,128)S(1)} %add.9), channel_id=1, source_target_pairs={{0,2},{1,3},{2,0},{3,1},{4,6},{5,7},{6,4},{7,5},{8,10},{9,11},{10,... | collective-permute-start | bytes 208904 | tf_op jit(solution)/shard_map/ppermute | solution.py:594

commit v4 on v3

--- a/solution.py
+++ b/solution.py
@@ -8,7 +8,7 @@
 from jax.sharding import PartitionSpec as P
 
 MAXT = 24
-ORDER = (0, 1, 4, 2, 6, 5, 3, 7)
+ORDER = (0, 7, 6, 5, 4, 1, 2, 3)
 F32 = jnp.float32
 BF16 = jnp.bfloat16
 VMEM = pl.BlockSpec(memory_space=pltpu.VMEM)
@@ -248,11 +248,39 @@
     return floats[0, g] * blocks[ints[0, g]] + floats[1, g] * blocks[ints[1, g]]
 
 
+def stack_halves(tile, stacked, k):
+    w = tile.shape[0]
+    at = slice(k * w, (k + 1) * w)
+    head, tail = heads_tails(tile[...])
+    stacked[0:w, at] = head
+    stacked[w : 2 * w, at] = head
+    stacked[2 * w : 3 * w, at] = tail
+    stacked[3 * w : 4 * w, at] = tail
+
+
+def multiply_blocks(lefts, stacked, entries, n, first):
+    w = lefts.shape[1] // 2
+    count = stacked.shape[1] // w
+    group = lefts.shape[0] // w // 2
+
+    def multiply(g, unused):
+        own = lefts[pl.ds(pl.multiple_of(g * (group * w), group * w), group * w)]
+        found = product(jnp.concatenate([own, own], axis=1), stacked[...])
+        for h in range(group):
+            for k in range(count):
+                entries[(g * group + h) * n + first + k] = found[
+                    h * w : (h + 1) * w, k * w : (k + 1) * w
+                ]
+        return unused
+
+    lax.fori_loop(0, 2, multiply, 0, unroll=2)
+
+
 def prepare_kernel(n, *refs):
-    psi, given, refs = refs[0], refs[1:13], refs[13:]
-    lefts, rights, up_ints, up_floats, mv_ints, mv_floats, own = refs[:7]
-    held = refs[7:19]
-    arrived, own_arrived = refs[19:]
+    psi, given, near, refs = refs[0], refs[1:13], refs[13 : 12 + n // 2], refs[12 + n // 2 :]
+    lefts, rights, up_ints, up_floats, mv_ints, mv_floats, own, entries = refs[:8]
+    held = refs[8:20]
+    bottoms, arrived, own_arrived = refs[20:]
     own_copy = pltpu.make_async_copy(psi.at[0, 0], own, own_arrived)
     own_copy.start()
     copies = [
@@ -299,9 +327,12 @@
 
     lax.fori_loop(0, channels, halve_right, 0, unroll=2)
     own_copy.wait()
-
-
-def prepare_call(n, psi, given):
+    for k, tile in enumerate((own, *near)):
+        stack_halves(tile, bottoms, k)
+    multiply_blocks(lefts, bottoms, entries, n, 0)
+
+
+def prepare_call(n, psi, given, near):
     channels, w = given[-1].shape[1], given[-1].shape[2]
     live = given[1].shape[2]
     table = (8, live)
@@ -315,21 +346,23 @@
             jax.ShapeDtypeStruct(table, jnp.int32),
             jax.ShapeDtypeStruct(table, F32),
             jax.ShapeDtypeStruct((w, w), F32),
+            pltpu.VMEM((2 * w + 1, w, w), F32),
         ),
-        in_specs=[HBM] * (len(given) + 1),
-        out_specs=(VMEM,) * 7,
+        in_specs=[HBM] * (len(given) + 1) + [VMEM] * len(near),
+        out_specs=(VMEM,) * 8,
         scratch_shapes=[
             *(
                 pltpu.SMEM(x.shape, x.dtype) if x.shape[-1] in (channels, n) else pltpu.VMEM(x.shape, x.dtype)
                 for x in given
             ),
+            pltpu.VMEM((4 * w, n // 2 * w), BF16),
             pltpu.SemaphoreType.DMA((len(given),)),
             pltpu.SemaphoreType.DMA,
         ],
-        compiler_params=pltpu.CompilerParams(vmem_limit_bytes=12 << 20),
+        compiler_params=pltpu.CompilerParams(vmem_limit_bytes=16 << 20),
         cost_estimate=pl.CostEstimate(flops=10**9, bytes_accessed=6 << 20, transcendentals=0),
         name="prepare",
-    )(*(pltpu.with_memory_space_constraint(x, pltpu.HBM) for x in (psi, *given)))
+    )(*(pltpu.with_memory_space_constraint(x, pltpu.HBM) for x in (psi, *given)), *near)
 
 
 def fetch_tables(sources, targets, arrived):
@@ -344,31 +377,17 @@
 
 def renew_kernel(n, *refs):
     tiles = [refs[ORDER.index(k)] for k in range(n)]
-    lefts, int_table, float_table, out, bottoms, tops, entries, renewed, ints, floats, arrived, left = refs[n:]
-    channels, w = out.shape[0], out.shape[1]
+    lefts, int_table, float_table, _, renewed, entries, bottoms, tops, ints, floats, arrived = refs[n:]
+    channels, w = renewed.shape[0], renewed.shape[1]
     copies = fetch_tables((int_table, float_table), (ints, floats), arrived)
+    for k in range(n // 2):
+        stack_halves(tiles[n // 2 + k], bottoms, k)
+    multiply_blocks(lefts, bottoms, entries, n, n // 2)
     for k in range(n):
         at = slice(k * w, (k + 1) * w)
-        value = tiles[k][...]
-        head, tail = heads_tails(value)
-        bottoms[0:w, at] = head
-        bottoms[w : 2 * w, at] = head
-        bottoms[2 * w : 3 * w, at] = tail
-        bottoms[3 * w : 4 * w, at] = tail
-        head, tail = heads_tails(value.T)
+        head, tail = heads_tails(tiles[k][...].T)
         tops[0:w, at] = head
         tops[w : 2 * w, at] = tail
-    group = channels // 2
-
-    def multiply(g, unused):
-        own = lefts[pl.ds(pl.multiple_of(g * (group * w), group * w), group * w)]
-        found = product(jnp.concatenate([own, own], axis=1), bottoms[...])
-        for h in range(group):
-            for k in range(n):
-                entries[(g * group + h) * n + k] = found[h * w : (h + 1) * w, k * w : (k + 1) * w]
-        return unused
-
-    lax.fori_loop(0, 2, multiply, 0, unroll=2)
     for copy in copies:
         copy.wait()
     spill(ints, floats, entries)
@@ -384,39 +403,40 @@
             b = 2 * g + i
             found = product(tops[0:w], jnp.concatenate([heads[i], tails[i]], axis=1))
             renewed[b] = found[:, :w] + (found[:, w:] + small[:, i * w : (i + 1) * w])
-            pltpu.make_async_copy(renewed.at[b], out.at[b], left.at[b]).start()
         return unused
 
     lax.fori_loop(0, channels // 2, finish, 0, unroll=4)
-    for b in range(channels):
-        pltpu.make_async_copy(renewed.at[b], out.at[b], left.at[b]).wait()
-
-
-def renew_call(tiles, lefts, int_table, float_table, channels):
+
+
+def renew_call(tiles, lefts, int_table, float_table, entries, channels):
     n, w = len(tiles), tiles[0].shape[0]
     return pl.pallas_call(
         functools.partial(renew_kernel, n),
-        out_shape=jax.ShapeDtypeStruct((channels, w, w), F32),
-        in_specs=[VMEM] * (n + 1) + [ANY] * 2,
-        out_specs=HBM,
+        out_shape=(pltpu.VMEM((channels, w, w), F32), pltpu.VMEM(entries.shape, F32)),
+        in_specs=[VMEM] * (n + 1) + [ANY] * 2 + [VMEM],
+        out_specs=(VMEM, VMEM),
+        input_output_aliases={n + 3: 1},
         scratch_shapes=[
-            pltpu.VMEM((4 * w, n * w), BF16),
+            pltpu.VMEM((4 * w, n // 2 * w), BF16),
             pltpu.VMEM((2 * w, n * w), BF16),
-            pltpu.VMEM((2 * w + 1, w, w), F32),
-            pltpu.VMEM((channels, w, w), F32),
             pltpu.SMEM(int_table.shape, jnp.int32),
             pltpu.SMEM(float_table.shape, F32),
             pltpu.SemaphoreType.DMA((2,)),
-            pltpu.SemaphoreType.DMA((channels,)),
         ],
-        compiler_params=pltpu.CompilerParams(vmem_limit_bytes=28 << 20),
+        compiler_params=pltpu.CompilerParams(vmem_limit_bytes=12 << 20),
         cost_estimate=pl.CostEstimate(flops=10**10, bytes_accessed=3 << 20, transcendentals=0),
         name="renew",
-    )(*(tiles[k] for k in ORDER), lefts, int_table, float_table)
+    )(
+        *(tiles[k] for k in ORDER),
+        lefts,
+        int_table,
+        float_table,
+        pltpu.with_memory_space_constraint(entries, pltpu.VMEM),
+    )[0]
 
 
 def source_kernel(n, *refs):
-    tiles = refs[:n]
+    tiles = [refs[ORDER.index(k)] for k in range(n)]
     rights, int_table, float_table, entries, stats, sources, ints, floats, arrived = refs[n:]
     channels, w = rights.shape[0], rights.shape[2]
     copies = fetch_tables((int_table, float_table), (ints, floats), arrived)
@@ -475,11 +495,11 @@
         compiler_params=pltpu.CompilerParams(vmem_limit_bytes=12 << 20),
         cost_estimate=pl.CostEstimate(flops=10**10, bytes_accessed=10 << 20, transcendentals=0),
         name="sources",
-    )(*tiles, rights, int_table, float_table)
+    )(*(tiles[k] for k in ORDER), rights, int_table, float_table)
 
 
 def apply_kernel(n, *refs):
-    tiles = refs[:n]
+    tiles = [refs[ORDER.index(k)] for k in range(n)]
     own, received, entries, int_table, float_table = refs[n : n + 5]
     outs = refs[n + 5 : 2 * n + 5]
     lefts, ints, floats, arrived = refs[2 * n + 5 :]
@@ -539,7 +559,7 @@
         cost_estimate=pl.CostEstimate(flops=5 * 10**9, bytes_accessed=10 << 20, transcendentals=0),
         name="applied",
     )(
-        *tiles,
+        *(tiles[k] for k in ORDER),
         own,
         received,
         pltpu.with_memory_space_constraint(entries, pltpu.VMEM),
@@ -594,23 +614,27 @@
         return lax.ppermute(value, "tile", [(i, i ^ k) for i in range(n)])
 
     own = psi[0, 0]
-    tiles = {k: across(own, k) for k in (1, 2, 3, 4, 6)}
-    tiles[5], tiles[7] = across(tiles[4], 1), across(tiles[6], 1)
+    half = n // 2
+    tiles = {k: across(own, k) for k in range(1, half + 1)}
+    for k in range(1, half):
+        tiles[half + k] = across(tiles[half], k)
 
     given = [up_counts, up_block, up_top, up_bot, up_coef, mv_counts, mv_src, mv_dst, mv_coef, site_energy]
-    lefts, rights, up_ints, up_floats, mv_ints, mv_floats, own = prepare_call(
-        n, psi, [*given, left_env, right_env]
+    lefts, rights, up_ints, up_floats, mv_ints, mv_floats, own, products = prepare_call(
+        n, psi, [*given, left_env, right_env], [tiles[k] for k in range(1, half)]
     )
     tiles[0] = own
     tiles = [tiles[k] for k in range(n)]
-    renewal = renew_call(tiles, lefts, up_ints, up_floats, left_env.shape[1])
+    renewal = renew_call(tiles, lefts, up_ints, up_floats, products, left_env.shape[1])
     received = lax.ppermute(renewal, "seg", [(0, 1), (1, 0)])
     entries, stats = source_call(tiles, rights, mv_ints, mv_floats)
     partials = apply_call(tiles, left_env[0], received, entries, mv_ints, mv_floats)
 
-    parts = [partials[0], across(partials[1], 1)]
-    for k in (2, 4, 6):
-        parts.append(across(partials[k] + across(partials[k + 1], 1), k))
+    far = partials[half]
+    for k in range(half - 1, 0, -1):
+        far = far + across(partials[half + k], k)
+    far = across(far, half)
+    parts = [partials[0], *(across(partials[k], k) for k in range(half - 1, 0, -1)), far]
     residual, quotient = finish_call(parts, own, stats)
     return (residual[None, None], renewal[None], quotient[0, :1])
 

time: 45.4 us -> 43.7 us (0.963)
  waiting for transfers between devices: 6.14 us -> 3.52 us
  local copies, waits for them, and re-layouts: 0.01 us -> 0.98 us
    ppermute x14, waiting for transfers between devices: 6.14 us -> 3.52 us  [across(): return lax.ppermute(value, 'tile', [(i, i ^ k) for i in range(n)])]
    pallas_call x1, Pallas kernels: 6.85 us -> 5.42 us  [renew_call(): pl.pallas_call(functools.partial(renew_kernel, n), out_shape=(pltpu.VMEM(...]
    pallas_call x1, Pallas kernels: 1.96 us -> 3.27 us  [prepare_call(): pl.pallas_call(functools.partial(prepare_kernel, n), out_shape=(jax.Shape...]
    unnamed x2 -> x3, local copies, waits for them, and re-layouts: 0.01 us -> 0.98 us
  transfers between devices with their start and end apart: 15 -> 15, of which waited for: 6 -> 3; matrix products, arithmetic and copies ran while one was open for 0% -> 2% of each run, Pallas kernels for 12% -> 16%
where the time goes in v4:
time: 43.7 us; the launch traced here: 43.6 us
  starting transfers between devices  22 us (50%)
  Pallas kernels  16.3 us (37%)
  waiting for transfers between devices  3.52 us (8%)
  local copies, waits for them, and re-layouts  0.98 us (2%)
  between operations  0.73 us (2%)
    ppermute x14, starting transfers between devices, across(): return lax.ppermute(value, 'tile', [(i, i ^ k) for i in range(n)])  22 us
    pallas_call x1, Pallas kernels, renew_call(): pl.pallas_call(functools.partial(renew_kernel, n), out_shape=(pltpu.VMEM(...  5.42 us
    pallas_call x1, Pallas kernels, source_call(): pl.pallas_call(functools.partial(source_kernel, n), out_shape=(pltpu.VMEM...  3.59 us
    ppermute x14, waiting for transfers between devices, across(): return lax.ppermute(value, 'tile', [(i, i ^ k) for i in range(n)])  3.52 us
    pallas_call x1, Pallas kernels, prepare_call(): pl.pallas_call(functools.partial(prepare_kernel, n), out_shape=(jax.Shape...  3.27 us
    pallas_call x1, Pallas kernels, apply_call(): pl.pallas_call(functools.partial(apply_kernel, n), out_shape=tuple((jax.S...  3.22 us
    unnamed x3, local copies, waits for them, and re-layouts  0.98 us
  transfers between devices with their start and end apart: 15, of which 3 were waited for; matrix products, arithmetic and copies ran while one was open for 2% of the time, Pallas kernels for 16%

profile of v4, /device:TPU:0, one launch (start us, length us, event | category | flops | bytes accessed | tf_op | source)
XLA Modules:
  0.0 43.6 jit_solution(11504458337453795473)
XLA Ops:
  0.6 4.1 %collective-permute-start.3 = (f32[128,128]{1,0:T(8,128)}, f32[128,128]{1,0:T(8,128)S(1)}, u32[]{:S(2)}, u32[]{:S(2)}) collective-permute-start(f32[128,128]{1,0:T(8,128)} %bitcast.8), channel_id=1, source_target_pairs={{0,4},{1,5},{2,6},{3,7},{4,0},{5,1},{6,2},{7,3},{8,12},{9,13},{10,... | collective-permute-start | bytes 196616 | tf_op jit(solution)/shard_map/ppermute | solution.py:614
  4.7 2.5 %collective-permute-start.2 = (f32[128,128]{1,0:T(8,128)}, f32[128,128]{1,0:T(8,128)S(1)}, u32[]{:S(2)}, u32[]{:S(2)}) collective-permute-start(f32[128,128]{1,0:T(8,128)} %bitcast.9), channel_id=1, source_target_pairs={{0,3},{1,2},{2,1},{3,0},{4,7},{5,6},{6,5},{7,4},{8,11},{9,10},{10,... | collective-permute-start | bytes 196616 | tf_op jit(solution)/shard_map/ppermute | solution.py:614
  7.3 0.4 %collective-permute-start.1 = (f32[128,128]{1,0:T(8,128)}, f32[128,128]{1,0:T(8,128)S(1)}, u32[]{:S(2)}, u32[]{:S(2)}) collective-permute-start(f32[128,128]{1,0:T(8,128)} %bitcast.10), channel_id=1, source_target_pairs={{0,2},{1,3},{2,0},{3,1},{4,6},{5,7},{6,4},{7,5},{8,10},{9,11},{10,... | collective-permute-start | bytes 196616 | tf_op jit(solution)/shard_map/ppermute | solution.py:614
  7.7 0.5 %collective-permute-start = (f32[128,128]{1,0:T(8,128)}, f32[128,128]{1,0:T(8,128)S(1)}, u32[]{:S(2)}, u32[]{:S(2)}) collective-permute-start(f32[128,128]{1,0:T(8,128)} %bitcast.11), channel_id=1, source_target_pairs={{0,1},{1,0},{2,3},{3,2},{4,5},{5,4},{6,7},{7,6},{8,9},{9,8},{10,11... | collective-permute-start | bytes 196616 | tf_op jit(solution)/shard_map/ppermute | solution.py:614
  8.2 0.0 collective-permute-done.3.refs_4_
  8.2 1.6 %collective-permute-start.6 = (f32[128,128]{1,0:T(8,128)S(1)}, f32[128,128]{1,0:T(8,128)S(1)}, u32[]{:S(2)}, u32[]{:S(2)}) collective-permute-start(f32[128,128]{1,0:T(8,128)S(1)} %collective-permute-done.3.refs_4_), channel_id=1, source_target_pairs={{0,1},{1,0},{2,3},{3,2},{4,5},{5,4},{6,7},{7,6},{8,9},{9,8},{10,11... | collective-permute-start | bytes 196616 | tf_op jit(solution)/shard_map/ppermute | solution.py:614
  9.9 1.5 %collective-permute-start.5 = (f32[128,128]{1,0:T(8,128)S(1)}, f32[128,128]{1,0:T(8,128)S(1)}, u32[]{:S(2)}, u32[]{:S(2)}) collective-permute-start(f32[128,128]{1,0:T(8,128)S(1)} %collective-permute-done.3.refs_4_), channel_id=1, source_target_pairs={{0,2},{1,3},{2,0},{3,1},{4,6},{5,7},{6,4},{7,5},{8,10},{9,11},{10,... | collective-permute-start | bytes 196616 | tf_op jit(solution)/shard_map/ppermute | solution.py:614
  11.3 0.0 collective-permute-done.2.refs_15_.refs_7_
  11.3 1.4 %collective-permute-start.4 = (f32[128,128]{1,0:T(8,128)S(1)}, f32[128,128]{1,0:T(8,128)S(1)}, u32[]{:S(2)}, u32[]{:S(2)}) collective-permute-start(f32[128,128]{1,0:T(8,128)S(1)} %collective-permute-done.3.refs_4_), channel_id=1, source_target_pairs={{0,3},{1,2},{2,1},{3,0},{4,7},{5,6},{6,5},{7,4},{8,11},{9,10},{10,... | collective-permute-start | bytes 196616 | tf_op jit(solution)/shard_map/ppermute | solution.py:614
  12.7 0.0 collective-permute-done.1.refs_14_.refs_6_
  12.7 0.0 collective-permute-done.refs_13_.refs_5_
  12.7 3.3 %prepare.1 = (bf16[2048,256]{1,0:T(8,128)(2,1)S(1)}, bf16[16,256,128]{2,1,0:T(8,128)(2,1)S(1)}, s32[8,192]{1,0:T(8,128)S(1)}, f32[8,192]{1,0:T(8,128)S(1)}, s32[...) custom-call(f32[1,1,128,128]{3,2,1,0:T(8,128)} %refs_0_.1, ...), custom_call_target="tpu_custom_call" | custom-call | flops 1000000000 | bytes 6291456 | tf_op jit(solution)/shard_map/prepare/pallas_call | solution.py:339
  16.0 0.0 collective-permute-done.6.refs_3_
  16.0 0.0 collective-permute-done.5.refs_2_
  16.0 0.5 %collective-permute-done.4.refs_1_ = f32[128,128]{1,0:T(8,128)S(1)} collective-permute-done((f32[128,128]{1,0:T(8,128)S(1)}, f32[128,128]{1,0:T(8,128)S(1)}, u32[]{:S(2)}, u32[]{:S(2)}) %collective-permute-start.4) | collective-permute-done | bytes 65568 | tf_op jit(solution)/shard_map/ppermute | solution.py:614
  16.5 5.4 %renew.1 = (f32[16,128,128]{2,1,0:T(8,128)S(1)}, f32[257,128,128]{2,1,0:T(8,128)S(1)}) custom-call(f32[128,128]{1,0:T(8,128)S(1)} %get-tuple-element.24.refs_0_.refs_5_, f32[128,128]{1,0:T(8,128)S(1)} %collective-permute-done.4.refs_1_, f32[128,128]{1,0:T(8,128)S(1)} %collective-permute-done.5.refs_2_, ...), custom_call_target="tpu_custom_call", output_to_operand_aliasing={{1}: (11, {})} | custom-call | flops 10000000000 | bytes 3145728 | tf_op jit(solution)/shard_map/renew/pallas_call | solution.py:413
  21.9 0.1 collective-permute-start.7
  22.0 0.0 copy-start
  22.0 3.6 %sources.1 = (f32[257,128,128]{2,1,0:T(8,128)S(1)}, f32[24,128]{1,0:T(8,128)S(1)}) custom-call(f32[128,128]{1,0:T(8,128)S(1)} %get-tuple-element.24.refs_0_.refs_5_, f32[128,128]{1,0:T(8,128)S(1)} %collective-permute-done.4.refs_1_, f32[128,128]{1,0:T(8,128)S(1)} %collective-permute-done.5.refs_2_, f32[128,128]{1,0:T(8,128)S(1)} %collective-permute-done.6.refs_3_, ...), custom_call_target="tpu_custom_call" | custom-call | flops 10000000000 | bytes 10485760 | tf_op jit(solution)/shard_map/sources/pallas_call | solution.py:481
  25.6 0.0 collective-permute-done.7.refs_9_
  25.6 0.0 copy-done
  25.6 3.2 %applied.1 = (f32[136,128]{1,0:T(8,128)S(1)}, f32[136,128]{1,0:T(8,128)S(1)}, f32[136,128]{1,0:T(8,128)S(1)}, f32[136,128]{1,0:T(8,128)S(1)}, f32[136,128]{1,0:T...) custom-call(f32[128,128]{1,0:T(8,128)S(1)} %get-tuple-element.24.refs_0_.refs_5_, ...), custom_call_target="tpu_custom_call" | custom-call | flops 5000000000 | bytes 10485760 | tf_op jit(solution)/shard_map/applied/pallas_call | solution.py:547
  28.9 1.4 %collective-permute-start.11 = (f32[136,128]{1,0:T(8,128)S(1)}, f32[136,128]{1,0:T(8,128)S(1)}, u32[]{:S(2)}, u32[]{:S(2)}) collective-permute-start(f32[136,128]{1,0:T(8,128)S(1)} %get-tuple-element.39), channel_id=1, source_target_pairs={{0,3},{1,2},{2,1},{3,0},{4,7},{5,6},{6,5},{7,4},{8,11},{9,10},{10,... | collective-permute-start | bytes 208904 | tf_op jit(solution)/shard_map/ppermute | solution.py:614
  30.2 1.3 %collective-permute-start.12 = (f32[136,128]{1,0:T(8,128)S(1)}, f32[136,128]{1,0:T(8,128)S(1)}, u32[]{:S(2)}, u32[]{:S(2)}) collective-permute-start(f32[136,128]{1,0:T(8,128)S(1)} %get-tuple-element.40), channel_id=1, source_target_pairs={{0,2},{1,3},{2,0},{3,1},{4,6},{5,7},{6,4},{7,5},{8,10},{9,11},{10,... | collective-permute-start | bytes 208904 | tf_op jit(solution)/shard_map/ppermute | solution.py:614
  31.6 0.9 %collective-permute-start.13 = (f32[136,128]{1,0:T(8,128)S(1)}, f32[136,128]{1,0:T(8,128)S(1)}, u32[]{:S(2)}, u32[]{:S(2)}) collective-permute-start(f32[136,128]{1,0:T(8,128)S(1)} %get-tuple-element.41), channel_id=1, source_target_pairs={{0,1},{1,0},{2,3},{3,2},{4,5},{5,4},{6,7},{7,6},{8,9},{9,8},{10,11... | collective-permute-start | bytes 208904 | tf_op jit(solution)/shard_map/ppermute | solution.py:614
  32.4 1.3 %collective-permute-start.8 = (f32[136,128]{1,0:T(8,128)S(1)}, f32[136,128]{1,0:T(8,128)S(1)}, u32[]{:S(2)}, u32[]{:S(2)}) collective-permute-start(f32[136,128]{1,0:T(8,128)S(1)} %get-tuple-element.35), channel_id=1, source_target_pairs={{0,3},{1,2},{2,1},{3,0},{4,7},{5,6},{6,5},{7,4},{8,11},{9,10},{10,... | collective-permute-start | bytes 208904 | tf_op jit(solution)/shard_map/ppermute | solution.py:614
  33.7 1.3 %collective-permute-start.9 = (f32[136,128]{1,0:T(8,128)S(1)}, f32[136,128]{1,0:T(8,128)S(1)}, u32[]{:S(2)}, u32[]{:S(2)}) collective-permute-start(f32[136,128]{1,0:T(8,128)S(1)} %get-tuple-element.36), channel_id=1, source_target_pairs={{0,2},{1,3},{2,0},{3,1},{4,6},{5,7},{6,4},{7,5},{8,10},{9,11},{10,... | collective-permute-start | bytes 208904 | tf_op jit(solution)/shard_map/ppermute | solution.py:614
  35.0 0.0 collective-permute-done.11
  35.0 0.9 %collective-permute-start.10 = (f32[136,128]{1,0:T(8,128)S(1)}, f32[136,128]{1,0:T(8,128)S(1)}, u32[]{:S(2)}, u32[]{:S(2)}) collective-permute-start(f32[136,128]{1,0:T(8,128)S(1)} %get-tuple-element.37), channel_id=1, source_target_pairs={{0,1},{1,0},{2,3},{3,2},{4,5},{5,4},{6,7},{7,6},{8,9},{9,8},{10,11... | collective-permute-start | bytes 208904 | tf_op jit(solution)/shard_map/ppermute | solution.py:614
  36.0 0.0 collective-permute-done.12
  36.0 0.4 collective-permute-done.13
  36.4 2.8 %collective-permute-start.14 = (f32[136,128]{1,0:T(8,128)S(1)}, f32[136,128]{1,0:T(8,128)S(1)}, u32[]{:S(2)}, u32[]{:S(2)}) collective-permute-start(f32[136,128]{1,0:T(8,128)S(1)} %add_add_fusion), channel_id=1, source_target_pairs={{0,4},{1,5},{2,6},{3,7},{4,0},{5,1},{6,2},{7,3},{8,12},{9,13},{10,... | collective-permute-start | bytes 208904 | tf_op jit(solution)/shard_map/ppermute | solution.py:614
  39.2 1.0 %copy.18 = f32[1,16,128,128]{3,2,1,0:T(8,128)} copy(f32[1,16,128,128]{3,2,1,0:T(8,128)S(1)} %bitcast.6) | data formatting | bytes 2097152
  40.2 0.0 collective-permute-done.8.refs_1_
  40.2 0.0 collective-permute-done.9.refs_2_
  40.2 0.0 collective-permute-done.10.refs_3_
  40.2 2.6 %collective-permute-done.14.refs_4_ = f32[136,128]{1,0:T(8,128)S(1)} collective-permute-done((f32[136,128]{1,0:T(8,128)S(1)}, f32[136,128]{1,0:T(8,128)S(1)}, u32[]{:S(2)}, u32[]{:S(2)}) %collective-permute-start.14) | collective-permute-done | bytes 69664 | tf_op jit(solution)/shard_map/ppermute | solution.py:614
  42.8 0.8 %finish.1 = (f32[128,128]{1,0:T(8,128)}, f32[1,128]{1,0:T(1,128)}) custom-call(f32[136,128]{1,0:T(8,128)S(1)} %get-tuple-element.34.refs_0_, f32[136,128]{1,0:T(8,128)S(1)} %collective-permute-done.8.refs_1_, f32[136,128]{1,0:T(8,128)S(1)} %collective-permute-done.9.refs_2_, f32[136,128]{1,0:T(8,128)S(1)} %collective-permute-done.10.refs_3_, ...), custom_call_target="tpu_custom_call" | custom-call | tf_op jit(solution)/shard_map/finish/pallas_call | solution.py:587
  (1 shorter events, 0.0 us)
Async XLA Ops:
  0.6 7.6 %collective-permute-start.3 = (f32[128,128]{1,0:T(8,128)}, f32[128,128]{1,0:T(8,128)S(1)}, u32[]{:S(2)}, u32[]{:S(2)}) collective-permute-start(f32[128,128]{1,0:T(8,128)} %bitcast.8), channel_id=1, source_target_pairs={{0,4},{1,5},{2,6},{3,7},{4,0},{5,1},{6,2},{7,3},{8,12},{9,13},{10,... | collective-permute-start | bytes 196616 | tf_op jit(solution)/shard_map/ppermute | solution.py:614
  4.7 6.6 %collective-permute-start.2 = (f32[128,128]{1,0:T(8,128)}, f32[128,128]{1,0:T(8,128)S(1)}, u32[]{:S(2)}, u32[]{:S(2)}) collective-permute-start(f32[128,128]{1,0:T(8,128)} %bitcast.9), channel_id=1, source_target_pairs={{0,3},{1,2},{2,1},{3,0},{4,7},{5,6},{6,5},{7,4},{8,11},{9,10},{10,... | collective-permute-start | bytes 196616 | tf_op jit(solution)/shard_map/ppermute | solution.py:614
  7.3 5.4 %collective-permute-start.1 = (f32[128,128]{1,0:T(8,128)}, f32[128,128]{1,0:T(8,128)S(1)}, u32[]{:S(2)}, u32[]{:S(2)}) collective-permute-start(f32[128,128]{1,0:T(8,128)} %bitcast.10), channel_id=1, source_target_pairs={{0,2},{1,3},{2,0},{3,1},{4,6},{5,7},{6,4},{7,5},{8,10},{9,11},{10,... | collective-permute-start | bytes 196616 | tf_op jit(solution)/shard_map/ppermute | solution.py:614
  7.7 5.0 %collective-permute-start = (f32[128,128]{1,0:T(8,128)}, f32[128,128]{1,0:T(8,128)S(1)}, u32[]{:S(2)}, u32[]{:S(2)}) collective-permute-start(f32[128,128]{1,0:T(8,128)} %bitcast.11), channel_id=1, source_target_pairs={{0,1},{1,0},{2,3},{3,2},{4,5},{5,4},{6,7},{7,6},{8,9},{9,8},{10,11... | collective-permute-start | bytes 196616 | tf_op jit(solution)/shard_map/ppermute | solution.py:614
  8.2 7.8 %collective-permute-start.6 = (f32[128,128]{1,0:T(8,128)S(1)}, f32[128,128]{1,0:T(8,128)S(1)}, u32[]{:S(2)}, u32[]{:S(2)}) collective-permute-start(f32[128,128]{1,0:T(8,128)S(1)} %collective-permute-done.3.refs_4_), channel_id=1, source_target_pairs={{0,1},{1,0},{2,3},{3,2},{4,5},{5,4},{6,7},{7,6},{8,9},{9,8},{10,11... | collective-permute-start | bytes 196616 | tf_op jit(solution)/shard_map/ppermute | solution.py:614
  9.9 6.1 %collective-permute-start.5 = (f32[128,128]{1,0:T(8,128)S(1)}, f32[128,128]{1,0:T(8,128)S(1)}, u32[]{:S(2)}, u32[]{:S(2)}) collective-permute-start(f32[128,128]{1,0:T(8,128)S(1)} %collective-permute-done.3.refs_4_), channel_id=1, source_target_pairs={{0,2},{1,3},{2,0},{3,1},{4,6},{5,7},{6,4},{7,5},{8,10},{9,11},{10,... | collective-permute-start | bytes 196616 | tf_op jit(solution)/shard_map/ppermute | solution.py:614
  11.3 5.2 %collective-permute-start.4 = (f32[128,128]{1,0:T(8,128)S(1)}, f32[128,128]{1,0:T(8,128)S(1)}, u32[]{:S(2)}, u32[]{:S(2)}) collective-permute-start(f32[128,128]{1,0:T(8,128)S(1)} %collective-permute-done.3.refs_4_), channel_id=1, source_target_pairs={{0,3},{1,2},{2,1},{3,0},{4,7},{5,6},{6,5},{7,4},{8,11},{9,10},{10,... | collective-permute-start | bytes 196616 | tf_op jit(solution)/shard_map/ppermute | solution.py:614
  21.9 3.7 %collective-permute-start.7 = (f32[16,128,128]{2,1,0:T(8,128)S(1)}, f32[16,128,128]{2,1,0:T(8,128)S(1)}, u32[]{:S(2)}, u32[]{:S(2)}) collective-permute-start(f32[16,128,128]{2,1,0:T(8,128)S(1)} %get-tuple-element.29), channel_id=1, source_target_pairs={{0,8},{8,0},{1,9},{9,1},{2,10},{10,2},{3,11},{11,3},{4,12},{12,4},... | collective-permute-start | bytes 3145736 | tf_op jit(solution)/shard_map/ppermute | solution.py:629
  22.0 3.6 %copy-start = (f32[1,16,128,128]{3,2,1,0:T(8,128)S(1)}, f32[1,16,128,128]{3,2,1,0:T(8,128)}, u32[]{:S(2)}) copy-start(f32[1,16,128,128]{3,2,1,0:T(8,128)} %refs_11_.1) | copy-start | bytes 3145732
  28.9 6.2 %collective-permute-start.11 = (f32[136,128]{1,0:T(8,128)S(1)}, f32[136,128]{1,0:T(8,128)S(1)}, u32[]{:S(2)}, u32[]{:S(2)}) collective-permute-start(f32[136,128]{1,0:T(8,128)S(1)} %get-tuple-element.39), channel_id=1, source_target_pairs={{0,3},{1,2},{2,1},{3,0},{4,7},{5,6},{6,5},{7,4},{8,11},{9,10},{10,... | collective-permute-start | bytes 208904 | tf_op jit(solution)/shard_map/ppermute | solution.py:614
  30.2 5.7 %collective-permute-start.12 = (f32[136,128]{1,0:T(8,128)S(1)}, f32[136,128]{1,0:T(8,128)S(1)}, u32[]{:S(2)}, u32[]{:S(2)}) collective-permute-start(f32[136,128]{1,0:T(8,128)S(1)} %get-tuple-element.40), channel_id=1, source_target_pairs={{0,2},{1,3},{2,0},{3,1},{4,6},{5,7},{6,4},{7,5},{8,10},{9,11},{10,... | collective-permute-start | bytes 208904 | tf_op jit(solution)/shard_map/ppermute | solution.py:614
  31.6 4.8 %collective-permute-start.13 = (f32[136,128]{1,0:T(8,128)S(1)}, f32[136,128]{1,0:T(8,128)S(1)}, u32[]{:S(2)}, u32[]{:S(2)}) collective-permute-start(f32[136,128]{1,0:T(8,128)S(1)} %get-tuple-element.41), channel_id=1, source_target_pairs={{0,1},{1,0},{2,3},{3,2},{4,5},{5,4},{6,7},{7,6},{8,9},{9,8},{10,11... | collective-permute-start | bytes 208904 | tf_op jit(solution)/shard_map/ppermute | solution.py:614
  32.4 7.7 %collective-permute-start.8 = (f32[136,128]{1,0:T(8,128)S(1)}, f32[136,128]{1,0:T(8,128)S(1)}, u32[]{:S(2)}, u32[]{:S(2)}) collective-permute-start(f32[136,128]{1,0:T(8,128)S(1)} %get-tuple-element.35), channel_id=1, source_target_pairs={{0,3},{1,2},{2,1},{3,0},{4,7},{5,6},{6,5},{7,4},{8,11},{9,10},{10,... | collective-permute-start | bytes 208904 | tf_op jit(solution)/shard_map/ppermute | solution.py:614
  33.7 6.4 %collective-permute-start.9 = (f32[136,128]{1,0:T(8,128)S(1)}, f32[136,128]{1,0:T(8,128)S(1)}, u32[]{:S(2)}, u32[]{:S(2)}) collective-permute-start(f32[136,128]{1,0:T(8,128)S(1)} %get-tuple-element.36), channel_id=1, source_target_pairs={{0,2},{1,3},{2,0},{3,1},{4,6},{5,7},{6,4},{7,5},{8,10},{9,11},{10,... | collective-permute-start | bytes 208904 | tf_op jit(solution)/shard_map/ppermute | solution.py:614
  35.0 5.1 %collective-permute-start.10 = (f32[136,128]{1,0:T(8,128)S(1)}, f32[136,128]{1,0:T(8,128)S(1)}, u32[]{:S(2)}, u32[]{:S(2)}) collective-permute-start(f32[136,128]{1,0:T(8,128)S(1)} %get-tuple-element.37), channel_id=1, source_target_pairs={{0,1},{1,0},{2,3},{3,2},{4,5},{5,4},{6,7},{7,6},{8,9},{9,8},{10,11... | collective-permute-start | bytes 208904 | tf_op jit(solution)/shard_map/ppermute | solution.py:614
  36.4 6.4 %collective-permute-start.14 = (f32[136,128]{1,0:T(8,128)S(1)}, f32[136,128]{1,0:T(8,128)S(1)}, u32[]{:S(2)}, u32[]{:S(2)}) collective-permute-start(f32[136,128]{1,0:T(8,128)S(1)} %add_add_fusion), channel_id=1, source_target_pairs={{0,4},{1,5},{2,6},{3,7},{4,0},{5,1},{6,2},{7,3},{8,12},{9,13},{10,... | collective-permute-start | bytes 208904 | tf_op jit(solution)/shard_map/ppermute | solution.py:614

commit v5 on v4

--- a/solution.py
+++ b/solution.py
@@ -211,37 +211,45 @@
     floats[0:1, 0:w] = first[1:2] + first[2:3] + first[3:4]
     floats[1:2, 0:w] = jnp.where(large, 1.0, second[1:2] + second[2:3] + second[3:4])
 
-    place = product(jnp.concatenate([spilled] * 8, axis=0).astype(BF16), earlier)[0:1]
+    twos = jnp.where(size > 2.0, jnp.floor(size * 0.5), 0.0)
+    column = lax.broadcasted_iota(jnp.int32, (w, w), 0)
+    lower = jnp.where(lax.broadcasted_iota(jnp.int32, (w, w), 1) < column, 1.0, 0.0).astype(BF16)
+    start = product(lower, jnp.broadcast_to(twos, (w, w)).astype(BF16))[:, 0:1]
+    count = jnp.sum(twos)
+    two = jnp.floor((rank - 1.0) * 0.5)
+    second = rank - 1.0 - 2.0 * two
+    place = jnp.sum(ones * start, axis=0, keepdims=True) + two
     place = jnp.where(spilled > 0.0, place, -1.0)
     column = lax.broadcasted_iota(jnp.int32, (live, live), 0).astype(F32)
-    chosen = jnp.where(place == column, 1.0, 0.0).astype(BF16)
-    again = jnp.where(rank > 1.0, 1.0, 0.0)
+    chosen = jnp.where(place == column, 1.0, 0.0)
+    again = jnp.where(two > 0.0, 1.0, 0.0)
     rows = jnp.concatenate(
         [sources, *parts, (group + w).astype(F32), again, zero, zero], axis=0
     )
-    listed = over_entries(rows, chosen)
-    ints[2:3] = listed[0:1].astype(jnp.int32)
-    count = jnp.sum(spilled)
     past = lax.broadcasted_iota(jnp.int32, (1, live), 1).astype(F32) >= count
-    ints[3:4] = jnp.where(past, 2 * w, listed[4:5].astype(jnp.int32))
-    ints[4:5] = jnp.full((1, live), count).astype(jnp.int32)
-    floats[2:3] = listed[1:2] + listed[2:3] + listed[3:4]
-    floats[3:4] = listed[5:6]
+    for i in range(2):
+        listed = over_entries(rows, (chosen * jnp.where(second == i, 1.0, 0.0)).astype(BF16))
+        ints[2 + i : 3 + i] = listed[0:1].astype(jnp.int32)
+        floats[2 + i : 3 + i] = listed[1:2] + listed[2:3] + listed[3:4]
+        if i == 0:
+            ints[4:5] = jnp.where(past, 2 * w, listed[4:5].astype(jnp.int32))
+            floats[5:6] = listed[5:6]
+    ints[5:6] = jnp.full((1, live), count).astype(jnp.int32)
 
 
 def spill(ints, floats, blocks):
-    def add(q, unused):
-        to = ints[3, q]
-        held = jnp.where(floats[3, q] > 0.0, blocks[to], 0.0)
-        blocks[to] = held + floats[2, q] * blocks[ints[2, q]]
-        return unused
+    def add(q):
+        to = ints[4, q]
+        held = jnp.where(floats[5, q] > 0.0, blocks[to], 0.0)
+        pair = floats[2, q] * blocks[ints[2, q]] + floats[3, q] * blocks[ints[3, q]]
+        blocks[to] = held + pair
 
     def four(q, unused):
         for i in range(4):
-            add(4 * q + i, unused)
+            add(4 * q + i)
         return unused
 
-    lax.fori_loop(0, lax.div(ints[4, 0] + 3, 4), four, 0)
+    lax.fori_loop(0, lax.div(ints[5, 0] + 3, 4), four, 0)
 
 
 def two_terms(ints, floats, blocks, g):
@@ -258,10 +266,10 @@
     stacked[3 * w : 4 * w, at] = tail
 
 
-def multiply_blocks(lefts, stacked, entries, n, first):
+def multiply_blocks(lefts, stacked, entries, n, first, parts=2):
     w = lefts.shape[1] // 2
     count = stacked.shape[1] // w
-    group = lefts.shape[0] // w // 2
+    group = lefts.shape[0] // w // parts
 
     def multiply(g, unused):
         own = lefts[pl.ds(pl.multiple_of(g * (group * w), group * w), group * w)]
@@ -273,29 +281,42 @@
                 ]
         return unused
 
-    lax.fori_loop(0, 2, multiply, 0, unroll=2)
+    lax.fori_loop(0, parts, multiply, 0, unroll=parts)
 
 
 def prepare_kernel(n, *refs):
-    psi, given, near, refs = refs[0], refs[1:13], refs[13 : 12 + n // 2], refs[12 + n // 2 :]
-    lefts, rights, up_ints, up_floats, mv_ints, mv_floats, own, entries = refs[:8]
-    held = refs[8:20]
-    bottoms, arrived, own_arrived = refs[20:]
-    own_copy = pltpu.make_async_copy(psi.at[0, 0], own, own_arrived)
-    own_copy.start()
+    psi, given, refs = refs[0], refs[1:13], refs[13:]
+    near, refs = refs[: n // 2 - 1], refs[n // 2 - 1 :]
+    lefts, rights, up_ints, up_floats, mv_ints, mv_floats, own, up_entries = refs[:8]
+    held, refs = refs[8:20], refs[20:]
+    bottoms, arrived, own_arrived, env_arrived = refs
+    left, right = held[10:]
+    channels, w = left.shape[1], left.shape[2]
+    pieces = env_arrived.shape[1]
+    deep = channels // pieces
+
+    def env_copy(i, q):
+        at = slice(q * deep, (q + 1) * deep)
+        return pltpu.make_async_copy(given[10 + i].at[0, at], held[10 + i].at[0, at], env_arrived.at[i, q])
+
     copies = [
         pltpu.make_async_copy(source, target, arrived.at[index])
-        for index, (source, target) in enumerate(zip(given, held))
+        for index, (source, target) in enumerate(zip(given[:10], held[:10]))
     ]
+    own_copy = pltpu.make_async_copy(psi.at[0, 0], own, own_arrived)
     for copy in copies:
         copy.start()
+    own_copy.start()
+    for i in range(2):
+        for q in range(pieces):
+            env_copy(i, q).start()
+    for k, tile in enumerate(near):
+        stack_halves(tile, bottoms, k + 1)
     up_counts, up_block, up_top, up_bot, up_coef = held[:5]
     mv_counts, mv_src, mv_dst, mv_coef, energies = held[5:10]
-    left, right = held[10:]
-    channels, w = left.shape[1], left.shape[2]
     live = up_block.shape[2]
     me = lax.axis_index("tile")
-    for copy in copies[:10]:
+    for copy in copies:
         copy.wait()
     channel = channel_row(up_counts, live, channels)
     plan_terms(
@@ -310,26 +331,19 @@
     for k in range(n):
         by_slot += jnp.where(at == k, energies[0, k ^ me], 0.0)
     mv_floats[4:5] = by_slot
-    copies[10].wait()
-
-    def halve_left(c, unused):
-        lefts[pl.ds(pl.multiple_of(c * w, w), w)] = side_by_side(left[0, c])
-        return unused
-
-    lax.fori_loop(0, channels, halve_left, 0, unroll=2)
-    copies[11].wait()
-
-    def halve_right(c, unused):
-        head, tail = heads_tails(right[0, c])
-        rights[c, 0:w] = head
-        rights[c, w : 2 * w] = tail
-        return unused
-
-    lax.fori_loop(0, channels, halve_right, 0, unroll=2)
     own_copy.wait()
-    for k, tile in enumerate((own, *near)):
-        stack_halves(tile, bottoms, k)
-    multiply_blocks(lefts, bottoms, entries, n, 0)
+    stack_halves(own, bottoms, 0)
+    for q in range(pieces):
+        env_copy(0, q).wait()
+        for c in range(q * deep, (q + 1) * deep):
+            lefts[c * w : (c + 1) * w] = side_by_side(left[0, c])
+    multiply_blocks(lefts, bottoms, up_entries, n, 0)
+    for q in range(pieces):
+        env_copy(1, q).wait()
+        for c in range(q * deep, (q + 1) * deep):
+            head, tail = heads_tails(right[0, c])
+            rights[c, 0:w] = head
+            rights[c, w : 2 * w] = tail
 
 
 def prepare_call(n, psi, given, near):
@@ -356,10 +370,11 @@
                 for x in given
             ),
             pltpu.VMEM((4 * w, n // 2 * w), BF16),
-            pltpu.SemaphoreType.DMA((len(given),)),
+            pltpu.SemaphoreType.DMA((len(given) - 2,)),
             pltpu.SemaphoreType.DMA,
+            pltpu.SemaphoreType.DMA((2, 4)),
         ],
-        compiler_params=pltpu.CompilerParams(vmem_limit_bytes=16 << 20),
+        compiler_params=pltpu.CompilerParams(vmem_limit_bytes=14 << 20),
         cost_estimate=pl.CostEstimate(flops=10**9, bytes_accessed=6 << 20, transcendentals=0),
         name="prepare",
     )(*(pltpu.with_memory_space_constraint(x, pltpu.HBM) for x in (psi, *given)), *near)

time: 43.7 us -> 43.2 us (0.989)
  starting transfers between devices: 22 us -> 21.5 us
    ppermute x14, starting transfers between devices: 22 us -> 21.4 us  [across(): return lax.ppermute(value, 'tile', [(i, i ^ k) for i in range(n)])]
    pallas_call x1, Pallas kernels: 3.27 us -> 3.82 us  [prepare_call(): pl.pallas_call(functools.partial(prepare_kernel, n), out_shape=(jax.Shape...]
  transfers between devices with their start and end apart: 15 -> 15, of which waited for: 3 -> 2; matrix products, arithmetic and copies ran while one was open for 2% -> 2% of each run, Pallas kernels for 16% -> 16%
where the time goes in v5:
time: 43.2 us; the launch traced here: 43.1 us
  starting transfers between devices  21.5 us (50%)
  Pallas kernels  16.2 us (38%)
  waiting for transfers between devices  3.72 us (9%)
  local copies, waits for them, and re-layouts  0.98 us (2%)
  between operations  0.74 us (2%)
    ppermute x14, starting transfers between devices, across(): return lax.ppermute(value, 'tile', [(i, i ^ k) for i in range(n)])  21.4 us
    pallas_call x1, Pallas kernels, renew_call(): pl.pallas_call(functools.partial(renew_kernel, n), out_shape=(pltpu.VMEM(...  5.14 us
    pallas_call x1, Pallas kernels, prepare_call(): pl.pallas_call(functools.partial(prepare_kernel, n), out_shape=(jax.Shape...  3.82 us
    ppermute x14, waiting for transfers between devices, across(): return lax.ppermute(value, 'tile', [(i, i ^ k) for i in range(n)])  3.72 us
    pallas_call x1, Pallas kernels, source_call(): pl.pallas_call(functools.partial(source_kernel, n), out_shape=(pltpu.VMEM...  3.23 us
    pallas_call x1, Pallas kernels, apply_call(): pl.pallas_call(functools.partial(apply_kernel, n), out_shape=tuple((jax.S...  3.22 us
    unnamed x3, local copies, waits for them, and re-layouts  0.98 us
  transfers between devices with their start and end apart: 15, of which 2 were waited for; matrix products, arithmetic and copies ran while one was open for 2% of the time, Pallas kernels for 16%

profile of v5, /device:TPU:0, one launch (start us, length us, event | category | flops | bytes accessed | tf_op | source)
XLA Modules:
  0.0 43.1 jit_solution(17455752753506246209)
XLA Ops:
  0.6 4.1 %collective-permute-start.3 = (f32[128,128]{1,0:T(8,128)}, f32[128,128]{1,0:T(8,128)S(1)}, u32[]{:S(2)}, u32[]{:S(2)}) collective-permute-start(f32[128,128]{1,0:T(8,128)} %bitcast.8), channel_id=1, source_target_pairs={{0,4},{1,5},{2,6},{3,7},{4,0},{5,1},{6,2},{7,3},{8,12},{9,13},{10,... | collective-permute-start | bytes 196616 | tf_op jit(solution)/shard_map/ppermute | solution.py:629
  4.7 2.5 %collective-permute-start.2 = (f32[128,128]{1,0:T(8,128)}, f32[128,128]{1,0:T(8,128)S(1)}, u32[]{:S(2)}, u32[]{:S(2)}) collective-permute-start(f32[128,128]{1,0:T(8,128)} %bitcast.9), channel_id=1, source_target_pairs={{0,3},{1,2},{2,1},{3,0},{4,7},{5,6},{6,5},{7,4},{8,11},{9,10},{10,... | collective-permute-start | bytes 196616 | tf_op jit(solution)/shard_map/ppermute | solution.py:629
  7.3 0.4 %collective-permute-start.1 = (f32[128,128]{1,0:T(8,128)}, f32[128,128]{1,0:T(8,128)S(1)}, u32[]{:S(2)}, u32[]{:S(2)}) collective-permute-start(f32[128,128]{1,0:T(8,128)} %bitcast.10), channel_id=1, source_target_pairs={{0,2},{1,3},{2,0},{3,1},{4,6},{5,7},{6,4},{7,5},{8,10},{9,11},{10,... | collective-permute-start | bytes 196616 | tf_op jit(solution)/shard_map/ppermute | solution.py:629
  7.7 0.5 %collective-permute-start = (f32[128,128]{1,0:T(8,128)}, f32[128,128]{1,0:T(8,128)S(1)}, u32[]{:S(2)}, u32[]{:S(2)}) collective-permute-start(f32[128,128]{1,0:T(8,128)} %bitcast.11), channel_id=1, source_target_pairs={{0,1},{1,0},{2,3},{3,2},{4,5},{5,4},{6,7},{7,6},{8,9},{9,8},{10,11... | collective-permute-start | bytes 196616 | tf_op jit(solution)/shard_map/ppermute | solution.py:629
  8.2 0.0 collective-permute-done.3.refs_4_
  8.2 1.6 %collective-permute-start.6 = (f32[128,128]{1,0:T(8,128)S(1)}, f32[128,128]{1,0:T(8,128)S(1)}, u32[]{:S(2)}, u32[]{:S(2)}) collective-permute-start(f32[128,128]{1,0:T(8,128)S(1)} %collective-permute-done.3.refs_4_), channel_id=1, source_target_pairs={{0,1},{1,0},{2,3},{3,2},{4,5},{5,4},{6,7},{7,6},{8,9},{9,8},{10,11... | collective-permute-start | bytes 196616 | tf_op jit(solution)/shard_map/ppermute | solution.py:629
  9.9 1.5 %collective-permute-start.5 = (f32[128,128]{1,0:T(8,128)S(1)}, f32[128,128]{1,0:T(8,128)S(1)}, u32[]{:S(2)}, u32[]{:S(2)}) collective-permute-start(f32[128,128]{1,0:T(8,128)S(1)} %collective-permute-done.3.refs_4_), channel_id=1, source_target_pairs={{0,2},{1,3},{2,0},{3,1},{4,6},{5,7},{6,4},{7,5},{8,10},{9,11},{10,... | collective-permute-start | bytes 196616 | tf_op jit(solution)/shard_map/ppermute | solution.py:629
  11.3 0.0 collective-permute-done.2.refs_15_.refs_7_
  11.3 1.4 %collective-permute-start.4 = (f32[128,128]{1,0:T(8,128)S(1)}, f32[128,128]{1,0:T(8,128)S(1)}, u32[]{:S(2)}, u32[]{:S(2)}) collective-permute-start(f32[128,128]{1,0:T(8,128)S(1)} %collective-permute-done.3.refs_4_), channel_id=1, source_target_pairs={{0,3},{1,2},{2,1},{3,0},{4,7},{5,6},{6,5},{7,4},{8,11},{9,10},{10,... | collective-permute-start | bytes 196616 | tf_op jit(solution)/shard_map/ppermute | solution.py:629
  12.7 0.0 collective-permute-done.1.refs_14_.refs_6_
  12.7 0.0 collective-permute-done.refs_13_.refs_5_
  12.7 3.8 %prepare.1 = (bf16[2048,256]{1,0:T(8,128)(2,1)S(1)}, bf16[16,256,128]{2,1,0:T(8,128)(2,1)S(1)}, s32[8,192]{1,0:T(8,128)S(1)}, f32[8,192]{1,0:T(8,128)S(1)}, s32[...) custom-call(f32[1,1,128,128]{3,2,1,0:T(8,128)} %refs_0_.1, ...), custom_call_target="tpu_custom_call" | custom-call | flops 1000000000 | bytes 6291456 | tf_op jit(solution)/shard_map/prepare/pallas_call | solution.py:353
  16.5 0.0 collective-permute-done.6.refs_3_
  16.6 0.0 collective-permute-done.5.refs_2_
  16.6 0.0 collective-permute-done.4.refs_1_
  16.6 5.1 %renew.1 = (f32[16,128,128]{2,1,0:T(8,128)S(1)}, f32[257,128,128]{2,1,0:T(8,128)S(1)}) custom-call(f32[128,128]{1,0:T(8,128)S(1)} %get-tuple-element.24.refs_0_.refs_5_, f32[128,128]{1,0:T(8,128)S(1)} %collective-permute-done.4.refs_1_, f32[128,128]{1,0:T(8,128)S(1)} %collective-permute-done.5.refs_2_, ...), custom_call_target="tpu_custom_call", output_to_operand_aliasing={{1}: (11, {})} | custom-call | flops 10000000000 | bytes 3145728 | tf_op jit(solution)/shard_map/renew/pallas_call | solution.py:428
  21.7 0.1 collective-permute-start.7
  21.8 0.0 copy-start
  21.8 3.2 %sources.1 = (f32[257,128,128]{2,1,0:T(8,128)S(1)}, f32[24,128]{1,0:T(8,128)S(1)}) custom-call(f32[128,128]{1,0:T(8,128)S(1)} %get-tuple-element.24.refs_0_.refs_5_, f32[128,128]{1,0:T(8,128)S(1)} %collective-permute-done.4.refs_1_, f32[128,128]{1,0:T(8,128)S(1)} %collective-permute-done.5.refs_2_, f32[128,128]{1,0:T(8,128)S(1)} %collective-permute-done.6.refs_3_, ...), custom_call_target="tpu_custom_call" | custom-call | flops 10000000000 | bytes 10485760 | tf_op jit(solution)/shard_map/sources/pallas_call | solution.py:496
  25.0 0.0 collective-permute-done.7.refs_9_
  25.1 0.0 copy-done
  25.1 3.2 %applied.1 = (f32[136,128]{1,0:T(8,128)S(1)}, f32[136,128]{1,0:T(8,128)S(1)}, f32[136,128]{1,0:T(8,128)S(1)}, f32[136,128]{1,0:T(8,128)S(1)}, f32[136,128]{1,0:T...) custom-call(f32[128,128]{1,0:T(8,128)S(1)} %get-tuple-element.24.refs_0_.refs_5_, ...), custom_call_target="tpu_custom_call" | custom-call | flops 5000000000 | bytes 10485760 | tf_op jit(solution)/shard_map/applied/pallas_call | solution.py:562
  28.3 1.6 %collective-permute-start.11 = (f32[136,128]{1,0:T(8,128)S(1)}, f32[136,128]{1,0:T(8,128)S(1)}, u32[]{:S(2)}, u32[]{:S(2)}) collective-permute-start(f32[136,128]{1,0:T(8,128)S(1)} %get-tuple-element.39), channel_id=1, source_target_pairs={{0,3},{1,2},{2,1},{3,0},{4,7},{5,6},{6,5},{7,4},{8,11},{9,10},{10,... | collective-permute-start | bytes 208904 | tf_op jit(solution)/shard_map/ppermute | solution.py:629
  29.9 1.2 %collective-permute-start.12 = (f32[136,128]{1,0:T(8,128)S(1)}, f32[136,128]{1,0:T(8,128)S(1)}, u32[]{:S(2)}, u32[]{:S(2)}) collective-permute-start(f32[136,128]{1,0:T(8,128)S(1)} %get-tuple-element.40), channel_id=1, source_target_pairs={{0,2},{1,3},{2,0},{3,1},{4,6},{5,7},{6,4},{7,5},{8,10},{9,11},{10,... | collective-permute-start | bytes 208904 | tf_op jit(solution)/shard_map/ppermute | solution.py:629
  31.1 0.8 %collective-permute-start.13 = (f32[136,128]{1,0:T(8,128)S(1)}, f32[136,128]{1,0:T(8,128)S(1)}, u32[]{:S(2)}, u32[]{:S(2)}) collective-permute-start(f32[136,128]{1,0:T(8,128)S(1)} %get-tuple-element.41), channel_id=1, source_target_pairs={{0,1},{1,0},{2,3},{3,2},{4,5},{5,4},{6,7},{7,6},{8,9},{9,8},{10,11... | collective-permute-start | bytes 208904 | tf_op jit(solution)/shard_map/ppermute | solution.py:629
  31.9 1.6 %collective-permute-start.8 = (f32[136,128]{1,0:T(8,128)S(1)}, f32[136,128]{1,0:T(8,128)S(1)}, u32[]{:S(2)}, u32[]{:S(2)}) collective-permute-start(f32[136,128]{1,0:T(8,128)S(1)} %get-tuple-element.35), channel_id=1, source_target_pairs={{0,3},{1,2},{2,1},{3,0},{4,7},{5,6},{6,5},{7,4},{8,11},{9,10},{10,... | collective-permute-start | bytes 208904 | tf_op jit(solution)/shard_map/ppermute | solution.py:629
  33.4 1.2 %collective-permute-start.9 = (f32[136,128]{1,0:T(8,128)S(1)}, f32[136,128]{1,0:T(8,128)S(1)}, u32[]{:S(2)}, u32[]{:S(2)}) collective-permute-start(f32[136,128]{1,0:T(8,128)S(1)} %get-tuple-element.36), channel_id=1, source_target_pairs={{0,2},{1,3},{2,0},{3,1},{4,6},{5,7},{6,4},{7,5},{8,10},{9,11},{10,... | collective-permute-start | bytes 208904 | tf_op jit(solution)/shard_map/ppermute | solution.py:629
  34.6 0.0 collective-permute-done.11
  34.6 0.9 %collective-permute-start.10 = (f32[136,128]{1,0:T(8,128)S(1)}, f32[136,128]{1,0:T(8,128)S(1)}, u32[]{:S(2)}, u32[]{:S(2)}) collective-permute-start(f32[136,128]{1,0:T(8,128)S(1)} %get-tuple-element.37), channel_id=1, source_target_pairs={{0,1},{1,0},{2,3},{3,2},{4,5},{5,4},{6,7},{7,6},{8,9},{9,8},{10,11... | collective-permute-start | bytes 208904 | tf_op jit(solution)/shard_map/ppermute | solution.py:629
  35.5 0.0 collective-permute-done.12
  35.5 0.6 %collective-permute-done.13 = f32[136,128]{1,0:T(8,128)S(1)} collective-permute-done((f32[136,128]{1,0:T(8,128)S(1)}, f32[136,128]{1,0:T(8,128)S(1)}, u32[]{:S(2)}, u32[]{:S(2)}) %collective-permute-start.13) | collective-permute-done | bytes 69664 | tf_op jit(solution)/shard_map/ppermute | solution.py:629
  36.2 2.1 %collective-permute-start.14 = (f32[136,128]{1,0:T(8,128)S(1)}, f32[136,128]{1,0:T(8,128)S(1)}, u32[]{:S(2)}, u32[]{:S(2)}) collective-permute-start(f32[136,128]{1,0:T(8,128)S(1)} %add_add_fusion), channel_id=1, source_target_pairs={{0,4},{1,5},{2,6},{3,7},{4,0},{5,1},{6,2},{7,3},{8,12},{9,13},{10,... | collective-permute-start | bytes 208904 | tf_op jit(solution)/shard_map/ppermute | solution.py:629
  38.3 1.0 %copy.18 = f32[1,16,128,128]{3,2,1,0:T(8,128)} copy(f32[1,16,128,128]{3,2,1,0:T(8,128)S(1)} %bitcast.6) | data formatting | bytes 2097152
  39.3 0.0 collective-permute-done.8.refs_1_
  39.3 0.0 collective-permute-done.9.refs_2_
  39.3 0.0 collective-permute-done.10.refs_3_
  39.3 3.1 %collective-permute-done.14.refs_4_ = f32[136,128]{1,0:T(8,128)S(1)} collective-permute-done((f32[136,128]{1,0:T(8,128)S(1)}, f32[136,128]{1,0:T(8,128)S(1)}, u32[]{:S(2)}, u32[]{:S(2)}) %collective-permute-start.14) | collective-permute-done | bytes 69664 | tf_op jit(solution)/shard_map/ppermute | solution.py:629
  42.4 0.8 %finish.1 = (f32[128,128]{1,0:T(8,128)}, f32[1,128]{1,0:T(1,128)}) custom-call(f32[136,128]{1,0:T(8,128)S(1)} %get-tuple-element.34.refs_0_, f32[136,128]{1,0:T(8,128)S(1)} %collective-permute-done.8.refs_1_, f32[136,128]{1,0:T(8,128)S(1)} %collective-permute-done.9.refs_2_, f32[136,128]{1,0:T(8,128)S(1)} %collective-permute-done.10.refs_3_, ...), custom_call_target="tpu_custom_call" | custom-call | tf_op jit(solution)/shard_map/finish/pallas_call | solution.py:602
  (1 shorter events, 0.0 us)
Async XLA Ops:
  0.6 7.6 %collective-permute-start.3 = (f32[128,128]{1,0:T(8,128)}, f32[128,128]{1,0:T(8,128)S(1)}, u32[]{:S(2)}, u32[]{:S(2)}) collective-permute-start(f32[128,128]{1,0:T(8,128)} %bitcast.8), channel_id=1, source_target_pairs={{0,4},{1,5},{2,6},{3,7},{4,0},{5,1},{6,2},{7,3},{8,12},{9,13},{10,... | collective-permute-start | bytes 196616 | tf_op jit(solution)/shard_map/ppermute | solution.py:629
  4.7 6.6 %collective-permute-start.2 = (f32[128,128]{1,0:T(8,128)}, f32[128,128]{1,0:T(8,128)S(1)}, u32[]{:S(2)}, u32[]{:S(2)}) collective-permute-start(f32[128,128]{1,0:T(8,128)} %bitcast.9), channel_id=1, source_target_pairs={{0,3},{1,2},{2,1},{3,0},{4,7},{5,6},{6,5},{7,4},{8,11},{9,10},{10,... | collective-permute-start | bytes 196616 | tf_op jit(solution)/shard_map/ppermute | solution.py:629
  7.3 5.4 %collective-permute-start.1 = (f32[128,128]{1,0:T(8,128)}, f32[128,128]{1,0:T(8,128)S(1)}, u32[]{:S(2)}, u32[]{:S(2)}) collective-permute-start(f32[128,128]{1,0:T(8,128)} %bitcast.10), channel_id=1, source_target_pairs={{0,2},{1,3},{2,0},{3,1},{4,6},{5,7},{6,4},{7,5},{8,10},{9,11},{10,... | collective-permute-start | bytes 196616 | tf_op jit(solution)/shard_map/ppermute | solution.py:629
  7.7 5.0 %collective-permute-start = (f32[128,128]{1,0:T(8,128)}, f32[128,128]{1,0:T(8,128)S(1)}, u32[]{:S(2)}, u32[]{:S(2)}) collective-permute-start(f32[128,128]{1,0:T(8,128)} %bitcast.11), channel_id=1, source_target_pairs={{0,1},{1,0},{2,3},{3,2},{4,5},{5,4},{6,7},{7,6},{8,9},{9,8},{10,11... | collective-permute-start | bytes 196616 | tf_op jit(solution)/shard_map/ppermute | solution.py:629
  8.2 8.3 %collective-permute-start.6 = (f32[128,128]{1,0:T(8,128)S(1)}, f32[128,128]{1,0:T(8,128)S(1)}, u32[]{:S(2)}, u32[]{:S(2)}) collective-permute-start(f32[128,128]{1,0:T(8,128)S(1)} %collective-permute-done.3.refs_4_), channel_id=1, source_target_pairs={{0,1},{1,0},{2,3},{3,2},{4,5},{5,4},{6,7},{7,6},{8,9},{9,8},{10,11... | collective-permute-start | bytes 196616 | tf_op jit(solution)/shard_map/ppermute | solution.py:629
  9.9 6.7 %collective-permute-start.5 = (f32[128,128]{1,0:T(8,128)S(1)}, f32[128,128]{1,0:T(8,128)S(1)}, u32[]{:S(2)}, u32[]{:S(2)}) collective-permute-start(f32[128,128]{1,0:T(8,128)S(1)} %collective-permute-done.3.refs_4_), channel_id=1, source_target_pairs={{0,2},{1,3},{2,0},{3,1},{4,6},{5,7},{6,4},{7,5},{8,10},{9,11},{10,... | collective-permute-start | bytes 196616 | tf_op jit(solution)/shard_map/ppermute | solution.py:629
  11.3 5.2 %collective-permute-start.4 = (f32[128,128]{1,0:T(8,128)S(1)}, f32[128,128]{1,0:T(8,128)S(1)}, u32[]{:S(2)}, u32[]{:S(2)}) collective-permute-start(f32[128,128]{1,0:T(8,128)S(1)} %collective-permute-done.3.refs_4_), channel_id=1, source_target_pairs={{0,3},{1,2},{2,1},{3,0},{4,7},{5,6},{6,5},{7,4},{8,11},{9,10},{10,... | collective-permute-start | bytes 196616 | tf_op jit(solution)/shard_map/ppermute | solution.py:629
  21.7 3.3 %collective-permute-start.7 = (f32[16,128,128]{2,1,0:T(8,128)S(1)}, f32[16,128,128]{2,1,0:T(8,128)S(1)}, u32[]{:S(2)}, u32[]{:S(2)}) collective-permute-start(f32[16,128,128]{2,1,0:T(8,128)S(1)} %get-tuple-element.29), channel_id=1, source_target_pairs={{0,8},{8,0},{1,9},{9,1},{2,10},{10,2},{3,11},{11,3},{4,12},{12,4},... | collective-permute-start | bytes 3145736 | tf_op jit(solution)/shard_map/ppermute | solution.py:644
  21.8 3.3 %copy-start = (f32[1,16,128,128]{3,2,1,0:T(8,128)S(1)}, f32[1,16,128,128]{3,2,1,0:T(8,128)}, u32[]{:S(2)}) copy-start(f32[1,16,128,128]{3,2,1,0:T(8,128)} %refs_11_.1) | copy-start | bytes 3145732
  28.3 6.3 %collective-permute-start.11 = (f32[136,128]{1,0:T(8,128)S(1)}, f32[136,128]{1,0:T(8,128)S(1)}, u32[]{:S(2)}, u32[]{:S(2)}) collective-permute-start(f32[136,128]{1,0:T(8,128)S(1)} %get-tuple-element.39), channel_id=1, source_target_pairs={{0,3},{1,2},{2,1},{3,0},{4,7},{5,6},{6,5},{7,4},{8,11},{9,10},{10,... | collective-permute-start | bytes 208904 | tf_op jit(solution)/shard_map/ppermute | solution.py:629
  29.9 5.6 %collective-permute-start.12 = (f32[136,128]{1,0:T(8,128)S(1)}, f32[136,128]{1,0:T(8,128)S(1)}, u32[]{:S(2)}, u32[]{:S(2)}) collective-permute-start(f32[136,128]{1,0:T(8,128)S(1)} %get-tuple-element.40), channel_id=1, source_target_pairs={{0,2},{1,3},{2,0},{3,1},{4,6},{5,7},{6,4},{7,5},{8,10},{9,11},{10,... | collective-permute-start | bytes 208904 | tf_op jit(solution)/shard_map/ppermute | solution.py:629
  31.1 5.1 %collective-permute-start.13 = (f32[136,128]{1,0:T(8,128)S(1)}, f32[136,128]{1,0:T(8,128)S(1)}, u32[]{:S(2)}, u32[]{:S(2)}) collective-permute-start(f32[136,128]{1,0:T(8,128)S(1)} %get-tuple-element.41), channel_id=1, source_target_pairs={{0,1},{1,0},{2,3},{3,2},{4,5},{5,4},{6,7},{7,6},{8,9},{9,8},{10,11... | collective-permute-start | bytes 208904 | tf_op jit(solution)/shard_map/ppermute | solution.py:629
  31.9 7.4 %collective-permute-start.8 = (f32[136,128]{1,0:T(8,128)S(1)}, f32[136,128]{1,0:T(8,128)S(1)}, u32[]{:S(2)}, u32[]{:S(2)}) collective-permute-start(f32[136,128]{1,0:T(8,128)S(1)} %get-tuple-element.35), channel_id=1, source_target_pairs={{0,3},{1,2},{2,1},{3,0},{4,7},{5,6},{6,5},{7,4},{8,11},{9,10},{10,... | collective-permute-start | bytes 208904 | tf_op jit(solution)/shard_map/ppermute | solution.py:629
  33.4 5.9 %collective-permute-start.9 = (f32[136,128]{1,0:T(8,128)S(1)}, f32[136,128]{1,0:T(8,128)S(1)}, u32[]{:S(2)}, u32[]{:S(2)}) collective-permute-start(f32[136,128]{1,0:T(8,128)S(1)} %get-tuple-element.36), channel_id=1, source_target_pairs={{0,2},{1,3},{2,0},{3,1},{4,6},{5,7},{6,4},{7,5},{8,10},{9,11},{10,... | collective-permute-start | bytes 208904 | tf_op jit(solution)/shard_map/ppermute | solution.py:629
  34.6 4.7 %collective-permute-start.10 = (f32[136,128]{1,0:T(8,128)S(1)}, f32[136,128]{1,0:T(8,128)S(1)}, u32[]{:S(2)}, u32[]{:S(2)}) collective-permute-start(f32[136,128]{1,0:T(8,128)S(1)} %get-tuple-element.37), channel_id=1, source_target_pairs={{0,1},{1,0},{2,3},{3,2},{4,5},{5,4},{6,7},{7,6},{8,9},{9,8},{10,11... | collective-permute-start | bytes 208904 | tf_op jit(solution)/shard_map/ppermute | solution.py:629
  36.2 6.2 %collective-permute-start.14 = (f32[136,128]{1,0:T(8,128)S(1)}, f32[136,128]{1,0:T(8,128)S(1)}, u32[]{:S(2)}, u32[]{:S(2)}) collective-permute-start(f32[136,128]{1,0:T(8,128)S(1)} %add_add_fusion), channel_id=1, source_target_pairs={{0,4},{1,5},{2,6},{3,7},{4,0},{5,1},{6,2},{7,3},{8,12},{9,13},{10,... | collective-permute-start | bytes 208904 | tf_op jit(solution)/shard_map/ppermute | solution.py:629

commit v6 on v5

--- a/solution.py
+++ b/solution.py
@@ -420,7 +420,7 @@
             renewed[b] = found[:, :w] + (found[:, w:] + small[:, i * w : (i + 1) * w])
         return unused
 
-    lax.fori_loop(0, channels // 2, finish, 0, unroll=4)
+    lax.fori_loop(0, channels // 2, finish, 0, unroll=8)
 
 
 def renew_call(tiles, lefts, int_table, float_table, entries, channels):
@@ -452,7 +452,7 @@
 
 def source_kernel(n, *refs):
     tiles = [refs[ORDER.index(k)] for k in range(n)]
-    rights, int_table, float_table, entries, stats, sources, ints, floats, arrived = refs[n:]
+    rights, int_table, float_table, entries, sources, ints, floats, arrived = refs[n:]
     channels, w = rights.shape[0], rights.shape[2]
     copies = fetch_tables((int_table, float_table), (ints, floats), arrived)
     for k in range(n):
@@ -479,28 +479,15 @@
     for copy in copies:
         copy.wait()
     spill(ints, floats, entries)
-    weight = jnp.zeros((8, w), F32)
-    energy = jnp.zeros((8, w), F32)
-    for k in range(n):
-        value = tiles[k][...]
-        squares = jnp.sum((value * value).reshape(w // 8, 8, w), axis=0)
-        weight += squares
-        energy += floats[4, k] * squares
-    stats[0:8] = weight
-    stats[8:16] = energy
-    stats[16:24] = jnp.full((8, w), floats[4, 0], F32)
 
 
 def source_call(tiles, rights, int_table, float_table):
     n, w = len(tiles), rights.shape[2]
     return pl.pallas_call(
         functools.partial(source_kernel, n),
-        out_shape=(
-            pltpu.VMEM((2 * w + 1, w, w), F32),
-            jax.ShapeDtypeStruct((24, w), F32),
-        ),
+        out_shape=pltpu.VMEM((2 * w + 1, w, w), F32),
         in_specs=[VMEM] * (n + 1) + [ANY] * 2,
-        out_specs=(VMEM, VMEM),
+        out_specs=VMEM,
         scratch_shapes=[
             pltpu.VMEM((n * w, 4 * w), BF16),
             pltpu.SMEM(int_table.shape, jnp.int32),
@@ -511,6 +498,33 @@
         cost_estimate=pl.CostEstimate(flops=10**10, bytes_accessed=10 << 20, transcendentals=0),
         name="sources",
     )(*(tiles[k] for k in ORDER), rights, int_table, float_table)
+
+
+def norm_kernel(n, *refs):
+    tiles, (floats, stats) = refs[:n], refs[n:]
+    w = stats.shape[1]
+    weight = jnp.zeros((8, w), F32)
+    energy = jnp.zeros((8, w), F32)
+    for k in range(n):
+        value = tiles[k][...]
+        squares = jnp.sum((value * value).reshape(w // 8, 8, w), axis=0)
+        weight += squares
+        energy += floats[4:5, k : k + 1] * squares
+    stats[0:8] = weight
+    stats[8:16] = energy
+    stats[16:24] = jnp.broadcast_to(floats[4:5, 0:1], (8, w))
+
+
+def norm_call(tiles, float_table):
+    n, w = len(tiles), tiles[0].shape[0]
+    return pl.pallas_call(
+        functools.partial(norm_kernel, n),
+        out_shape=jax.ShapeDtypeStruct((24, w), F32),
+        in_specs=[VMEM] * (n + 1),
+        out_specs=VMEM,
+        compiler_params=pltpu.CompilerParams(vmem_limit_bytes=2 << 20),
+        name="norms",
+    )(*tiles, float_table)
 
 
 def apply_kernel(n, *refs):
@@ -642,7 +656,8 @@
     tiles = [tiles[k] for k in range(n)]
     renewal = renew_call(tiles, lefts, up_ints, up_floats, products, left_env.shape[1])
     received = lax.ppermute(renewal, "seg", [(0, 1), (1, 0)])
-    entries, stats = source_call(tiles, rights, mv_ints, mv_floats)
+    entries = source_call(tiles, rights, mv_ints, mv_floats)
+    stats = norm_call(tiles, mv_floats)
     partials = apply_call(tiles, left_env[0], received, entries, mv_ints, mv_floats)
 
     far = partials[half]

time: 43.2 us -> 42.9 us (level)
  waiting for transfers between devices: 3.72 us -> 2.74 us
  starting transfers between devices: 21.5 us -> 22.1 us
    ppermute x14, waiting for transfers between devices: 3.72 us -> 2.73 us  [across(): return lax.ppermute(value, 'tile', [(i, i ^ k) for i in range(n)])]
    ppermute x14, starting transfers between devices: 21.4 us -> 22 us  [across(): return lax.ppermute(value, 'tile', [(i, i ^ k) for i in range(n)])]
    pallas_call x1 -> x2, Pallas kernels: 3.23 us -> 3.12 us  [the longest x1 3.04 us: source_call(): pl.pallas_call(functools.partial(source_kernel, n), out_shape=pltpu.VMEM(...]
where the time goes in v6:
time: 42.9 us; the launch traced here: 42.5 us
  starting transfers between devices  22.1 us (52%)
  Pallas kernels  16 us (37%)
  waiting for transfers between devices  2.74 us (6%)
  local copies, waits for them, and re-layouts  0.98 us (2%)
  between operations  0.75 us (2%)
    ppermute x14, starting transfers between devices, across(): return lax.ppermute(value, 'tile', [(i, i ^ k) for i in range(n)])  22 us
    pallas_call x1, Pallas kernels, renew_call(): pl.pallas_call(functools.partial(renew_kernel, n), out_shape=(pltpu.VMEM(...  5.05 us
    pallas_call x1, Pallas kernels, prepare_call(): pl.pallas_call(functools.partial(prepare_kernel, n), out_shape=(jax.Shape...  3.82 us
    pallas_call x1, Pallas kernels, apply_call(): pl.pallas_call(functools.partial(apply_kernel, n), out_shape=tuple((jax.S...  3.22 us
    pallas_call x1, Pallas kernels, source_call(): pl.pallas_call(functools.partial(source_kernel, n), out_shape=pltpu.VMEM(...  3.04 us
    ppermute x14, waiting for transfers between devices, across(): return lax.ppermute(value, 'tile', [(i, i ^ k) for i in range(n)])  2.73 us
    unnamed x3, local copies, waits for them, and re-layouts  0.98 us
  transfers between devices with their start and end apart: 15, of which 2 were waited for; matrix products, arithmetic and copies ran while one was open for 2% of the time, Pallas kernels for 16%

profile of v6, /device:TPU:0, one launch (start us, length us, event | category | flops | bytes accessed | tf_op | source)
XLA Modules:
  0.0 42.5 jit_solution(6519113715066380875)
XLA Ops:
  0.6 4.1 %collective-permute-start.3 = (f32[128,128]{1,0:T(8,128)}, f32[128,128]{1,0:T(8,128)S(1)}, u32[]{:S(2)}, u32[]{:S(2)}) collective-permute-start(f32[128,128]{1,0:T(8,128)} %bitcast.8), channel_id=1, source_target_pairs={{0,4},{1,5},{2,6},{3,7},{4,0},{5,1},{6,2},{7,3},{8,12},{9,13},{10,... | collective-permute-start | bytes 196616 | tf_op jit(solution)/shard_map/ppermute | solution.py:643
  4.7 2.5 %collective-permute-start.2 = (f32[128,128]{1,0:T(8,128)}, f32[128,128]{1,0:T(8,128)S(1)}, u32[]{:S(2)}, u32[]{:S(2)}) collective-permute-start(f32[128,128]{1,0:T(8,128)} %bitcast.9), channel_id=1, source_target_pairs={{0,3},{1,2},{2,1},{3,0},{4,7},{5,6},{6,5},{7,4},{8,11},{9,10},{10,... | collective-permute-start | bytes 196616 | tf_op jit(solution)/shard_map/ppermute | solution.py:643
  7.3 0.4 %collective-permute-start.1 = (f32[128,128]{1,0:T(8,128)}, f32[128,128]{1,0:T(8,128)S(1)}, u32[]{:S(2)}, u32[]{:S(2)}) collective-permute-start(f32[128,128]{1,0:T(8,128)} %bitcast.10), channel_id=1, source_target_pairs={{0,2},{1,3},{2,0},{3,1},{4,6},{5,7},{6,4},{7,5},{8,10},{9,11},{10,... | collective-permute-start | bytes 196616 | tf_op jit(solution)/shard_map/ppermute | solution.py:643
  7.7 0.5 %collective-permute-start = (f32[128,128]{1,0:T(8,128)}, f32[128,128]{1,0:T(8,128)S(1)}, u32[]{:S(2)}, u32[]{:S(2)}) collective-permute-start(f32[128,128]{1,0:T(8,128)} %bitcast.11), channel_id=1, source_target_pairs={{0,1},{1,0},{2,3},{3,2},{4,5},{5,4},{6,7},{7,6},{8,9},{9,8},{10,11... | collective-permute-start | bytes 196616 | tf_op jit(solution)/shard_map/ppermute | solution.py:643
  8.2 0.0 collective-permute-done.3.refs_4_
  8.2 1.6 %collective-permute-start.6 = (f32[128,128]{1,0:T(8,128)S(1)}, f32[128,128]{1,0:T(8,128)S(1)}, u32[]{:S(2)}, u32[]{:S(2)}) collective-permute-start(f32[128,128]{1,0:T(8,128)S(1)} %collective-permute-done.3.refs_4_), channel_id=1, source_target_pairs={{0,1},{1,0},{2,3},{3,2},{4,5},{5,4},{6,7},{7,6},{8,9},{9,8},{10,11... | collective-permute-start | bytes 196616 | tf_op jit(solution)/shard_map/ppermute | solution.py:643
  9.9 1.5 %collective-permute-start.5 = (f32[128,128]{1,0:T(8,128)S(1)}, f32[128,128]{1,0:T(8,128)S(1)}, u32[]{:S(2)}, u32[]{:S(2)}) collective-permute-start(f32[128,128]{1,0:T(8,128)S(1)} %collective-permute-done.3.refs_4_), channel_id=1, source_target_pairs={{0,2},{1,3},{2,0},{3,1},{4,6},{5,7},{6,4},{7,5},{8,10},{9,11},{10,... | collective-permute-start | bytes 196616 | tf_op jit(solution)/shard_map/ppermute | solution.py:643
  11.3 0.0 collective-permute-done.2.refs_15_.refs_7_.refs_3_
  11.3 1.4 %collective-permute-start.4 = (f32[128,128]{1,0:T(8,128)S(1)}, f32[128,128]{1,0:T(8,128)S(1)}, u32[]{:S(2)}, u32[]{:S(2)}) collective-permute-start(f32[128,128]{1,0:T(8,128)S(1)} %collective-permute-done.3.refs_4_), channel_id=1, source_target_pairs={{0,3},{1,2},{2,1},{3,0},{4,7},{5,6},{6,5},{7,4},{8,11},{9,10},{10,... | collective-permute-start | bytes 196616 | tf_op jit(solution)/shard_map/ppermute | solution.py:643
  12.7 0.0 collective-permute-done.1.refs_14_.refs_6_.refs_2_
  12.7 0.0 collective-permute-done.refs_13_.refs_5_.refs_1_
  12.7 3.8 %prepare.1 = (bf16[2048,256]{1,0:T(8,128)(2,1)S(1)}, bf16[16,256,128]{2,1,0:T(8,128)(2,1)S(1)}, s32[8,192]{1,0:T(8,128)S(1)}, f32[8,192]{1,0:T(8,128)S(1)}, s32[...) custom-call(f32[1,1,128,128]{3,2,1,0:T(8,128)} %refs_0_.1, ...), custom_call_target="tpu_custom_call" | custom-call | flops 1000000000 | bytes 6291456 | tf_op jit(solution)/shard_map/prepare/pallas_call | solution.py:353
  16.5 0.0 collective-permute-done.6.refs_3_.refs_5_
  16.6 0.0 collective-permute-done.5.refs_2_.refs_6_
  16.6 0.0 collective-permute-done.4.refs_1_.refs_7_
  16.6 5.1 %renew.1 = (f32[16,128,128]{2,1,0:T(8,128)S(1)}, f32[257,128,128]{2,1,0:T(8,128)S(1)}) custom-call(f32[128,128]{1,0:T(8,128)S(1)} %get-tuple-element.22.refs_0_.refs_5_, f32[128,128]{1,0:T(8,128)S(1)} %collective-permute-done.4.refs_1_.refs_7_, f32[128,128]{1,0:T(8,128)S(1)} %collective-permute-done.5.refs_2_.refs_6_, ...), custom_call_target="tpu_custom_call", output_to_operand_aliasing={{1}: (11, {})} | custom-call | flops 10000000000 | bytes 3145728 | tf_op jit(solution)/shard_map/renew/pallas_call | solution.py:428
  21.6 0.1 collective-permute-start.7
  21.7 0.0 copy-start
  21.7 3.0 %sources.1.refs_10_ = f32[257,128,128]{2,1,0:T(8,128)S(1)} custom-call(f32[128,128]{1,0:T(8,128)S(1)} %get-tuple-element.22.refs_0_.refs_5_, f32[128,128]{1,0:T(8,128)S(1)} %collective-permute-done.4.refs_1_.refs_7_, f32[128,128]{1,0:T(8,128)S(1)} %collective-permute-done.5.refs_2_.refs_6_, f32[128,128]{1,0:T(8,128)S(1)} %collective-permute-done.6.refs_3_.refs_5_, ...), custom_call_target="tpu_custom_call" | custom-call | flops 10000000000 | bytes 10485760 | tf_op jit(solution)/shard_map/sources/pallas_call | solution.py:486
  24.8 0.0 collective-permute-done.7.refs_9_
  24.8 0.0 copy-done
  24.8 3.2 %applied.1 = (f32[136,128]{1,0:T(8,128)S(1)}, f32[136,128]{1,0:T(8,128)S(1)}, f32[136,128]{1,0:T(8,128)S(1)}, f32[136,128]{1,0:T(8,128)S(1)}, f32[136,128]{1,0:T...) custom-call(f32[128,128]{1,0:T(8,128)S(1)} %get-tuple-element.22.refs_0_.refs_5_, ...), custom_call_target="tpu_custom_call" | custom-call | flops 5000000000 | bytes 10485760 | tf_op jit(solution)/shard_map/applied/pallas_call | solution.py:576
  28.0 1.7 %collective-permute-start.11 = (f32[136,128]{1,0:T(8,128)S(1)}, f32[136,128]{1,0:T(8,128)S(1)}, u32[]{:S(2)}, u32[]{:S(2)}) collective-permute-start(f32[136,128]{1,0:T(8,128)S(1)} %get-tuple-element.36), channel_id=1, source_target_pairs={{0,3},{1,2},{2,1},{3,0},{4,7},{5,6},{6,5},{7,4},{8,11},{9,10},{10,... | collective-permute-start | bytes 208904 | tf_op jit(solution)/shard_map/ppermute | solution.py:643
  29.7 1.1 %collective-permute-start.12 = (f32[136,128]{1,0:T(8,128)S(1)}, f32[136,128]{1,0:T(8,128)S(1)}, u32[]{:S(2)}, u32[]{:S(2)}) collective-permute-start(f32[136,128]{1,0:T(8,128)S(1)} %get-tuple-element.37), channel_id=1, source_target_pairs={{0,2},{1,3},{2,0},{3,1},{4,6},{5,7},{6,4},{7,5},{8,10},{9,11},{10,... | collective-permute-start | bytes 208904 | tf_op jit(solution)/shard_map/ppermute | solution.py:643
  30.8 0.8 %collective-permute-start.13 = (f32[136,128]{1,0:T(8,128)S(1)}, f32[136,128]{1,0:T(8,128)S(1)}, u32[]{:S(2)}, u32[]{:S(2)}) collective-permute-start(f32[136,128]{1,0:T(8,128)S(1)} %get-tuple-element.38), channel_id=1, source_target_pairs={{0,1},{1,0},{2,3},{3,2},{4,5},{5,4},{6,7},{7,6},{8,9},{9,8},{10,11... | collective-permute-start | bytes 208904 | tf_op jit(solution)/shard_map/ppermute | solution.py:643
  31.6 1.6 %collective-permute-start.8 = (f32[136,128]{1,0:T(8,128)S(1)}, f32[136,128]{1,0:T(8,128)S(1)}, u32[]{:S(2)}, u32[]{:S(2)}) collective-permute-start(f32[136,128]{1,0:T(8,128)S(1)} %get-tuple-element.32), channel_id=1, source_target_pairs={{0,3},{1,2},{2,1},{3,0},{4,7},{5,6},{6,5},{7,4},{8,11},{9,10},{10,... | collective-permute-start | bytes 208904 | tf_op jit(solution)/shard_map/ppermute | solution.py:643
  33.2 1.1 %collective-permute-start.9 = (f32[136,128]{1,0:T(8,128)S(1)}, f32[136,128]{1,0:T(8,128)S(1)}, u32[]{:S(2)}, u32[]{:S(2)}) collective-permute-start(f32[136,128]{1,0:T(8,128)S(1)} %get-tuple-element.33), channel_id=1, source_target_pairs={{0,2},{1,3},{2,0},{3,1},{4,6},{5,7},{6,4},{7,5},{8,10},{9,11},{10,... | collective-permute-start | bytes 208904 | tf_op jit(solution)/shard_map/ppermute | solution.py:643
  34.3 0.0 collective-permute-done.11
  34.3 0.9 %collective-permute-start.10 = (f32[136,128]{1,0:T(8,128)S(1)}, f32[136,128]{1,0:T(8,128)S(1)}, u32[]{:S(2)}, u32[]{:S(2)}) collective-permute-start(f32[136,128]{1,0:T(8,128)S(1)} %get-tuple-element.34), channel_id=1, source_target_pairs={{0,1},{1,0},{2,3},{3,2},{4,5},{5,4},{6,7},{7,6},{8,9},{9,8},{10,11... | collective-permute-start | bytes 208904 | tf_op jit(solution)/shard_map/ppermute | solution.py:643
  35.2 0.0 collective-permute-done.12
  35.2 0.2 collective-permute-done.13
  35.5 2.7 %collective-permute-start.14 = (f32[136,128]{1,0:T(8,128)S(1)}, f32[136,128]{1,0:T(8,128)S(1)}, u32[]{:S(2)}, u32[]{:S(2)}) collective-permute-start(f32[136,128]{1,0:T(8,128)S(1)} %add_add_fusion), channel_id=1, source_target_pairs={{0,4},{1,5},{2,6},{3,7},{4,0},{5,1},{6,2},{7,3},{8,12},{9,13},{10,... | collective-permute-start | bytes 208904 | tf_op jit(solution)/shard_map/ppermute | solution.py:643
  38.2 1.0 %copy.18 = f32[1,16,128,128]{3,2,1,0:T(8,128)} copy(f32[1,16,128,128]{3,2,1,0:T(8,128)S(1)} %bitcast.6) | data formatting | bytes 2097152
  39.1 0.1 norms.1.refs_6_
  39.2 0.0 collective-permute-done.8.refs_1_
  39.2 0.0 collective-permute-done.9.refs_2_
  39.2 0.0 collective-permute-done.10.refs_3_
  39.2 2.5 %collective-permute-done.14.refs_4_ = f32[136,128]{1,0:T(8,128)S(1)} collective-permute-done((f32[136,128]{1,0:T(8,128)S(1)}, f32[136,128]{1,0:T(8,128)S(1)}, u32[]{:S(2)}, u32[]{:S(2)}) %collective-permute-start.14) | collective-permute-done | bytes 69664 | tf_op jit(solution)/shard_map/ppermute | solution.py:643
  41.8 0.8 %finish.1 = (f32[128,128]{1,0:T(8,128)}, f32[1,128]{1,0:T(1,128)}) custom-call(f32[136,128]{1,0:T(8,128)S(1)} %get-tuple-element.31.refs_0_, f32[136,128]{1,0:T(8,128)S(1)} %collective-permute-done.8.refs_1_, f32[136,128]{1,0:T(8,128)S(1)} %collective-permute-done.9.refs_2_, f32[136,128]{1,0:T(8,128)S(1)} %collective-permute-done.10.refs_3_, ...), custom_call_target="tpu_custom_call" | custom-call | tf_op jit(solution)/shard_map/finish/pallas_call | solution.py:616
  (1 shorter events, 0.0 us)
Async XLA Ops:
  0.6 7.6 %collective-permute-start.3 = (f32[128,128]{1,0:T(8,128)}, f32[128,128]{1,0:T(8,128)S(1)}, u32[]{:S(2)}, u32[]{:S(2)}) collective-permute-start(f32[128,128]{1,0:T(8,128)} %bitcast.8), channel_id=1, source_target_pairs={{0,4},{1,5},{2,6},{3,7},{4,0},{5,1},{6,2},{7,3},{8,12},{9,13},{10,... | collective-permute-start | bytes 196616 | tf_op jit(solution)/shard_map/ppermute | solution.py:643
  4.7 6.6 %collective-permute-start.2 = (f32[128,128]{1,0:T(8,128)}, f32[128,128]{1,0:T(8,128)S(1)}, u32[]{:S(2)}, u32[]{:S(2)}) collective-permute-start(f32[128,128]{1,0:T(8,128)} %bitcast.9), channel_id=1, source_target_pairs={{0,3},{1,2},{2,1},{3,0},{4,7},{5,6},{6,5},{7,4},{8,11},{9,10},{10,... | collective-permute-start | bytes 196616 | tf_op jit(solution)/shard_map/ppermute | solution.py:643
  7.3 5.4 %collective-permute-start.1 = (f32[128,128]{1,0:T(8,128)}, f32[128,128]{1,0:T(8,128)S(1)}, u32[]{:S(2)}, u32[]{:S(2)}) collective-permute-start(f32[128,128]{1,0:T(8,128)} %bitcast.10), channel_id=1, source_target_pairs={{0,2},{1,3},{2,0},{3,1},{4,6},{5,7},{6,4},{7,5},{8,10},{9,11},{10,... | collective-permute-start | bytes 196616 | tf_op jit(solution)/shard_map/ppermute | solution.py:643
  7.7 5.0 %collective-permute-start = (f32[128,128]{1,0:T(8,128)}, f32[128,128]{1,0:T(8,128)S(1)}, u32[]{:S(2)}, u32[]{:S(2)}) collective-permute-start(f32[128,128]{1,0:T(8,128)} %bitcast.11), channel_id=1, source_target_pairs={{0,1},{1,0},{2,3},{3,2},{4,5},{5,4},{6,7},{7,6},{8,9},{9,8},{10,11... | collective-permute-start | bytes 196616 | tf_op jit(solution)/shard_map/ppermute | solution.py:643
  8.2 8.3 %collective-permute-start.6 = (f32[128,128]{1,0:T(8,128)S(1)}, f32[128,128]{1,0:T(8,128)S(1)}, u32[]{:S(2)}, u32[]{:S(2)}) collective-permute-start(f32[128,128]{1,0:T(8,128)S(1)} %collective-permute-done.3.refs_4_), channel_id=1, source_target_pairs={{0,1},{1,0},{2,3},{3,2},{4,5},{5,4},{6,7},{7,6},{8,9},{9,8},{10,11... | collective-permute-start | bytes 196616 | tf_op jit(solution)/shard_map/ppermute | solution.py:643
  9.9 6.7 %collective-permute-start.5 = (f32[128,128]{1,0:T(8,128)S(1)}, f32[128,128]{1,0:T(8,128)S(1)}, u32[]{:S(2)}, u32[]{:S(2)}) collective-permute-start(f32[128,128]{1,0:T(8,128)S(1)} %collective-permute-done.3.refs_4_), channel_id=1, source_target_pairs={{0,2},{1,3},{2,0},{3,1},{4,6},{5,7},{6,4},{7,5},{8,10},{9,11},{10,... | collective-permute-start | bytes 196616 | tf_op jit(solution)/shard_map/ppermute | solution.py:643
  11.3 5.2 %collective-permute-start.4 = (f32[128,128]{1,0:T(8,128)S(1)}, f32[128,128]{1,0:T(8,128)S(1)}, u32[]{:S(2)}, u32[]{:S(2)}) collective-permute-start(f32[128,128]{1,0:T(8,128)S(1)} %collective-permute-done.3.refs_4_), channel_id=1, source_target_pairs={{0,3},{1,2},{2,1},{3,0},{4,7},{5,6},{6,5},{7,4},{8,11},{9,10},{10,... | collective-permute-start | bytes 196616 | tf_op jit(solution)/shard_map/ppermute | solution.py:643
  21.6 3.1 %collective-permute-start.7 = (f32[16,128,128]{2,1,0:T(8,128)S(1)}, f32[16,128,128]{2,1,0:T(8,128)S(1)}, u32[]{:S(2)}, u32[]{:S(2)}) collective-permute-start(f32[16,128,128]{2,1,0:T(8,128)S(1)} %get-tuple-element.27), channel_id=1, source_target_pairs={{0,8},{8,0},{1,9},{9,1},{2,10},{10,2},{3,11},{11,3},{4,12},{12,4},... | collective-permute-start | bytes 3145736 | tf_op jit(solution)/shard_map/ppermute | solution.py:658
  21.7 3.1 %copy-start = (f32[1,16,128,128]{3,2,1,0:T(8,128)S(1)}, f32[1,16,128,128]{3,2,1,0:T(8,128)}, u32[]{:S(2)}) copy-start(f32[1,16,128,128]{3,2,1,0:T(8,128)} %refs_11_.1) | copy-start | bytes 3145732
  28.0 6.3 %collective-permute-start.11 = (f32[136,128]{1,0:T(8,128)S(1)}, f32[136,128]{1,0:T(8,128)S(1)}, u32[]{:S(2)}, u32[]{:S(2)}) collective-permute-start(f32[136,128]{1,0:T(8,128)S(1)} %get-tuple-element.36), channel_id=1, source_target_pairs={{0,3},{1,2},{2,1},{3,0},{4,7},{5,6},{6,5},{7,4},{8,11},{9,10},{10,... | collective-permute-start | bytes 208904 | tf_op jit(solution)/shard_map/ppermute | solution.py:643
  29.7 5.5 %collective-permute-start.12 = (f32[136,128]{1,0:T(8,128)S(1)}, f32[136,128]{1,0:T(8,128)S(1)}, u32[]{:S(2)}, u32[]{:S(2)}) collective-permute-start(f32[136,128]{1,0:T(8,128)S(1)} %get-tuple-element.37), channel_id=1, source_target_pairs={{0,2},{1,3},{2,0},{3,1},{4,6},{5,7},{6,4},{7,5},{8,10},{9,11},{10,... | collective-permute-start | bytes 208904 | tf_op jit(solution)/shard_map/ppermute | solution.py:643
  30.8 4.6 %collective-permute-start.13 = (f32[136,128]{1,0:T(8,128)S(1)}, f32[136,128]{1,0:T(8,128)S(1)}, u32[]{:S(2)}, u32[]{:S(2)}) collective-permute-start(f32[136,128]{1,0:T(8,128)S(1)} %get-tuple-element.38), channel_id=1, source_target_pairs={{0,1},{1,0},{2,3},{3,2},{4,5},{5,4},{6,7},{7,6},{8,9},{9,8},{10,11... | collective-permute-start | bytes 208904 | tf_op jit(solution)/shard_map/ppermute | solution.py:643
  31.6 7.7 %collective-permute-start.8 = (f32[136,128]{1,0:T(8,128)S(1)}, f32[136,128]{1,0:T(8,128)S(1)}, u32[]{:S(2)}, u32[]{:S(2)}) collective-permute-start(f32[136,128]{1,0:T(8,128)S(1)} %get-tuple-element.32), channel_id=1, source_target_pairs={{0,3},{1,2},{2,1},{3,0},{4,7},{5,6},{6,5},{7,4},{8,11},{9,10},{10,... | collective-permute-start | bytes 208904 | tf_op jit(solution)/shard_map/ppermute | solution.py:643
  33.2 6.0 %collective-permute-start.9 = (f32[136,128]{1,0:T(8,128)S(1)}, f32[136,128]{1,0:T(8,128)S(1)}, u32[]{:S(2)}, u32[]{:S(2)}) collective-permute-start(f32[136,128]{1,0:T(8,128)S(1)} %get-tuple-element.33), channel_id=1, source_target_pairs={{0,2},{1,3},{2,0},{3,1},{4,6},{5,7},{6,4},{7,5},{8,10},{9,11},{10,... | collective-permute-start | bytes 208904 | tf_op jit(solution)/shard_map/ppermute | solution.py:643
  34.3 4.9 %collective-permute-start.10 = (f32[136,128]{1,0:T(8,128)S(1)}, f32[136,128]{1,0:T(8,128)S(1)}, u32[]{:S(2)}, u32[]{:S(2)}) collective-permute-start(f32[136,128]{1,0:T(8,128)S(1)} %get-tuple-element.34), channel_id=1, source_target_pairs={{0,1},{1,0},{2,3},{3,2},{4,5},{5,4},{6,7},{7,6},{8,9},{9,8},{10,11... | collective-permute-start | bytes 208904 | tf_op jit(solution)/shard_map/ppermute | solution.py:643
  35.5 6.3 %collective-permute-start.14 = (f32[136,128]{1,0:T(8,128)S(1)}, f32[136,128]{1,0:T(8,128)S(1)}, u32[]{:S(2)}, u32[]{:S(2)}) collective-permute-start(f32[136,128]{1,0:T(8,128)S(1)} %add_add_fusion), channel_id=1, source_target_pairs={{0,4},{1,5},{2,6},{3,7},{4,0},{5,1},{6,2},{7,3},{8,12},{9,13},{10,... | collective-permute-start | bytes 208904 | tf_op jit(solution)/shard_map/ppermute | solution.py:643
